TPU v7x, 32 devices: a whole 2x2x4 slice. The times are simulated.
32 devices in a mesh: grp: 4 (over x, core), dom: 8 (over z, y).
Axes of the slice: x: 2, y: 2, z: 4, core: 2. Of those that a mesh axis runs over, the one named last changes fastest.
Arguments:
- nodes: bfloat16 [32768, 256], P(('grp', 'dom')), may hold values from -8 to 8
- neighbours: int32 [32768, 8], P(('grp', 'dom')), may hold values from 0 to 1279
- send_rows: int32 [8192], P(('grp', 'dom')), may hold values from 0 to 1023
- landmark_ids: int32 [8192], P(('grp', 'dom')), may hold values from 0 to 1023
- w_dst: bfloat16 [256, 256], replicated, may hold values from -0.375 to 0.375
- w_src: bfloat16 [256, 256], replicated, may hold values from -0.375 to 0.375
- w_msg: bfloat16 [256, 256], replicated, may hold values from -0.375 to 0.375
- edge_bias: float32 [256], replicated, may hold values from -4 to 4
- w_query: bfloat16 [256, 256], replicated, may hold values from -0.375 to 0.375
- w_key: bfloat16 [256, 256], replicated, may hold values from -0.375 to 0.375
- w_value: bfloat16 [256, 256], replicated, may hold values from -0.375 to 0.375
- w_out: bfloat16 [256, 256], replicated, may hold values from -0.375 to 0.375
Outputs:
- result: bfloat16 [32768, 256], P(('grp', 'dom'))
- kernel_term: float32 [32768, 256], P(('grp', 'dom'))
Inputs may be any that keep to these rules, and one draw needn't show every extreme that they name: `neighbours`: entries index the device's own 1024 rows, then the 128 rows received from the previous partition, then the 128 rows from the next one. `send_rows`: each partition's entries are rows of its own nodes. `landmark_ids`: each partition's entries are rows of its own nodes.
All inputs are finite; a program needn't handle non-finite values.
Results may differ from a plain program's by a relative error of at most 0.0054.
Values may be sent and summed in bfloat16 or wider, within the bound.
No kernel may reach another device: no remote copies, remote signals or barrier semaphores. Data moves between devices by JAX's collectives and lax.ppermute only.
A program may use at most 64 MiB of HBM per device.

v0:
```python
import math

import jax
import jax.numpy as jnp
from jax import lax
from jax.sharding import PartitionSpec as P


def extended_2(cells, sides, width):
    for axis, dim in sides:
        count = lax.axis_size(axis)
        head = lax.slice_in_dim(cells, 0, width, axis=dim)
        tail = lax.slice_in_dim(cells, cells.shape[dim] - width, cells.shape[dim], axis=dim)
        cells = jnp.concatenate(
            [
                lax.ppermute(tail, axis, [(i, (i + 1) % count) for i in range(count)]),
                cells,
                lax.ppermute(head, axis, [((i + 1) % count, i) for i in range(count)]),
            ],
            axis=dim,
        )
    return cells


def rms_scale(values):
    return values * lax.rsqrt(jnp.mean(values * values, axis=-1, keepdims=True) + 1e-06)


def kernel_tile(query, key_rows):
    scale = 2.0 * query.shape[1] ** (-0.5)
    return jnp.exp(jnp.dot(query, key_rows.T, preferred_element_type=jnp.float32) * scale).astype(
        jnp.bfloat16
    )


def partial_sums(query, value, key_rows):
    total_rows = key_rows.shape[0]
    block_size = math.gcd(total_rows, 512)
    blocks = key_rows.reshape(total_rows // block_size, block_size, key_rows.shape[1])

    def partial_one_block(block_keys):
        kernel = kernel_tile(query, block_keys)
        return lax.dot_general(
            kernel, value, (((0,), (0,)), ((), ())), preferred_element_type=jnp.float32
        )

    return lax.map(partial_one_block, blocks).reshape(total_rows, value.shape[1])


def apply_sums(query, key_rows, sum_rows):
    total_rows = key_rows.shape[0]
    block_size = math.gcd(total_rows, 512)
    key_blocks = key_rows.reshape(total_rows // block_size, block_size, key_rows.shape[1])
    sum_blocks = sum_rows.reshape(total_rows // block_size, block_size, sum_rows.shape[1])

    def apply_one_block(accum, pair):
        block_keys, block_sums = pair
        kernel = kernel_tile(query, block_keys)
        return (accum + jnp.dot(kernel, block_sums, preferred_element_type=jnp.float32), None)

    start_value = jnp.zeros((query.shape[0], sum_rows.shape[1]), jnp.float32)
    accum, _ = lax.scan(apply_one_block, start_value, (key_blocks, sum_blocks))
    return accum


def shards(
    nodes,
    neighbours,
    send_rows,
    landmark_ids,
    w_dst,
    w_src,
    w_msg,
    edge_bias,
    w_query,
    w_key,
    w_value,
    w_out,
):
    halo_count = send_rows.shape[0] // 2
    outgoing = jnp.concatenate(
        [nodes[send_rows[:halo_count]], nodes[send_rows[halo_count:]]], axis=0
    )
    padded = extended_2(outgoing, ((("grp", "dom"), 0),), halo_count)
    extended = jnp.concatenate([nodes, padded[:halo_count], padded[3 * halo_count :]], axis=0)
    source = jnp.dot(extended, w_src, preferred_element_type=jnp.float32)
    target = jnp.dot(nodes, w_dst, preferred_element_type=jnp.float32)
    preact = target[:, None, :] + source[neighbours] + edge_bias
    messages = jnp.mean(jax.nn.gelu(preact), axis=1).astype(jnp.bfloat16)
    updated = (
        nodes.astype(jnp.float32) + jnp.dot(messages, w_msg, preferred_element_type=jnp.float32)
    ).astype(jnp.bfloat16)
    normed = rms_scale(updated.astype(jnp.float32)).astype(jnp.bfloat16)
    query = jnp.dot(normed, w_query, preferred_element_type=jnp.float32).astype(jnp.bfloat16)
    value = jnp.dot(normed, w_value, preferred_element_type=jnp.float32).astype(jnp.bfloat16)
    local_keys = jnp.dot(normed[landmark_ids], w_key, preferred_element_type=jnp.float32).astype(
        jnp.bfloat16
    )
    all_keys = lax.all_gather(local_keys, ("grp", "dom"), axis=0, tiled=True)
    own_sums = partial_sums(query, value, all_keys)
    total_sums = lax.psum(own_sums, ("grp", "dom")).astype(jnp.bfloat16)
    smooth = apply_sums(query, all_keys, total_sums)
    kernel_term = rms_scale(smooth)
    scaled = kernel_term.astype(jnp.bfloat16)
    result = updated.astype(jnp.float32) + jnp.dot(
        scaled, w_out, preferred_element_type=jnp.float32
    )
    return (result.astype(jnp.bfloat16), kernel_term)


def solution(mesh):
    return jax.shard_map(
        shards,
        mesh=mesh,
        in_specs=(
            P(("grp", "dom"), None),
            P(("grp", "dom"), None),
            P(("grp", "dom")),
            P(("grp", "dom")),
            P(),
            P(),
            P(),
            P(),
            P(),
            P(),
            P(),
            P(),
        ),
        out_specs=(P(("grp", "dom"), None), P(("grp", "dom"), None)),
        check_vma=False,
    )
```

profile of v0, /device:TPU:0, one launch (start us, length us, event | category | flops | bytes accessed | tf_op | source)
XLA Modules:
  0.0 363.8 jit_solution(12061024520757388193)
XLA Ops:
  9.9 3.0 collective-permute-start
  14.8 3.5 collective-permute-start.1
  24.9 31.5 %gather_fusion.2 = f32[8192,256]{1,0:T(8,128)} fusion(f32[1280,256]{1,0:T(8,128)S(1)} %fusion.36, s32[8192]{0:T(1024)S(1)} %broadcast_clamp_fusion), kind=kCustom, calls=%fused_computation.2 | custom fusion | bytes 16809984 | tf_op jit(solution)/shard_map/gather | solution.py:88
  56.4 7.7 %fusion.30 = f32[1024,256]{1,0:T(8,128)S(1)} fusion(f32[8192,256]{1,0:T(8,128)} %gather_fusion.2, f32[256]{0:T(256)S(1)} %copy-done.6, f32[1024,256]{1,0:T(8,128)S(1)} %fusion.46), kind=kLoop, calls=%fused_computation.31 | loop fusion | flops 22806528 | bytes 10486784 | tf_op jit(solution)/shard_map/reduce_sum | solution.py:89
  69.5 58.1 %all-gather.2.cloned.1.call-done = bf16[8192,256]{1,0:T(8,128)(2,1)} async-done(((bf16[256,256]{1,0:T(8,128)(2,1)}), bf16[8192,256]{1,0:T(8,128)(2,1)}) %all-gather.2.cloned.1.call-update) | async-done | bytes 4194320 | tf_op jit(solution)/shard_map/all_gather | solution.py:99
  127.6 41.7 %while.21 = (s32[]{:T(128)}, f32[16,512,256]{2,1,0:T(8,128)}, bf16[16,512,256]{2,1,0:T(8,128)(2,1)}, bf16[1024,256]{1,0:T(8,128)(2,1)S(1)}, bf16[1024,256]{1,0:T(8,128)(2,1)S(1)}, /*index=5*/s32[]{:T(128)}) while((s32[]{:T(128)}, f32[16,512,256]{2,1,0:T(8,128)}, bf16[16,512,256]{2,1,0:T(8,128)(2,1)}, bf16[1024,256]{1,0:T(8,128)(2,1)S(1)}, ...), condition=%wide.region_3.4_spmd, body=%wide.region_2.3_spmd.sunk | while | flops 537919488 | bytes 1836101 | solution.py:47
  127.6 2.6 fusion.72
  130.2 2.6 fusion.72
  132.8 2.6 fusion.72
  135.4 2.6 fusion.72
  138.0 2.6 fusion.72
  140.6 2.6 fusion.72
  143.2 2.6 fusion.72
  145.8 2.6 fusion.72
  148.4 2.6 fusion.72
  151.0 2.6 fusion.72
  153.6 2.6 fusion.72
  156.3 2.6 fusion.72
  158.9 2.6 fusion.72
  161.5 2.6 fusion.72
  164.1 2.6 fusion.72
  166.7 2.6 fusion.72
  169.3 149.8 %all-reduce.1 = bf16[8192,256]{1,0:T(8,128)(2,1)} all-reduce(f32[8192,256]{1,0:T(8,128)} %bitcast.52), channel_id=1, replica_groups=mesh['grp'=4,'dom'=8] {'grp','dom'}, use_global_device_ids=true, to_apply=%region_4.5 | all-reduce | flops 2097152 | bytes 12582912 | tf_op jit(solution)/shard_map/psum | solution.py:101
  319.1 36.1 %while.22 = (s32[]{:T(128)}, f32[1024,256]{1,0:T(8,128)S(1)}, bf16[16,512,256]{2,1,0:T(8,128)(2,1)}, bf16[1024,256]{1,0:T(8,128)(2,1)S(1)}, bf16[16,512,256]{2,1,0:T(8,128)(2,1)}, /*index=5*/s32[]{:T(128)}, s32[]{:T(128)}) while((s32[]{:T(128)}, f32[1024,256]{1,0:T(8,128)S(1)}, bf16[16,512,256]{2,1,0:T(8,128)(2,1)}, ...), condition=%wide.region_6.7_spmd.clone, body=%wide.region_5.6_spmd.clone.sunk | while | flops 538443776 | bytes 3146839 | solution.py:62
  (63 shorter events, 53.8 us)
Async XLA Ops:
  7.2 16.3 %copy-start = (bf16[256,256]{1,0:T(8,128)(2,1)S(1)}, bf16[256,256]{1,0:T(8,128)(2,1)}, u32[]{:S(2)}) copy-start(bf16[256,256]{1,0:T(8,128)(2,1)} %param.21) | copy-start | bytes 393220
  7.2 120.4 %all-gather.2.cloned.1.call-start = ((), (), s32[]{:S(2)}) async-start(), calls=%async_computation | async-start | bytes 4325376 | tf_op jit(solution)/shard_map/all_gather | solution.py:99
  9.9 12.9 %collective-permute-start = (bf16[128,256]{1,0:T(8,128)(2,1)S(1)}, bf16[128,256]{1,0:T(8,128)(2,1)S(1)}, u32[]{:S(2)}, u32[]{:S(2)}) collective-permute-start(bf16[128,256]{1,0:T(8,128)(2,1)S(1)} %gather_fusion), channel_id=1, source_target_pairs={{0,1},{1,2},{2,3},{3,4},{4,5},{5,6},{6,7},{7,8},{8,9},{9,10},{10,1... | collective-permute-start | bytes 196616 | tf_op jit(solution)/shard_map/ppermute | solution.py:16
  14.8 8.7 %collective-permute-start.1 = (bf16[128,256]{1,0:T(8,128)(2,1)S(1)}, bf16[128,256]{1,0:T(8,128)(2,1)}, u32[]{:S(2)}, u32[]{:S(2)}) collective-permute-start(bf16[128,256]{1,0:T(8,128)(2,1)S(1)} %gather_fusion.1), channel_id=1, source_target_pairs={{1,0},{2,1},{3,2},{4,3},{5,4},{6,5},{7,6},{8,7},{9,8},{10,9},{11,1... | collective-permute-start | bytes 196616 | tf_op jit(solution)/shard_map/ppermute | solution.py:18
  22.8 0.6 copy-start.5
  24.9 31.5 %copy-start.6 = (f32[256]{0:T(256)S(1)}, f32[256]{0:T(256)}, u32[]{:S(2)}) copy-start(f32[256]{0:T(256)} %param.23) | copy-start | bytes 3076
  56.4 7.8 %copy-start.2 = (bf16[256,256]{1,0:T(8,128)(2,1)S(1)}, bf16[256,256]{1,0:T(8,128)(2,1)}, u32[]{:S(2)}) copy-start(bf16[256,256]{1,0:T(8,128)(2,1)} %param.22) | copy-start | bytes 393220
  56.4 9.6 %copy-start.3 = (bf16[256,256]{1,0:T(8,128)(2,1)S(1)}, bf16[256,256]{1,0:T(8,128)(2,1)}, u32[]{:S(2)}) copy-start(bf16[256,256]{1,0:T(8,128)(2,1)} %param.25) | copy-start | bytes 393220
  319.1 36.5 %copy-start.4 = (bf16[256,256]{1,0:T(8,128)(2,1)S(1)}, bf16[256,256]{1,0:T(8,128)(2,1)}, u32[]{:S(2)}) copy-start(bf16[256,256]{1,0:T(8,128)(2,1)} %param.27) | copy-start | bytes 393220
  355.6 1.4 copy-start.1
Sparse Core Ops, SparseCore 0:
  67.0 60.5 all-gather.1
where the time goes:
time: 365 us; the launch traced here: 364 us
  blocking collectives  150 us (41%)
  matrix products  84.3 us (23%)
  waiting for transfers between devices  58.2 us (16%)
  local copies, waits for them, and re-layouts  40 us (11%)
  between operations  14.2 us (4%)
  other arithmetic  10.5 us (3%)
  starting transfers between devices  6.54 us (2%)
    psum x1, blocking collectives, shards(): total_sums = lax.psum(own_sums, ('grp', 'dom')).astype(jnp.bfloat16)  150 us
    all_gather x1, waiting for transfers between devices, shards(): all_keys = lax.all_gather(local_keys, ('grp', 'dom'), axis=0, tiled=True)  58.1 us
    dot_general x16, matrix products, partial_one_block(): lax.dot_general(kernel, value, (((0,), (0,)), ((), ())), preferred_elemen...  41.7 us
    dot_general x16, matrix products, apply_one_block(): jnp.dot(kernel, block_sums, preferred_element_type=jnp.float32)  35.7 us
    gather x1, local copies, waits for them, and re-layouts, shards(): preact = target[:, None, :] + source[neighbours] + edge_bias  31.5 us
    reduce_sum x1, other arithmetic, shards(): messages = jnp.mean(jax.nn.gelu(preact), axis=1).astype(jnp.bfloat16)  7.74 us
  transfers between devices with their start and end apart: 3, of which 1 were waited for; matrix products, arithmetic and copies ran while one was open for 2% of the time, Pallas kernels for 0%

commit v1 on v0

v1 whole, which is shorter than its diff:
```python
import functools
import math

import jax
import jax.numpy as jnp
from jax import lax
from jax.experimental import pallas as pl
from jax.experimental.pallas import tpu as pltpu
from jax.sharding import PartitionSpec as P

BF16 = jnp.bfloat16
F32 = jnp.float32
BOTH = ("grp", "dom")
EPS = 1e-06
VMEM_LIMIT = 48 * 2**20


def dot(a, b, ca=1, cb=0):
    return lax.dot_general(a, b, (((ca,), (cb,)), ((), ())), preferred_element_type=F32)


def whole(shape):
    return pl.BlockSpec(shape, lambda *_: (0,) * len(shape))


def call(body, name, out_shape, in_specs, out_specs, args, grid=(1,), scratch=(), flops=0, exps=0):
    outs = out_shape if isinstance(out_shape, (list, tuple)) else [out_shape]
    moved = sum(a.size * a.dtype.itemsize for a in (*args, *outs))
    return pl.pallas_call(
        body,
        grid=grid,
        in_specs=in_specs,
        out_specs=out_specs,
        out_shape=out_shape,
        scratch_shapes=list(scratch),
        name=name,
        compiler_params=pltpu.CompilerParams(vmem_limit_bytes=VMEM_LIMIT),
        cost_estimate=pl.CostEstimate(flops=flops, bytes_accessed=moved, transcendentals=exps),
    )(*args)


def picked(ids, table):
    rows = table.shape[0]
    place = lax.broadcasted_iota(jnp.int32, (rows, ids.shape[1]), 0)
    hot = jnp.where(place == ids, 1.0, 0.0).astype(BF16)
    return dot(hot, table, 0, 0).astype(BF16)


def send_body(ids_ref, nodes_ref, prev_ref, next_ref):
    rows = picked(ids_ref[...], nodes_ref[...])
    half = rows.shape[0] // 2
    prev_ref[...] = rows[:half]
    next_ref[...] = rows[half:]


def hot_rows(ids, first, width):
    n = ids.shape[1]
    spread = jnp.transpose(jnp.broadcast_to(ids, (128, n)))
    lane = lax.broadcasted_iota(jnp.int32, (n, 128), 1)
    parts = [
        jnp.where(spread == lane + (first + 128 * c), 1.0, 0.0).astype(BF16)
        for c in range(width // 128)
    ]
    return jnp.concatenate(parts, axis=1)


def own_body(links_ref, nodes_ref, tile_ref, w_src_ref, w_dst_ref, bias_ref, pre_ref, source):
    @pl.when(pl.program_id(0) == 0)
    def _():
        source[...] = dot(nodes_ref[...], w_src_ref[...]).astype(BF16)

    target = dot(tile_ref[...], w_dst_ref[...]) + bias_ref[...]
    links = links_ref[...]
    for k in range(links.shape[0]):
        hot = hot_rows(links[k : k + 1], 0, source.shape[0])
        pre_ref[k] = dot(hot, source[...]) + target


def gelu(x):
    inner = math.sqrt(2.0 / math.pi) * (x + 0.044715 * (x * x * x))
    return 0.5 * x * (1.0 + jnp.tanh(inner))


def edge_body(
    links_ref,
    pre_ref,
    prev_ref,
    next_ref,
    tile_ref,
    ids_ref,
    w_src_ref,
    w_msg_ref,
    w_key_ref,
    updated_ref,
    normed_ref,
    keys_ref,
    source,
    table,
):
    step = pl.program_id(0)
    halo = prev_ref.shape[0]
    rows = table.shape[0]

    @pl.when(step == 0)
    def _():
        source[:halo] = dot(prev_ref[...], w_src_ref[...]).astype(BF16)
        source[halo:] = dot(next_ref[...], w_src_ref[...]).astype(BF16)

    links = links_ref[...]
    count = links.shape[0]
    total = 0.0
    for k in range(count):
        hot = hot_rows(links[k : k + 1], rows, 2 * halo)
        total += gelu(pre_ref[k] + dot(hot, source[...]))
    messages = (total * (1.0 / count)).astype(BF16)
    updated = (tile_ref[...].astype(F32) + dot(messages, w_msg_ref[...])).astype(BF16)
    updated_ref[...] = updated
    wide = updated.astype(F32)
    normed = (wide * lax.rsqrt(jnp.mean(wide * wide, axis=1, keepdims=True) + EPS)).astype(BF16)
    normed_ref[...] = normed
    n = normed.shape[0]
    table[pl.ds(pl.multiple_of(step * n, n), n), :] = normed

    @pl.when(step == pl.num_programs(0) - 1)
    def _():
        keys_ref[...] = dot(picked(ids_ref[...], table[...]), w_key_ref[...]).astype(BF16)


def smooth_up_body(count, scale, has_start, *refs):
    nodes, refs = refs[:count], refs[count:]
    keys_ref, w_query_ref, w_value_ref, *refs = refs
    if has_start:
        start_ref, *refs = refs
    tiles, refs = refs[:count], refs[count:]
    sums_ref, *refs = refs
    query, value = refs[:count], refs[count:]

    @pl.when(pl.program_id(0) == 0)
    def _():
        for b in range(count):
            query[b][...] = dot(nodes[b][...], w_query_ref[...]).astype(BF16)
            value[b][...] = dot(nodes[b][...], w_value_ref[...]).astype(BF16)

    total = start_ref[...] if has_start else 0.0
    for b in range(count):
        tile = jnp.exp2(dot(keys_ref[...], query[b][...], 1, 1) * scale).astype(BF16)
        tiles[b][...] = tile
        total += dot(tile, value[b][...])
    sums_ref[...] = total.astype(sums_ref.dtype)


def smooth_up(blocks, keys, w_query, w_value, start, out_dtype, name):
    marks, c = keys.shape
    step = min(marks, 512)
    scale = 2.0 * c ** (-0.5) * math.log2(math.e)
    sizes = [b.shape[0] for b in blocks]
    in_specs = [whole(b.shape) for b in blocks]
    in_specs += [pl.BlockSpec((step, c), lambda j: (j, 0)), whole((c, c)), whole((c, c))]
    args = [*blocks, keys, w_query, w_value]
    if start is not None:
        in_specs.append(pl.BlockSpec((step, c), lambda j: (j, 0)))
        args.append(start)
    out = call(
        functools.partial(smooth_up_body, len(blocks), scale, start is not None),
        name,
        [jax.ShapeDtypeStruct((marks, n), BF16) for n in sizes]
        + [jax.ShapeDtypeStruct((marks, c), out_dtype)],
        in_specs,
        [pl.BlockSpec((step, n), lambda j: (j, 0)) for n in sizes]
        + [pl.BlockSpec((step, c), lambda j: (j, 0))],
        args,
        grid=(marks // step,),
        scratch=[pltpu.VMEM((n, c), BF16) for n in sizes] * 2,
        flops=4 * marks * sum(sizes) * c + 4 * sum(sizes) * c * c,
        exps=marks * sum(sizes),
    )
    return out[:-1], out[-1]


def smooth_down_body(tile_ref, sums_ref, out_ref):
    out_ref[...] = dot(tile_ref[...], sums_ref[...], 0, 0).astype(out_ref.dtype)


def smooth_down(tiles, sums, out_dtype, name):
    marks, n = tiles.shape
    c = sums.shape[1]
    step = min(n, 256)
    return call(
        smooth_down_body,
        name,
        jax.ShapeDtypeStruct((n, c), out_dtype),
        [pl.BlockSpec((marks, step), lambda j: (0, j)), whole((marks, c))],
        pl.BlockSpec((step, c), lambda j: (j, 0)),
        [tiles, sums],
        grid=(n // step,),
        flops=2 * marks * n * c,
    )


def last_body(own_ref, a_ref, b_ref, c_ref, updated_ref, w_out_ref, result_ref, term_ref):
    smooth = own_ref[...] + a_ref[...].astype(F32) + b_ref[...].astype(F32) + c_ref[...].astype(F32)
    term = smooth * lax.rsqrt(jnp.mean(smooth * smooth, axis=1, keepdims=True) + EPS)
    term_ref[...] = term
    result = updated_ref[...].astype(F32) + dot(term.astype(BF16), w_out_ref[...])
    result_ref[...] = result.astype(BF16)


def shards(
    groups,
    domains,
    nodes,
    neighbours,
    send_rows,
    landmark_ids,
    w_dst,
    w_src,
    w_msg,
    edge_bias,
    w_query,
    w_key,
    w_value,
    w_out,
):
    rows, c = nodes.shape
    halo = send_rows.shape[0] // 2
    mine = landmark_ids.shape[0]
    slots = neighbours.shape[1]
    line = domains // 2
    parts = groups * domains
    half = rows // 2

    def pair(axis, size, flip):
        return lambda v: lax.ppermute(v, axis, [(i, i ^ flip) for i in range(size)])

    over_core = pair("grp", groups, 1)
    over_x = pair("grp", groups, 2)
    over_y = pair("dom", domains, 1)
    over_z = [pair("dom", domains, 2 * t) for t in range(line)]
    over_xy = lambda v: lax.ppermute(
        v,
        BOTH,
        [
            (g * domains + d, (g ^ 2) * domains + (d ^ 1))
            for g in range(groups)
            for d in range(domains)
        ],
    )

    to_prev, to_next = call(
        send_body,
        "send_rows",
        [jax.ShapeDtypeStruct((halo, c), BF16)] * 2,
        [whole((1, 2 * halo)), whole((rows, c))],
        [whole((halo, c))] * 2,
        [send_rows.reshape(1, 2 * halo), nodes],
        flops=4 * halo * rows * c,
    )
    from_prev = lax.ppermute(to_next, BOTH, [(i, (i + 1) % parts) for i in range(parts)])
    from_next = lax.ppermute(to_prev, BOTH, [((i + 1) % parts, i) for i in range(parts)])

    links = neighbours.T
    tile = min(rows, 256)
    steps = rows // tile
    links_spec = pl.BlockSpec((slots, tile), lambda i: (0, i))
    tile_spec = pl.BlockSpec((tile, c), lambda i: (i, 0))
    pre_spec = pl.BlockSpec((slots, tile, c), lambda i: (0, i, 0))
    pre = call(
        own_body,
        "own_edges",
        jax.ShapeDtypeStruct((slots, rows, c), F32),
        [links_spec, whole((rows, c)), tile_spec, whole((c, c)), whole((c, c)), whole((1, c))],
        pre_spec,
        [links, nodes, nodes, w_src, w_dst, edge_bias.reshape(1, c)],
        grid=(steps,),
        scratch=[pltpu.VMEM((rows, c), BF16)],
        flops=2 * slots * rows * rows * c,
    )
    updated, normed, keys = call(
        edge_body,
        "edges",
        [
            jax.ShapeDtypeStruct((rows, c), BF16),
            jax.ShapeDtypeStruct((rows, c), BF16),
            jax.ShapeDtypeStruct((mine, c), BF16),
        ],
        [
            links_spec,
            pre_spec,
            whole((halo, c)),
            whole((halo, c)),
            tile_spec,
            whole((1, mine)),
            whole((c, c)),
            whole((c, c)),
            whole((c, c)),
        ],
        [tile_spec, tile_spec, whole((mine, c))],
        [
            links,
            pre,
            from_prev,
            from_next,
            nodes,
            landmark_ids.reshape(1, mine),
            w_src,
            w_msg,
            w_key,
        ],
        grid=(steps,),
        scratch=[pltpu.VMEM((2 * halo, c), BF16), pltpu.VMEM((rows, c), BF16)],
        flops=4 * slots * rows * halo * c,
        exps=slots * rows * c,
    )

    side_keys = jnp.concatenate([keys] + [over_z[t](keys) for t in range(1, line)], axis=0)
    normed_x = over_x(normed)
    normed_y = over_y(normed)
    all_keys = jnp.concatenate([side_keys, over_core(side_keys)], axis=0)
    normed_a = over_y(normed_x[:half])
    normed_b = over_x(normed_y[half:])

    (own_tiles,), sums = smooth_up([normed], all_keys, w_query, w_value, None, F32, "up_own")
    (x_tiles, y_tiles), sums = smooth_up(
        [normed_x, normed_y], all_keys, w_query, w_value, sums, F32, "up_xy"
    )
    (a_tiles, b_tiles), sums = smooth_up(
        [normed_a, normed_b], all_keys, w_query, w_value, sums, BF16, "up_diagonal"
    )

    side = line * mine
    side_sums = (sums[:side].astype(F32) + over_core(sums[side:]).astype(F32)).astype(BF16)
    blocks = [side_sums[t * mine : (t + 1) * mine] for t in range(line)]
    arrived = [over_z[t](blocks[t]) for t in range(1, line)]
    total = blocks[0].astype(F32)
    for block in arrived:
        total = total + block.astype(F32)
    total = total.astype(BF16)
    side_total = jnp.concatenate([total] + [over_z[t](total) for t in range(1, line)], axis=0)
    all_total = jnp.concatenate([side_total, over_core(side_total)], axis=0)

    a_part = smooth_down(a_tiles, all_total, BF16, "down_a")
    b_part = smooth_down(b_tiles, all_total, BF16, "down_b")
    from_xy = over_xy(jnp.concatenate([a_part, b_part], axis=0))
    from_x = over_x(smooth_down(x_tiles, all_total, BF16, "down_x"))
    from_y = over_y(smooth_down(y_tiles, all_total, BF16, "down_y"))
    own = smooth_down(own_tiles, all_total, F32, "down_own")

    return call(
        last_body,
        "last",
        [jax.ShapeDtypeStruct((rows, c), BF16), jax.ShapeDtypeStruct((rows, c), F32)],
        [tile_spec] * 5 + [whole((c, c))],
        [tile_spec] * 2,
        [own, from_x, from_y, from_xy, updated, w_out],
        grid=(steps,),
        flops=2 * rows * c * c,
    )


def solution(mesh):
    split = P(BOTH, None)
    return jax.shard_map(
        functools.partial(shards, mesh.shape["grp"], mesh.shape["dom"]),
        mesh=mesh,
        in_specs=(split, split, P(BOTH), P(BOTH)) + (P(),) * 8,
        out_specs=(split, split),
        check_vma=False,
    )
```

time: 365 us -> 138 us (0.38)
  blocking collectives: 150 us -> 0 us
  matrix products: 84.3 us -> 0 us
  Pallas kernels: 0 us -> 47.9 us
  local copies, waits for them, and re-layouts: 40 us -> 8.86 us
  starting transfers between devices: 6.54 us -> 26.8 us
  between operations: 14.2 us -> 0.95 us
  other arithmetic: 10.5 us -> 0.3 us
  waiting for transfers between devices: 58.2 us -> 52.3 us
    psum x1 -> x0, blocking collectives: 150 us -> none  [shards(): total_sums = lax.psum(own_sums, ('grp', 'dom')).astype(jnp.bfloat16)]
    dot_general x39 -> x0, matrix products: 84.3 us -> none  [the longest x16 41.7 us: partial_one_block(): lax.dot_general(kernel, value, (((0,), (0,)), ((), ())), preferred_elemen...]
    all_gather x1 -> x0, waiting for transfers between devices: 58.1 us -> none  [shards(): all_keys = lax.all_gather(local_keys, ('grp', 'dom'), axis=0, tiled=True)]
    ppermute x2 -> x21, waiting for transfers between devices: 0.01 us -> 52.3 us  [the longest x18 44.1 us: pair(): return lambda v: lax.ppermute(v, axis, [(i, i ^ flip) for i in range(size)])]
    pallas_call x0 -> x12, Pallas kernels: none -> 47.9 us  [call(): pl.pallas_call(body, grid=grid, in_specs=in_specs, out_specs=out_specs, o...]
    gather x4 -> x0, local copies, waits for them, and re-layouts: 36.4 us -> none  [the longest x1 31.5 us: shards(): preact = target[:, None, :] + source[neighbours] + edge_bias]
    ppermute x2 -> x21, starting transfers between devices: 6.5 us -> 26.8 us  [the longest x18 18.8 us: pair(): return lambda v: lax.ppermute(v, axis, [(i, i ^ flip) for i in range(size)])]
    reduce_sum x2 -> x0, other arithmetic: 7.95 us -> none  [the longest x1 7.74 us: shards(): messages = jnp.mean(jax.nn.gelu(preact), axis=1).astype(jnp.bfloat16)]
  transfers between devices with their start and end apart: 3 -> 21, of which waited for: 1 -> 12; matrix products, arithmetic and copies ran while one was open for 2% -> 0% of each run, Pallas kernels for 0% -> 18%
where the time goes in v1:
time: 138 us; the launch traced here: 137 us
  waiting for transfers between devices  52.3 us (38%)
  Pallas kernels  47.9 us (35%)
  starting transfers between devices  26.8 us (19%)
  local copies, waits for them, and re-layouts  8.86 us (6%)
    pallas_call x12, Pallas kernels, call(): pl.pallas_call(body, grid=grid, in_specs=in_specs, out_specs=out_specs, o...  47.9 us
    ppermute x18, waiting for transfers between devices, pair(): return lambda v: lax.ppermute(v, axis, [(i, i ^ flip) for i in range(size)])  44.1 us
    ppermute x18, starting transfers between devices, pair(): return lambda v: lax.ppermute(v, axis, [(i, i ^ flip) for i in range(size)])  18.8 us
    unnamed x43, local copies, waits for them, and re-layouts  8.7 us
    ppermute x1, waiting for transfers between devices, shards(): lax.ppermute(v, BOTH, [(g * domains + d, (g ^ 2) * domains + (d ^ 1)) for...  8.2 us
    ppermute x1, starting transfers between devices, shards(): lax.ppermute(to_prev, BOTH, [((i + 1) % parts, i) for i in range(parts)])  3.47 us
    ppermute x1, starting transfers between devices, shards(): lax.ppermute(to_next, BOTH, [(i, (i + 1) % parts) for i in range(parts)])  3.02 us
  transfers between devices with their start and end apart: 21, of which 12 were waited for; matrix products, arithmetic and copies ran while one was open for 0% of the time, Pallas kernels for 18%

profile of v1, /device:TPU:0, one launch (start us, length us, event | category | flops | bytes accessed | tf_op | source)
XLA Modules:
  0.0 137.1 jit_solution(7832446322977006738)
XLA Ops:
  2.7 3.0 %collective-permute-start = (bf16[128,256]{1,0:T(8,128)(2,1)S(1)}, bf16[128,256]{1,0:T(8,128)(2,1)S(1)}, u32[]{:S(2)}, u32[]{:S(2)}) collective-permute-start(bf16[128,256]{1,0:T(8,128)(2,1)S(1)} %get-tuple-element.15), channel_id=1, source_target_pairs={{0,1},{1,2},{2,3},{3,4},{4,5},{5,6},{6,7},{7,8},{8,9},{9,10},{10,1... | collective-permute-start | bytes 196616 | tf_op jit(solution)/shard_map/ppermute | solution.py:258
  5.7 3.5 %collective-permute-start.1 = (bf16[128,256]{1,0:T(8,128)(2,1)S(1)}, bf16[128,256]{1,0:T(8,128)(2,1)S(1)}, u32[]{:S(2)}, u32[]{:S(2)}) collective-permute-start(bf16[128,256]{1,0:T(8,128)(2,1)S(1)} %get-tuple-element.16), channel_id=1, source_target_pairs={{1,0},{2,1},{3,2},{4,3},{5,4},{6,5},{7,6},{8,7},{9,8},{10,9},{11,1... | collective-permute-start | bytes 196616 | tf_op jit(solution)/shard_map/ppermute | solution.py:259
  13.5 6.9 %own_edges.1.pre_ref = f32[8,1024,256]{2,1,0:T(8,128)} custom-call(s32[8,1024]{1,0:T(8,128)S(1)} %bitcast.4, bf16[1024,256]{1,0:T(8,128)(2,1)S(1)} %copy-done.3, bf16[1024,256]{1,0:T(8,128)(2,1)S(1)} %copy-done.3, bf16[256,256]{1,0:T(8,128)(2,1)S(1)} %copy-done.5, bf16[256,256]{1,0:T(8,128)(2,1)S(1)} %copy-done.12, f32[1,256]{1,0:T(1,128)S(1)} %bitcast.8), custom_call_target="tpu_custom_call" | custom-call | flops 4294967296 | bytes 9733120 | tf_op jit(solution)/shard_map/own_edges/pallas_call | solution.py:29
  20.4 7.8 %edges.1 = (bf16[1024,256]{1,0:T(8,128)(2,1)S(1)}, bf16[1024,256]{1,0:T(8,128)(2,1)S(1)}, bf16[256,256]{1,0:T(8,128)(2,1)S(1)}) custom-call(s32[8,1024]{1,0:T(8,128)S(1)} %bitcast.5, f32[8,1024,256]{2,1,0:T(8,128)} %own_edges.1.pre_ref, bf16[128,256]{1,0:T(8,128)(2,1)S(1)} %collective-permute-done.prev_ref, ...), custom_call_target="tpu_custom_call" | custom-call | flops 1073741824 | bytes 10650624 | tf_op jit(solution)/shard_map/edges/pallas_call | solution.py:29
  29.9 2.9 %collective-permute-start.2 = (bf16[256,256]{1,0:T(8,128)(2,1)S(1)}, bf16[256,256]{1,0:T(8,128)(2,1)S(1)}, u32[]{:S(2)}, u32[]{:S(2)}) collective-permute-start(bf16[256,256]{1,0:T(8,128)(2,1)S(1)} %get-tuple-element.18), channel_id=1, source_target_pairs={{0,2},{1,3},{2,0},{3,1},{4,6},{5,7},{6,4},{7,5},{8,10},{9,11},{10,... | collective-permute-start | bytes 393224 | tf_op jit(solution)/shard_map/ppermute | solution.py:233
  34.6 2.0 %collective-permute-done.4 = bf16[256,256]{1,0:T(8,128)(2,1)S(1)} collective-permute-done((bf16[256,256]{1,0:T(8,128)(2,1)S(1)}, bf16[256,256]{1,0:T(8,128)(2,1)S(1)}, u32[]{:S(2)}, u32[]{:S(2)}) %collective-permute-start.4) | collective-permute-done | bytes 131104 | tf_op jit(solution)/shard_map/ppermute | solution.py:233
  36.6 4.2 %collective-permute-done.3 = bf16[256,256]{1,0:T(8,128)(2,1)S(1)} collective-permute-done((bf16[256,256]{1,0:T(8,128)(2,1)S(1)}, bf16[256,256]{1,0:T(8,128)(2,1)S(1)}, u32[]{:S(2)}, u32[]{:S(2)}) %collective-permute-start.3) | collective-permute-done | bytes 131104 | tf_op jit(solution)/shard_map/ppermute | solution.py:233
  41.0 4.5 %collective-permute-done.8.refs_1_ = bf16[1024,256]{1,0:T(8,128)(2,1)S(1)} collective-permute-done((bf16[1024,256]{1,0:T(8,128)(2,1)S(1)}, bf16[1024,256]{1,0:T(8,128)(2,1)S(1)}, u32[]{:S(2)}, u32[]{:S(2)}) %collective-permute-start.8) | collective-permute-done | bytes 524320 | tf_op jit(solution)/shard_map/ppermute | solution.py:233
  47.8 4.8 %up_own.1 = (bf16[2048,1024]{1,0:T(8,128)(2,1)}, f32[2048,256]{1,0:T(8,128)S(1)}) custom-call(bf16[1024,256]{1,0:T(8,128)(2,1)S(1)} %get-tuple-element.17.refs_0_, bf16[2048,256]{1,0:T(8,128)(2,1)S(1)} %constant_dynamic-update-slice_fusion.refs_1_.refs_2_, bf16[256,256]{1,0:T(8,128)(2,1)S(1)} %copy-done.13, bf16[256,256]{1,0:T(8,128)(2,1)S(1)} %copy-done.14), custom_call_target="tpu_custom_call" | custom-call | flops 2415919104 | bytes 8126464 | tf_op jit(solution)/shard_map/up_own/pallas_call | solution.py:29
  53.9 8.5 %up_xy.1 = (bf16[2048,1024]{1,0:T(8,128)(2,1)}, bf16[2048,1024]{1,0:T(8,128)(2,1)}, f32[2048,256]{1,0:T(8,128)S(1)}) custom-call(bf16[1024,256]{1,0:T(8,128)(2,1)S(1)} %collective-permute-done.6.refs_0_, bf16[1024,256]{1,0:T(8,128)(2,1)S(1)} %collective-permute-done.8.refs_1_, bf16[2048,256]{1,0:T(8,128)(2,1)S(1)} %constant_dynamic-update-slice_fusion.refs_1_.refs_2_, ...), custom_call_target="tpu_custom_call" | custom-call | flops 4831838208 | bytes 14942208 | tf_op jit(solution)/shard_map/up_xy/pallas_call | solution.py:29
  63.7 5.9 %up_diagonal.1 = (bf16[2048,512]{1,0:T(8,128)(2,1)S(1)}, bf16[2048,512]{1,0:T(8,128)(2,1)}, bf16[2048,256]{1,0:T(8,128)(2,1)S(1)}) custom-call(bf16[512,256]{1,0:T(8,128)(2,1)S(1)} %collective-permute-done.7.refs_0_, bf16[512,256]{1,0:T(8,128)(2,1)S(1)} %collective-permute-done.9.refs_1_, ...), custom_call_target="tpu_custom_call" | custom-call | flops 2415919104 | bytes 9175040 | tf_op jit(solution)/shard_map/up_diagonal/pallas_call | solution.py:29
  71.9 2.1 %collective-permute-start.13 = (bf16[256,256]{1,0:T(8,128)(2,1)S(1)}, bf16[256,256]{1,0:T(8,128)(2,1)S(1)}, u32[]{:S(2)}, u32[]{:S(2)}) collective-permute-start(bf16[256,256]{1,0:T(8,128)(2,1)S(1)} %get-tuple-element.31), channel_id=1, source_target_pairs={{0,6},{1,7},{2,4},{3,5},{4,2},{5,3},{6,0},{7,1},{8,14},{9,15},{10,... | collective-permute-start | bytes 393224 | tf_op jit(solution)/shard_map/ppermute | solution.py:233
  75.3 2.7 %collective-permute-done.11 = bf16[256,256]{1,0:T(8,128)(2,1)S(1)} collective-permute-done((bf16[256,256]{1,0:T(8,128)(2,1)S(1)}, bf16[256,256]{1,0:T(8,128)(2,1)S(1)}, u32[]{:S(2)}, u32[]{:S(2)}) %collective-permute-start.11) | collective-permute-done | bytes 131104 | tf_op jit(solution)/shard_map/ppermute | solution.py:233
  78.1 3.2 %collective-permute-done.13 = bf16[256,256]{1,0:T(8,128)(2,1)S(1)} collective-permute-done((bf16[256,256]{1,0:T(8,128)(2,1)S(1)}, bf16[256,256]{1,0:T(8,128)(2,1)S(1)}, u32[]{:S(2)}, u32[]{:S(2)}) %collective-permute-start.13) | collective-permute-done | bytes 131104 | tf_op jit(solution)/shard_map/ppermute | solution.py:233
  81.2 5.8 %collective-permute-done.12 = bf16[256,256]{1,0:T(8,128)(2,1)S(1)} collective-permute-done((bf16[256,256]{1,0:T(8,128)(2,1)S(1)}, bf16[256,256]{1,0:T(8,128)(2,1)S(1)}, u32[]{:S(2)}, u32[]{:S(2)}) %collective-permute-start.12) | collective-permute-done | bytes 131104 | tf_op jit(solution)/shard_map/ppermute | solution.py:233
  88.6 3.0 %collective-permute-start.14 = (bf16[256,256]{1,0:T(8,128)(2,1)S(1)}, bf16[256,256]{1,0:T(8,128)(2,1)S(1)}, u32[]{:S(2)}, u32[]{:S(2)}) collective-permute-start(bf16[256,256]{1,0:T(8,128)(2,1)S(1)} %get-tuple-element.29), channel_id=1, source_target_pairs={{0,2},{1,3},{2,0},{3,1},{4,6},{5,7},{6,4},{7,5},{8,10},{9,11},{10,... | collective-permute-start | bytes 393224 | tf_op jit(solution)/shard_map/ppermute | solution.py:233
  91.6 3.9 %collective-permute-done.16 = bf16[256,256]{1,0:T(8,128)(2,1)S(1)} collective-permute-done((bf16[256,256]{1,0:T(8,128)(2,1)S(1)}, bf16[256,256]{1,0:T(8,128)(2,1)S(1)}, u32[]{:S(2)}, u32[]{:S(2)}) %collective-permute-start.16) | collective-permute-done | bytes 131104 | tf_op jit(solution)/shard_map/ppermute | solution.py:233
  95.5 3.6 %collective-permute-done.15 = bf16[256,256]{1,0:T(8,128)(2,1)S(1)} collective-permute-done((bf16[256,256]{1,0:T(8,128)(2,1)S(1)}, bf16[256,256]{1,0:T(8,128)(2,1)S(1)}, u32[]{:S(2)}, u32[]{:S(2)}) %collective-permute-start.15) | collective-permute-done | bytes 131104 | tf_op jit(solution)/shard_map/ppermute | solution.py:233
  101.1 2.5 %down_y.1 = bf16[1024,256]{1,0:T(8,128)(2,1)S(1)} custom-call(bf16[2048,1024]{1,0:T(8,128)(2,1)S(1)} %copy-done.1, bf16[2048,256]{1,0:T(8,128)(2,1)S(1)} %constant_dynamic-update-slice_fusion.5.sums_ref), custom_call_target="tpu_custom_call" | custom-call | flops 1073741824 | bytes 5767168 | tf_op jit(solution)/shard_map/down_y/pallas_call | solution.py:29
  103.7 2.5 %down_x.1 = bf16[1024,256]{1,0:T(8,128)(2,1)S(1)} custom-call(bf16[2048,1024]{1,0:T(8,128)(2,1)S(1)} %copy-done, bf16[2048,256]{1,0:T(8,128)(2,1)S(1)} %constant_dynamic-update-slice_fusion.5.sums_ref), custom_call_target="tpu_custom_call" | custom-call | flops 1073741824 | bytes 5767168 | tf_op jit(solution)/shard_map/down_x/pallas_call | solution.py:29
  112.2 4.0 %down_own.1.own_ref = f32[1024,256]{1,0:T(8,128)S(1)} custom-call(bf16[2048,1024]{1,0:T(8,128)(2,1)} %get-tuple-element.19.tile_ref, bf16[2048,256]{1,0:T(8,128)(2,1)S(1)} %constant_dynamic-update-slice_fusion.5.sums_ref), custom_call_target="tpu_custom_call" | custom-call | flops 1073741824 | bytes 6291456 | tf_op jit(solution)/shard_map/down_own/pallas_call | solution.py:29
  116.3 8.2 %collective-permute-done.20.c_ref = bf16[1024,256]{1,0:T(8,128)(2,1)S(1)} collective-permute-done((bf16[1024,256]{1,0:T(8,128)(2,1)S(1)}, bf16[1024,256]{1,0:T(8,128)(2,1)S(1)}, u32[]{:S(2)}, u32[]{:S(2)}) %collective-permute-start.20) | collective-permute-done | bytes 524320 | tf_op jit(solution)/shard_map/ppermute | solution.py:239
  124.5 10.5 %collective-permute-done.18.a_ref = bf16[1024,256]{1,0:T(8,128)(2,1)S(1)} collective-permute-done((bf16[1024,256]{1,0:T(8,128)(2,1)S(1)}, bf16[1024,256]{1,0:T(8,128)(2,1)S(1)}, u32[]{:S(2)}, u32[]{:S(2)}) %collective-permute-start.18) | collective-permute-done | bytes 524320 | tf_op jit(solution)/shard_map/ppermute | solution.py:233
  134.9 2.2 %last.1 = (bf16[1024,256]{1,0:T(8,128)(2,1)}, f32[1024,256]{1,0:T(8,128)}) custom-call(f32[1024,256]{1,0:T(8,128)S(1)} %down_own.1.own_ref, bf16[1024,256]{1,0:T(8,128)(2,1)S(1)} %collective-permute-done.18.a_ref, bf16[1024,256]{1,0:T(8,128)(2,1)S(1)} %collective-permute-done.19.b_ref, bf16[1024,256]{1,0:T(8,128)(2,1)S(1)} %collective-permute-done.20.c_ref, ...), custom_call_target="tpu_custom_call" | custom-call | flops 134217728 | bytes 4849664 | tf_op jit(solution)/shard_map/last/pallas_call | solution.py:29
  (84 shorter events, 28.0 us)
Async XLA Ops:
  2.7 17.7 %collective-permute-start = (bf16[128,256]{1,0:T(8,128)(2,1)S(1)}, bf16[128,256]{1,0:T(8,128)(2,1)S(1)}, u32[]{:S(2)}, u32[]{:S(2)}) collective-permute-start(bf16[128,256]{1,0:T(8,128)(2,1)S(1)} %get-tuple-element.15), channel_id=1, source_target_pairs={{0,1},{1,2},{2,3},{3,4},{4,5},{5,6},{6,7},{7,8},{8,9},{9,10},{10,1... | collective-permute-start | bytes 196616 | tf_op jit(solution)/shard_map/ppermute | solution.py:258
  5.7 14.7 %collective-permute-start.1 = (bf16[128,256]{1,0:T(8,128)(2,1)S(1)}, bf16[128,256]{1,0:T(8,128)(2,1)S(1)}, u32[]{:S(2)}, u32[]{:S(2)}) collective-permute-start(bf16[128,256]{1,0:T(8,128)(2,1)S(1)} %get-tuple-element.16), channel_id=1, source_target_pairs={{1,0},{2,1},{3,2},{4,3},{5,4},{6,5},{7,6},{8,7},{9,8},{10,9},{11,1... | collective-permute-start | bytes 196616 | tf_op jit(solution)/shard_map/ppermute | solution.py:259
  28.3 19.5 %copy-start.13 = (bf16[256,256]{1,0:T(8,128)(2,1)S(1)}, bf16[256,256]{1,0:T(8,128)(2,1)}, u32[]{:S(2)}) copy-start(bf16[256,256]{1,0:T(8,128)(2,1)} %refs_3_.5) | copy-start | bytes 393220
  28.3 8.3 %collective-permute-start.4 = (bf16[256,256]{1,0:T(8,128)(2,1)S(1)}, bf16[256,256]{1,0:T(8,128)(2,1)S(1)}, u32[]{:S(2)}, u32[]{:S(2)}) collective-permute-start(bf16[256,256]{1,0:T(8,128)(2,1)S(1)} %get-tuple-element.18), channel_id=1, source_target_pairs={{0,6},{1,7},{2,4},{3,5},{4,2},{5,3},{6,0},{7,1},{8,14},{9,15},{10,... | collective-permute-start | bytes 393224 | tf_op jit(solution)/shard_map/ppermute | solution.py:233
  29.9 10.9 %collective-permute-start.3 = (bf16[256,256]{1,0:T(8,128)(2,1)S(1)}, bf16[256,256]{1,0:T(8,128)(2,1)S(1)}, u32[]{:S(2)}, u32[]{:S(2)}) collective-permute-start(bf16[256,256]{1,0:T(8,128)(2,1)S(1)} %get-tuple-element.18), channel_id=1, source_target_pairs={{0,4},{1,5},{2,6},{3,7},{4,0},{5,1},{6,2},{7,3},{8,12},{9,13},{10,... | collective-permute-start | bytes 393224 | tf_op jit(solution)/shard_map/ppermute | solution.py:233
  29.9 10.9 %collective-permute-start.2 = (bf16[256,256]{1,0:T(8,128)(2,1)S(1)}, bf16[256,256]{1,0:T(8,128)(2,1)S(1)}, u32[]{:S(2)}, u32[]{:S(2)}) collective-permute-start(bf16[256,256]{1,0:T(8,128)(2,1)S(1)} %get-tuple-element.18), channel_id=1, source_target_pairs={{0,2},{1,3},{2,0},{3,1},{4,6},{5,7},{6,4},{7,5},{8,10},{9,11},{10,... | collective-permute-start | bytes 393224 | tf_op jit(solution)/shard_map/ppermute | solution.py:233
  32.7 12.7 %collective-permute-start.8 = (bf16[1024,256]{1,0:T(8,128)(2,1)S(1)}, bf16[1024,256]{1,0:T(8,128)(2,1)S(1)}, u32[]{:S(2)}, u32[]{:S(2)}) collective-permute-start(bf16[1024,256]{1,0:T(8,128)(2,1)S(1)} %get-tuple-element.17.refs_0_), channel_id=1, source_target_pairs={{0,1},{1,0},{2,3},{3,2},{4,5},{5,4},{6,7},{7,6},{8,9},{9,8},{10,11... | collective-permute-start | bytes 1572872 | tf_op jit(solution)/shard_map/ppermute | solution.py:233
  32.7 14.3 %collective-permute-start.6 = (bf16[1024,256]{1,0:T(8,128)(2,1)S(1)}, bf16[1024,256]{1,0:T(8,128)(2,1)S(1)}, u32[]{:S(2)}, u32[]{:S(2)}) collective-permute-start(bf16[1024,256]{1,0:T(8,128)(2,1)S(1)} %get-tuple-element.17.refs_0_), channel_id=1, source_target_pairs={{0,16},{8,24},{16,0},{24,8},{1,17},{9,25},{17,1},{25,9},{2,18},{10... | collective-permute-start | bytes 1572872 | tf_op jit(solution)/shard_map/ppermute | solution.py:233
  40.8 6.9 %collective-permute-start.5 = (bf16[1024,256]{1,0:T(8,128)(2,1)S(1)}, bf16[1024,256]{1,0:T(8,128)(2,1)S(1)}, u32[]{:S(2)}, u32[]{:S(2)}) collective-permute-start(bf16[1024,256]{1,0:T(8,128)(2,1)S(1)} %pad_maximum_fusion), channel_id=1, source_target_pairs={{0,8},{8,0},{16,24},{24,16},{1,9},{9,1},{17,25},{25,17},{2,10},{10... | collective-permute-start | bytes 1572872 | tf_op jit(solution)/shard_map/ppermute | solution.py:233
  45.5 18.2 %collective-permute-start.9 = (bf16[512,256]{1,0:T(8,128)(2,1)S(1)}, bf16[512,256]{1,0:T(8,128)(2,1)S(1)}, u32[]{:S(2)}, u32[]{:S(2)}) collective-permute-start(bf16[512,256]{1,0:T(8,128)(2,1)S(1)} %slice.33), channel_id=1, source_target_pairs={{0,16},{8,24},{16,0},{24,8},{1,17},{9,25},{17,1},{25,9},{2,18},{10... | collective-permute-start | bytes 786440 | tf_op jit(solution)/shard_map/ppermute | solution.py:233
  47.1 16.6 %collective-permute-start.7 = (bf16[512,256]{1,0:T(8,128)(2,1)S(1)}, bf16[512,256]{1,0:T(8,128)(2,1)S(1)}, u32[]{:S(2)}, u32[]{:S(2)}) collective-permute-start(bf16[512,256]{1,0:T(8,128)(2,1)S(1)} %slice.32), channel_id=1, source_target_pairs={{0,1},{1,0},{2,3},{3,2},{4,5},{5,4},{6,7},{7,6},{8,9},{9,8},{10,11... | collective-permute-start | bytes 786440 | tf_op jit(solution)/shard_map/ppermute | solution.py:233
  69.6 31.5 %copy-start.1 = (bf16[2048,1024]{1,0:T(8,128)(2,1)S(1)}, bf16[2048,1024]{1,0:T(8,128)(2,1)}, u32[]{:S(2)}) copy-start(bf16[2048,1024]{1,0:T(8,128)(2,1)} %get-tuple-element.24.tile_ref) | copy-start | bytes 12582916
  69.6 2.0 %collective-permute-start.10 = (bf16[1024,256]{1,0:T(8,128)(2,1)S(1)}, bf16[1024,256]{1,0:T(8,128)(2,1)S(1)}, u32[]{:S(2)}, u32[]{:S(2)}) collective-permute-start(bf16[1024,256]{1,0:T(8,128)(2,1)S(1)} %slice.27), channel_id=1, source_target_pairs={{0,8},{8,0},{16,24},{24,16},{1,9},{9,1},{17,25},{25,17},{2,10},{10... | collective-permute-start | bytes 1572872 | tf_op jit(solution)/shard_map/ppermute | solution.py:233
  71.8 6.3 %collective-permute-start.11 = (bf16[256,256]{1,0:T(8,128)(2,1)S(1)}, bf16[256,256]{1,0:T(8,128)(2,1)S(1)}, u32[]{:S(2)}, u32[]{:S(2)}) collective-permute-start(bf16[256,256]{1,0:T(8,128)(2,1)S(1)} %get-tuple-element.30), channel_id=1, source_target_pairs={{0,2},{1,3},{2,0},{3,1},{4,6},{5,7},{6,4},{7,5},{8,10},{9,11},{10,... | collective-permute-start | bytes 393224 | tf_op jit(solution)/shard_map/ppermute | solution.py:233
  71.9 9.4 %collective-permute-start.13 = (bf16[256,256]{1,0:T(8,128)(2,1)S(1)}, bf16[256,256]{1,0:T(8,128)(2,1)S(1)}, u32[]{:S(2)}, u32[]{:S(2)}) collective-permute-start(bf16[256,256]{1,0:T(8,128)(2,1)S(1)} %get-tuple-element.31), channel_id=1, source_target_pairs={{0,6},{1,7},{2,4},{3,5},{4,2},{5,3},{6,0},{7,1},{8,14},{9,15},{10,... | collective-permute-start | bytes 393224 | tf_op jit(solution)/shard_map/ppermute | solution.py:233
  74.0 13.0 %collective-permute-start.12 = (bf16[256,256]{1,0:T(8,128)(2,1)S(1)}, bf16[256,256]{1,0:T(8,128)(2,1)S(1)}, u32[]{:S(2)}, u32[]{:S(2)}) collective-permute-start(bf16[256,256]{1,0:T(8,128)(2,1)S(1)} %get-tuple-element.32), channel_id=1, source_target_pairs={{0,4},{1,5},{2,6},{3,7},{4,0},{5,1},{6,2},{7,3},{8,12},{9,13},{10,... | collective-permute-start | bytes 393224 | tf_op jit(solution)/shard_map/ppermute | solution.py:233
  87.1 8.4 %collective-permute-start.16 = (bf16[256,256]{1,0:T(8,128)(2,1)S(1)}, bf16[256,256]{1,0:T(8,128)(2,1)S(1)}, u32[]{:S(2)}, u32[]{:S(2)}) collective-permute-start(bf16[256,256]{1,0:T(8,128)(2,1)S(1)} %get-tuple-element.29), channel_id=1, source_target_pairs={{0,6},{1,7},{2,4},{3,5},{4,2},{5,3},{6,0},{7,1},{8,14},{9,15},{10,... | collective-permute-start | bytes 393224 | tf_op jit(solution)/shard_map/ppermute | solution.py:233
  88.6 10.5 %collective-permute-start.15 = (bf16[256,256]{1,0:T(8,128)(2,1)S(1)}, bf16[256,256]{1,0:T(8,128)(2,1)S(1)}, u32[]{:S(2)}, u32[]{:S(2)}) collective-permute-start(bf16[256,256]{1,0:T(8,128)(2,1)S(1)} %get-tuple-element.29), channel_id=1, source_target_pairs={{0,4},{1,5},{2,6},{3,7},{4,0},{5,1},{6,2},{7,3},{8,12},{9,13},{10,... | collective-permute-start | bytes 393224 | tf_op jit(solution)/shard_map/ppermute | solution.py:233
  88.6 10.5 %collective-permute-start.14 = (bf16[256,256]{1,0:T(8,128)(2,1)S(1)}, bf16[256,256]{1,0:T(8,128)(2,1)S(1)}, u32[]{:S(2)}, u32[]{:S(2)}) collective-permute-start(bf16[256,256]{1,0:T(8,128)(2,1)S(1)} %get-tuple-element.29), channel_id=1, source_target_pairs={{0,2},{1,3},{2,0},{3,1},{4,6},{5,7},{6,4},{7,5},{8,10},{9,11},{10,... | collective-permute-start | bytes 393224 | tf_op jit(solution)/shard_map/ppermute | solution.py:233
  99.1 2.0 %collective-permute-start.17 = (bf16[1024,256]{1,0:T(8,128)(2,1)S(1)}, bf16[1024,256]{1,0:T(8,128)(2,1)S(1)}, u32[]{:S(2)}, u32[]{:S(2)}) collective-permute-start(bf16[1024,256]{1,0:T(8,128)(2,1)S(1)} %pad_maximum_fusion.1), channel_id=1, source_target_pairs={{0,8},{8,0},{16,24},{24,16},{1,9},{9,1},{17,25},{25,17},{2,10},{10... | collective-permute-start | bytes 1572872 | tf_op jit(solution)/shard_map/ppermute | solution.py:233
  108.6 26.3 %copy-start.8 = (bf16[256,256]{1,0:T(8,128)(2,1)S(1)}, bf16[256,256]{1,0:T(8,128)(2,1)}, u32[]{:S(2)}) copy-start(bf16[256,256]{1,0:T(8,128)(2,1)} %w_out_ref.1) | copy-start | bytes 393220
  108.7 15.8 %collective-permute-start.20 = (bf16[1024,256]{1,0:T(8,128)(2,1)S(1)}, bf16[1024,256]{1,0:T(8,128)(2,1)S(1)}, u32[]{:S(2)}, u32[]{:S(2)}) collective-permute-start(bf16[1024,256]{1,0:T(8,128)(2,1)S(1)} %pad_maximum_fusion.2), channel_id=1, source_target_pairs={{0,17},{1,16},{2,19},{3,18},{4,21},{5,20},{6,23},{7,22},{8,25},{9,... | collective-permute-start | bytes 1572872 | tf_op jit(solution)/shard_map/ppermute | solution.py:239
  110.2 24.7 %collective-permute-start.18 = (bf16[1024,256]{1,0:T(8,128)(2,1)S(1)}, bf16[1024,256]{1,0:T(8,128)(2,1)S(1)}, u32[]{:S(2)}, u32[]{:S(2)}) collective-permute-start(bf16[1024,256]{1,0:T(8,128)(2,1)S(1)} %down_x.1), channel_id=1, source_target_pairs={{0,16},{8,24},{16,0},{24,8},{1,17},{9,25},{17,1},{25,9},{2,18},{10... | collective-permute-start | bytes 1572872 | tf_op jit(solution)/shard_map/ppermute | solution.py:233
  111.7 23.2 %collective-permute-start.19 = (bf16[1024,256]{1,0:T(8,128)(2,1)S(1)}, bf16[1024,256]{1,0:T(8,128)(2,1)S(1)}, u32[]{:S(2)}, u32[]{:S(2)}) collective-permute-start(bf16[1024,256]{1,0:T(8,128)(2,1)S(1)} %down_y.1), channel_id=1, source_target_pairs={{0,1},{1,0},{2,3},{3,2},{4,5},{5,4},{6,7},{7,6},{8,9},{9,8},{10,11... | collective-permute-start | bytes 1572872 | tf_op jit(solution)/shard_map/ppermute | solution.py:233
  (15 other events, 68.1 us)

commit v2 on v1

--- a/solution.py
+++ b/solution.py
@@ -23,7 +23,7 @@
     return pl.BlockSpec(shape, lambda *_: (0,) * len(shape))
 
 
-def call(body, name, out_shape, in_specs, out_specs, args, grid=(1,), scratch=(), flops=0, exps=0):
+def call(body, name, out_shape, in_specs, out_specs, args, grid=(1,), scratch=(), flops=0, exps=0, limit=VMEM_LIMIT):
     outs = out_shape if isinstance(out_shape, (list, tuple)) else [out_shape]
     moved = sum(a.size * a.dtype.itemsize for a in (*args, *outs))
     return pl.pallas_call(
@@ -34,7 +34,7 @@
         out_shape=out_shape,
         scratch_shapes=list(scratch),
         name=name,
-        compiler_params=pltpu.CompilerParams(vmem_limit_bytes=VMEM_LIMIT),
+        compiler_params=pltpu.CompilerParams(vmem_limit_bytes=limit),
         cost_estimate=pl.CostEstimate(flops=flops, bytes_accessed=moved, transcendentals=exps),
     )(*args)
 
@@ -91,6 +91,7 @@
     w_src_ref,
     w_msg_ref,
     w_key_ref,
+    w_query_ref,
     updated_ref,
     normed_ref,
     keys_ref,
@@ -123,86 +124,75 @@
 
     @pl.when(step == pl.num_programs(0) - 1)
     def _():
-        keys_ref[...] = dot(picked(ids_ref[...], table[...]), w_key_ref[...]).astype(BF16)
-
-
-def smooth_up_body(count, scale, has_start, *refs):
-    nodes, refs = refs[:count], refs[count:]
-    keys_ref, w_query_ref, w_value_ref, *refs = refs
-    if has_start:
-        start_ref, *refs = refs
-    tiles, refs = refs[:count], refs[count:]
-    sums_ref, *refs = refs
-    query, value = refs[:count], refs[count:]
-
-    @pl.when(pl.program_id(0) == 0)
-    def _():
-        for b in range(count):
-            query[b][...] = dot(nodes[b][...], w_query_ref[...]).astype(BF16)
-            value[b][...] = dot(nodes[b][...], w_value_ref[...]).astype(BF16)
-
-    total = start_ref[...] if has_start else 0.0
-    for b in range(count):
-        tile = jnp.exp2(dot(keys_ref[...], query[b][...], 1, 1) * scale).astype(BF16)
-        tiles[b][...] = tile
-        total += dot(tile, value[b][...])
-    sums_ref[...] = total.astype(sums_ref.dtype)
-
-
-def smooth_up(blocks, keys, w_query, w_value, start, out_dtype, name):
+        keys = dot(picked(ids_ref[...], table[...]), w_key_ref[...]).astype(BF16)
+        keys_ref[...] = dot(keys, w_query_ref[...], 1, 1).astype(BF16)
+
+
+def smooth_up_body(count, scale, *refs):
+    nodes, keys_ref, tiles, sums_ref = refs[:count], refs[count], refs[count + 1 : -1], refs[-1]
+    total = 0.0
+    for node_ref, tile_ref in zip(nodes, tiles):
+        tile = jnp.exp2(dot(keys_ref[...], node_ref[...], 1, 1) * scale).astype(BF16)
+        tile_ref[...] = tile
+        total += dot(tile, node_ref[...])
+    sums_ref[...] = total.astype(BF16)
+
+
+def smooth_up(blocks, keys, name):
     marks, c = keys.shape
     step = min(marks, 512)
     scale = 2.0 * c ** (-0.5) * math.log2(math.e)
     sizes = [b.shape[0] for b in blocks]
-    in_specs = [whole(b.shape) for b in blocks]
-    in_specs += [pl.BlockSpec((step, c), lambda j: (j, 0)), whole((c, c)), whole((c, c))]
-    args = [*blocks, keys, w_query, w_value]
-    if start is not None:
-        in_specs.append(pl.BlockSpec((step, c), lambda j: (j, 0)))
-        args.append(start)
+    keys_spec = pl.BlockSpec((step, c), lambda j: (j, 0))
     out = call(
-        functools.partial(smooth_up_body, len(blocks), scale, start is not None),
+        functools.partial(smooth_up_body, len(blocks), scale),
         name,
         [jax.ShapeDtypeStruct((marks, n), BF16) for n in sizes]
-        + [jax.ShapeDtypeStruct((marks, c), out_dtype)],
-        in_specs,
-        [pl.BlockSpec((step, n), lambda j: (j, 0)) for n in sizes]
-        + [pl.BlockSpec((step, c), lambda j: (j, 0))],
-        args,
+        + [jax.ShapeDtypeStruct((marks, c), BF16)],
+        [whole(b.shape) for b in blocks] + [keys_spec],
+        [pl.BlockSpec((step, n), lambda j: (j, 0)) for n in sizes] + [keys_spec],
+        [*blocks, keys],
         grid=(marks // step,),
-        scratch=[pltpu.VMEM((n, c), BF16) for n in sizes] * 2,
-        flops=4 * marks * sum(sizes) * c + 4 * sum(sizes) * c * c,
+        flops=4 * marks * sum(sizes) * c,
         exps=marks * sum(sizes),
     )
     return out[:-1], out[-1]
 
 
-def smooth_down_body(tile_ref, sums_ref, out_ref):
-    out_ref[...] = dot(tile_ref[...], sums_ref[...], 0, 0).astype(out_ref.dtype)
+def smooth_down_body(count, *refs):
+    tiles, sums, out_ref = refs[:count], refs[count:-1], refs[-1]
+    total = 0.0
+    for tile_ref, sum_ref in zip(tiles, sums):
+        total += dot(tile_ref[...], sum_ref[...], 0, 0)
+    out_ref[...] = total.astype(out_ref.dtype)
 
 
 def smooth_down(tiles, sums, out_dtype, name):
-    marks, n = tiles.shape
-    c = sums.shape[1]
+    n = tiles[0].shape[1]
+    c = sums[0].shape[1]
     step = min(n, 256)
     return call(
-        smooth_down_body,
+        functools.partial(smooth_down_body, len(tiles)),
         name,
         jax.ShapeDtypeStruct((n, c), out_dtype),
-        [pl.BlockSpec((marks, step), lambda j: (0, j)), whole((marks, c))],
+        [pl.BlockSpec((t.shape[0], step), lambda j: (0, j)) for t in tiles]
+        + [whole(v.shape) for v in sums],
         pl.BlockSpec((step, c), lambda j: (j, 0)),
-        [tiles, sums],
+        [*tiles, *sums],
         grid=(n // step,),
-        flops=2 * marks * n * c,
-    )
-
-
-def last_body(own_ref, a_ref, b_ref, c_ref, updated_ref, w_out_ref, result_ref, term_ref):
-    smooth = own_ref[...] + a_ref[...].astype(F32) + b_ref[...].astype(F32) + c_ref[...].astype(F32)
-    term = smooth * lax.rsqrt(jnp.mean(smooth * smooth, axis=1, keepdims=True) + EPS)
-    term_ref[...] = term
-    result = updated_ref[...].astype(F32) + dot(term.astype(BF16), w_out_ref[...])
-    result_ref[...] = result.astype(BF16)
+        flops=sum(2 * t.shape[0] * n * c for t in tiles),
+    )
+
+
+def last_body(own_ref, xa_ref, ya_ref, yb_ref, xb_ref, updated_ref, w_out_ref, result_ref, term_ref):
+    half = own_ref.shape[0] // 2
+    for h, first, second in ((0, xa_ref, ya_ref), (1, yb_ref, xb_ref)):
+        at = slice(h * half, (h + 1) * half)
+        smooth = own_ref[at, :] + first[...].astype(F32) + second[...].astype(F32)
+        term = smooth * lax.rsqrt(jnp.mean(smooth * smooth, axis=1, keepdims=True) + EPS)
+        term_ref[at, :] = term
+        result = updated_ref[at, :].astype(F32) + dot(term.astype(BF16), w_out_ref[...])
+        result_ref[at, :] = result.astype(BF16)
 
 
 def shards(
@@ -236,16 +226,6 @@
     over_x = pair("grp", groups, 2)
     over_y = pair("dom", domains, 1)
     over_z = [pair("dom", domains, 2 * t) for t in range(line)]
-    over_xy = lambda v: lax.ppermute(
-        v,
-        BOTH,
-        [
-            (g * domains + d, (g ^ 2) * domains + (d ^ 1))
-            for g in range(groups)
-            for d in range(domains)
-        ],
-    )
-
     to_prev, to_next = call(
         send_body,
         "send_rows",
@@ -293,6 +273,7 @@
             whole((c, c)),
             whole((c, c)),
             whole((c, c)),
+            whole((c, c)),
         ],
         [tile_spec, tile_spec, whole((mine, c))],
         [
@@ -305,6 +286,7 @@
             w_src,
             w_msg,
             w_key,
+            w_query,
         ],
         grid=(steps,),
         scratch=[pltpu.VMEM((2 * halo, c), BF16), pltpu.VMEM((rows, c), BF16)],
@@ -312,47 +294,53 @@
         exps=slots * rows * c,
     )
 
-    side_keys = jnp.concatenate([keys] + [over_z[t](keys) for t in range(1, line)], axis=0)
-    normed_x = over_x(normed)
-    normed_y = over_y(normed)
-    all_keys = jnp.concatenate([side_keys, over_core(side_keys)], axis=0)
-    normed_a = over_y(normed_x[:half])
-    normed_b = over_x(normed_y[half:])
-
-    (own_tiles,), sums = smooth_up([normed], all_keys, w_query, w_value, None, F32, "up_own")
-    (x_tiles, y_tiles), sums = smooth_up(
-        [normed_x, normed_y], all_keys, w_query, w_value, sums, F32, "up_xy"
-    )
-    (a_tiles, b_tiles), sums = smooth_up(
-        [normed_a, normed_b], all_keys, w_query, w_value, sums, BF16, "up_diagonal"
-    )
-
-    side = line * mine
-    side_sums = (sums[:side].astype(F32) + over_core(sums[side:]).astype(F32)).astype(BF16)
-    blocks = [side_sums[t * mine : (t + 1) * mine] for t in range(line)]
-    arrived = [over_z[t](blocks[t]) for t in range(1, line)]
-    total = blocks[0].astype(F32)
-    for block in arrived:
-        total = total + block.astype(F32)
-    total = total.astype(BF16)
-    side_total = jnp.concatenate([total] + [over_z[t](total) for t in range(1, line)], axis=0)
-    all_total = jnp.concatenate([side_total, over_core(side_total)], axis=0)
-
-    a_part = smooth_down(a_tiles, all_total, BF16, "down_a")
-    b_part = smooth_down(b_tiles, all_total, BF16, "down_b")
-    from_xy = over_xy(jnp.concatenate([a_part, b_part], axis=0))
-    from_x = over_x(smooth_down(x_tiles, all_total, BF16, "down_x"))
-    from_y = over_y(smooth_down(y_tiles, all_total, BF16, "down_y"))
-    own = smooth_down(own_tiles, all_total, F32, "down_own")
+    x_a, y_b = over_x(normed[:half]), over_y(normed[half:])
+    key_blocks = [keys] + [over_z[t](keys) for t in range(1, line)]
+    x_b, y_a = over_x(normed[half:]), over_y(normed[:half])
+    xy_a, xy_b = over_y(x_a), over_x(y_b)
+    part = mine // 2
+    side = line * part
+    near = (normed, x_a, x_b, y_a, y_b)
+    tiles = [[] for _ in range(7)]
+    sums = []
+    for h in range(2):
+        side_keys = jnp.concatenate([k[h * part : (h + 1) * part] for k in key_blocks], axis=0)
+        marks = jnp.concatenate([side_keys, over_core(side_keys)], axis=0)
+        near_tiles, near_sums = smooth_up(near, marks, f"up_near_{h}")
+        far_tiles, far_sums = smooth_up((xy_a, xy_b), marks, f"up_far_{h}")
+        for held, tile in zip(tiles, [*near_tiles, *far_tiles]):
+            held.append(tile)
+        both = (near_sums.astype(F32) + far_sums.astype(F32)).astype(BF16)
+        core_sums = (both[:side].astype(F32) + over_core(both[side:]).astype(F32)).astype(BF16)
+        blocks = [core_sums[t * part : (t + 1) * part] for t in range(line)]
+        total = blocks[0].astype(F32)
+        for t in range(1, line):
+            total = total + over_z[t](blocks[t]).astype(F32)
+        total = dot(total.astype(BF16), w_value).astype(BF16)
+        side_sums = jnp.concatenate([total] + [over_z[t](total) for t in range(1, line)], axis=0)
+        sums.append(jnp.concatenate([side_sums, over_core(side_sums)], axis=0))
+
+    def down(block, dtype, name):
+        return smooth_down(tiles[block], sums, dtype, name)
+
+    own_tiles, x_a_tiles, x_b_tiles, y_a_tiles, y_b_tiles, xy_a_tiles, xy_b_tiles = range(7)
+    far_a = over_x(down(xy_a_tiles, BF16, "down_far_a"))
+    far_b = over_y(down(xy_b_tiles, BF16, "down_far_b"))
+    first_a = over_x(down(x_a_tiles, BF16, "down_x_a"))
+    first_b = over_y(down(y_b_tiles, BF16, "down_y_b"))
+    pass_a = down(y_a_tiles, F32, "down_y_a")
+    pass_b = down(x_b_tiles, F32, "down_x_b")
+    second_a = over_y((pass_a + far_a.astype(F32)).astype(BF16))
+    second_b = over_x((pass_b + far_b.astype(F32)).astype(BF16))
+    own = down(own_tiles, F32, "down_own")
 
     return call(
         last_body,
         "last",
         [jax.ShapeDtypeStruct((rows, c), BF16), jax.ShapeDtypeStruct((rows, c), F32)],
-        [tile_spec] * 5 + [whole((c, c))],
-        [tile_spec] * 2,
-        [own, from_x, from_y, from_xy, updated, w_out],
-        grid=(steps,),
+        [whole((rows, c))] + [whole((half, c))] * 4 + [whole((rows, c)), whole((c, c))],
+        [whole((rows, c))] * 2,
+        [own, first_a, second_a, first_b, second_b, updated, w_out],
         flops=2 * rows * c * c,
     )
 

time: 138 us -> 125 us (0.906)
  waiting for transfers between devices: 52.3 us -> 30.8 us
  starting transfers between devices: 26.8 us -> 41.4 us
  Pallas kernels: 47.9 us -> 43.9 us
  local copies, waits for them, and re-layouts: 8.86 us -> 6.37 us
    ppermute x18 -> x33, starting transfers between devices: 18.8 us -> 34.9 us  [pair(): return lambda v: lax.ppermute(v, axis, [(i, i ^ flip) for i in range(size)])]
    ppermute x18 -> x33, waiting for transfers between devices: 44.1 us -> 30.8 us  [pair(): return lambda v: lax.ppermute(v, axis, [(i, i ^ flip) for i in range(size)])]
    ppermute x1 -> x0, waiting for transfers between devices: 8.2 us -> none  [shards(): lax.ppermute(v, BOTH, [(g * domains + d, (g ^ 2) * domains + (d ^ 1)) for...]
    pallas_call x12 -> x15, Pallas kernels: 47.9 us -> 43.9 us  [call(): pl.pallas_call(body, grid=grid, in_specs=in_specs, out_specs=out_specs, o...]
    unnamed x43 -> x38, local copies, waits for them, and re-layouts: 8.7 us -> 6.12 us
    ppermute x1 -> x0, starting transfers between devices: 1.52 us -> none  [shards(): lax.ppermute(v, BOTH, [(g * domains + d, (g ^ 2) * domains + (d ^ 1)) for...]
  transfers between devices with their start and end apart: 21 -> 35, of which waited for: 12 -> 11; matrix products, arithmetic and copies ran while one was open for 0% -> 1% of each run, Pallas kernels for 18% -> 25%
where the time goes in v2:
time: 125 us; the launch traced here: 124 us
  Pallas kernels  43.9 us (35%)
  starting transfers between devices  41.4 us (33%)
  waiting for transfers between devices  30.8 us (25%)
  local copies, waits for them, and re-layouts  6.37 us (5%)
    pallas_call x15, Pallas kernels, call(): pl.pallas_call(body, grid=grid, in_specs=in_specs, out_specs=out_specs, o...  43.9 us
    ppermute x33, starting transfers between devices, pair(): return lambda v: lax.ppermute(v, axis, [(i, i ^ flip) for i in range(size)])  34.9 us
    ppermute x33, waiting for transfers between devices, pair(): return lambda v: lax.ppermute(v, axis, [(i, i ^ flip) for i in range(size)])  30.8 us
    unnamed x38, local copies, waits for them, and re-layouts  6.12 us
    ppermute x1, starting transfers between devices, shards(): lax.ppermute(to_prev, BOTH, [((i + 1) % parts, i) for i in range(parts)])  3.47 us
    ppermute x1, starting transfers between devices, shards(): lax.ppermute(to_next, BOTH, [(i, (i + 1) % parts) for i in range(parts)])  3.02 us
  transfers between devices with their start and end apart: 35, of which 11 were waited for; matrix products, arithmetic and copies ran while one was open for 1% of the time, Pallas kernels for 25%

profile of v2, /device:TPU:0, one launch (start us, length us, event | category | flops | bytes accessed | tf_op | source)
XLA Modules:
  0.0 124.5 jit_solution(16159965065967804035)
XLA Ops:
  2.8 3.0 %collective-permute-start = (bf16[128,256]{1,0:T(8,128)(2,1)S(1)}, bf16[128,256]{1,0:T(8,128)(2,1)S(1)}, u32[]{:S(2)}, u32[]{:S(2)}) collective-permute-start(bf16[128,256]{1,0:T(8,128)(2,1)S(1)} %get-tuple-element.25), channel_id=1, source_target_pairs={{0,1},{1,2},{2,3},{3,4},{4,5},{5,6},{6,7},{7,8},{8,9},{9,10},{10,1... | collective-permute-start | bytes 196616 | tf_op jit(solution)/shard_map/ppermute | solution.py:238
  5.8 3.5 %collective-permute-start.1 = (bf16[128,256]{1,0:T(8,128)(2,1)S(1)}, bf16[128,256]{1,0:T(8,128)(2,1)S(1)}, u32[]{:S(2)}, u32[]{:S(2)}) collective-permute-start(bf16[128,256]{1,0:T(8,128)(2,1)S(1)} %get-tuple-element.26), channel_id=1, source_target_pairs={{1,0},{2,1},{3,2},{4,3},{5,4},{6,5},{7,6},{8,7},{9,8},{10,9},{11,1... | collective-permute-start | bytes 196616 | tf_op jit(solution)/shard_map/ppermute | solution.py:239
  13.6 6.9 %own_edges.1.pre_ref = f32[8,1024,256]{2,1,0:T(8,128)} custom-call(s32[8,1024]{1,0:T(8,128)S(1)} %bitcast.6, bf16[1024,256]{1,0:T(8,128)(2,1)S(1)} %copy-done.3, bf16[1024,256]{1,0:T(8,128)(2,1)S(1)} %copy-done.3, bf16[256,256]{1,0:T(8,128)(2,1)S(1)} %copy-done.6, bf16[256,256]{1,0:T(8,128)(2,1)S(1)} %copy-done.14, f32[1,256]{1,0:T(1,128)S(1)} %bitcast.10), custom_call_target="tpu_custom_call" | custom-call | flops 4294967296 | bytes 9733120 | tf_op jit(solution)/shard_map/own_edges/pallas_call | solution.py:29
  20.5 8.0 %edges.1 = (bf16[1024,256]{1,0:T(8,128)(2,1)S(1)}, bf16[1024,256]{1,0:T(8,128)(2,1)S(1)}, bf16[256,256]{1,0:T(8,128)(2,1)S(1)}) custom-call(s32[8,1024]{1,0:T(8,128)S(1)} %bitcast.7, f32[8,1024,256]{2,1,0:T(8,128)} %own_edges.1.pre_ref, bf16[128,256]{1,0:T(8,128)(2,1)S(1)} %collective-permute-done.prev_ref, ...), custom_call_target="tpu_custom_call" | custom-call | flops 1073741824 | bytes 10781696 | tf_op jit(solution)/shard_map/edges/pallas_call | solution.py:29
  30.1 2.9 %collective-permute-start.6 = (bf16[256,256]{1,0:T(8,128)(2,1)S(1)}, bf16[256,256]{1,0:T(8,128)(2,1)S(1)}, u32[]{:S(2)}, u32[]{:S(2)}) collective-permute-start(bf16[256,256]{1,0:T(8,128)(2,1)S(1)} %get-tuple-element.28), channel_id=1, source_target_pairs={{0,2},{1,3},{2,0},{3,1},{4,6},{5,7},{6,4},{7,5},{8,10},{9,11},{10,... | collective-permute-start | bytes 393224 | tf_op jit(solution)/shard_map/ppermute | solution.py:223
  33.0 1.9 %collective-permute-start.2 = (bf16[512,256]{1,0:T(8,128)(2,1)S(1)}, bf16[512,256]{1,0:T(8,128)(2,1)S(1)}, u32[]{:S(2)}, u32[]{:S(2)}) collective-permute-start(bf16[512,256]{1,0:T(8,128)(2,1)S(1)} %get-tuple-element.49), channel_id=1, source_target_pairs={{0,16},{8,24},{16,0},{24,8},{1,17},{9,25},{17,1},{25,9},{2,18},{10... | collective-permute-start | bytes 786440 | tf_op jit(solution)/shard_map/ppermute | solution.py:223
  34.9 4.7 %collective-permute-done.6 = bf16[256,256]{1,0:T(8,128)(2,1)S(1)} collective-permute-done((bf16[256,256]{1,0:T(8,128)(2,1)S(1)}, bf16[256,256]{1,0:T(8,128)(2,1)S(1)}, u32[]{:S(2)}, u32[]{:S(2)}) %collective-permute-start.6) | collective-permute-done | bytes 131104 | tf_op jit(solution)/shard_map/ppermute | solution.py:223
  43.5 1.8 %collective-permute-start.11 = (bf16[512,256]{1,0:T(8,128)(2,1)S(1)}, bf16[512,256]{1,0:T(8,128)(2,1)S(1)}, u32[]{:S(2)}, u32[]{:S(2)}) collective-permute-start(bf16[512,256]{1,0:T(8,128)(2,1)S(1)} %collective-permute-done.2.refs_1_), channel_id=1, source_target_pairs={{0,1},{1,0},{2,3},{3,2},{4,5},{5,4},{6,7},{7,6},{8,9},{9,8},{10,11... | collective-permute-start | bytes 786440 | tf_op jit(solution)/shard_map/ppermute | solution.py:223
  45.9 5.0 %collective-permute-done.3.refs_2_ = bf16[512,256]{1,0:T(8,128)(2,1)S(1)} collective-permute-done((bf16[512,256]{1,0:T(8,128)(2,1)S(1)}, bf16[512,256]{1,0:T(8,128)(2,1)S(1)}, u32[]{:S(2)}, u32[]{:S(2)}) %collective-permute-start.3) | collective-permute-done | bytes 262176 | tf_op jit(solution)/shard_map/ppermute | solution.py:223
  52.5 5.8 %up_near_0.1 = (bf16[1024,1024]{1,0:T(8,128)(2,1)}, bf16[1024,512]{1,0:T(8,128)(2,1)S(1)}, bf16[1024,512]{1,0:T(8,128)(2,1)S(1)}, bf16[1024,512]{1,0:T(8,128)(2,...) custom-call(bf16[1024,256]{1,0:T(8,128)(2,1)S(1)} %get-tuple-element.27.refs_0_, ...), custom_call_target="tpu_custom_call" | custom-call | flops 3221225472 | bytes 8912896 | tf_op jit(solution)/shard_map/up_near_0/pallas_call | solution.py:29
  58.3 5.8 %up_near_1.1 = (bf16[1024,1024]{1,0:T(8,128)(2,1)}, bf16[1024,512]{1,0:T(8,128)(2,1)S(1)}, bf16[1024,512]{1,0:T(8,128)(2,1)S(1)}, bf16[1024,512]{1,0:T(8,128)(2,...) custom-call(bf16[1024,256]{1,0:T(8,128)(2,1)S(1)} %get-tuple-element.27.refs_0_, ...), custom_call_target="tpu_custom_call" | custom-call | flops 3221225472 | bytes 8912896 | tf_op jit(solution)/shard_map/up_near_1/pallas_call | solution.py:29
  64.1 2.3 %up_far_0.1 = (bf16[1024,512]{1,0:T(8,128)(2,1)S(1)}, bf16[1024,512]{1,0:T(8,128)(2,1)S(1)}, bf16[1024,256]{1,0:T(8,128)(2,1)S(1)}) custom-call(bf16[512,256]{1,0:T(8,128)(2,1)S(1)} %collective-permute-done.11.refs_0_, bf16[512,256]{1,0:T(8,128)(2,1)S(1)} %collective-permute-done.12.refs_1_, ...), custom_call_target="tpu_custom_call" | custom-call | flops 1073741824 | bytes 3670016 | tf_op jit(solution)/shard_map/up_far_0/pallas_call | solution.py:29
  66.7 2.5 %up_far_1.1 = (bf16[1024,512]{1,0:T(8,128)(2,1)S(1)}, bf16[1024,512]{1,0:T(8,128)(2,1)S(1)}, bf16[1024,256]{1,0:T(8,128)(2,1)S(1)}) custom-call(bf16[512,256]{1,0:T(8,128)(2,1)S(1)} %collective-permute-done.11.refs_0_, bf16[512,256]{1,0:T(8,128)(2,1)S(1)} %collective-permute-done.12.refs_1_, ...), custom_call_target="tpu_custom_call" | custom-call | flops 1073741824 | bytes 3670016 | tf_op jit(solution)/shard_map/up_far_1/pallas_call | solution.py:29
  69.9 2.4 %collective-permute-start.16 = (bf16[128,256]{1,0:T(8,128)(2,1)S(1)}, bf16[128,256]{1,0:T(8,128)(2,1)S(1)}, u32[]{:S(2)}, u32[]{:S(2)}) collective-permute-start(bf16[128,256]{1,0:T(8,128)(2,1)S(1)} %get-tuple-element.54), channel_id=1, source_target_pairs={{0,6},{1,7},{2,4},{3,5},{4,2},{5,3},{6,0},{7,1},{8,14},{9,15},{10,... | collective-permute-start | bytes 196616 | tf_op jit(solution)/shard_map/ppermute | solution.py:223
  72.4 2.0 %collective-permute-start.14 = (bf16[128,256]{1,0:T(8,128)(2,1)S(1)}, bf16[128,256]{1,0:T(8,128)(2,1)S(1)}, u32[]{:S(2)}, u32[]{:S(2)}) collective-permute-start(bf16[128,256]{1,0:T(8,128)(2,1)S(1)} %get-tuple-element.53), channel_id=1, source_target_pairs={{0,2},{1,3},{2,0},{3,1},{4,6},{5,7},{6,4},{7,5},{8,10},{9,11},{10,... | collective-permute-start | bytes 196616 | tf_op jit(solution)/shard_map/ppermute | solution.py:223
  74.5 2.4 %collective-permute-start.24 = (bf16[128,256]{1,0:T(8,128)(2,1)S(1)}, bf16[128,256]{1,0:T(8,128)(2,1)S(1)}, u32[]{:S(2)}, u32[]{:S(2)}) collective-permute-start(bf16[128,256]{1,0:T(8,128)(2,1)S(1)} %get-tuple-element.51), channel_id=1, source_target_pairs={{0,6},{1,7},{2,4},{3,5},{4,2},{5,3},{6,0},{7,1},{8,14},{9,15},{10,... | collective-permute-start | bytes 196616 | tf_op jit(solution)/shard_map/ppermute | solution.py:223
  76.9 2.0 %collective-permute-start.22 = (bf16[128,256]{1,0:T(8,128)(2,1)S(1)}, bf16[128,256]{1,0:T(8,128)(2,1)S(1)}, u32[]{:S(2)}, u32[]{:S(2)}) collective-permute-start(bf16[128,256]{1,0:T(8,128)(2,1)S(1)} %get-tuple-element.50), channel_id=1, source_target_pairs={{0,2},{1,3},{2,0},{3,1},{4,6},{5,7},{6,4},{7,5},{8,10},{9,11},{10,... | collective-permute-start | bytes 196616 | tf_op jit(solution)/shard_map/ppermute | solution.py:223
  79.9 3.6 %collective-permute-start.18 = (bf16[128,256]{1,0:T(8,128)(2,1)S(1)}, bf16[128,256]{1,0:T(8,128)(2,1)S(1)}, u32[]{:S(2)}, u32[]{:S(2)}) collective-permute-start(bf16[128,256]{1,0:T(8,128)(2,1)S(1)} %get-tuple-element.73), channel_id=1, source_target_pairs={{0,4},{1,5},{2,6},{3,7},{4,0},{5,1},{6,2},{7,3},{8,12},{9,13},{10,... | collective-permute-start | bytes 196616 | tf_op jit(solution)/shard_map/ppermute | solution.py:223
  85.2 2.9 %collective-permute-start.26 = (bf16[128,256]{1,0:T(8,128)(2,1)S(1)}, bf16[128,256]{1,0:T(8,128)(2,1)S(1)}, u32[]{:S(2)}, u32[]{:S(2)}) collective-permute-start(bf16[128,256]{1,0:T(8,128)(2,1)S(1)} %get-tuple-element.75), channel_id=1, source_target_pairs={{0,4},{1,5},{2,6},{3,7},{4,0},{5,1},{6,2},{7,3},{8,12},{9,13},{10,... | collective-permute-start | bytes 196616 | tf_op jit(solution)/shard_map/ppermute | solution.py:223
  90.2 4.1 %collective-permute-done.26 = bf16[128,256]{1,0:T(8,128)(2,1)S(1)} collective-permute-done((bf16[128,256]{1,0:T(8,128)(2,1)S(1)}, bf16[128,256]{1,0:T(8,128)(2,1)S(1)}, u32[]{:S(2)}, u32[]{:S(2)}) %collective-permute-start.26) | collective-permute-done | bytes 65568 | tf_op jit(solution)/shard_map/ppermute | solution.py:223
  103.2 1.8 %collective-permute-start.33 = (bf16[512,256]{1,0:T(8,128)(2,1)S(1)}, bf16[512,256]{1,0:T(8,128)(2,1)S(1)}, u32[]{:S(2)}, u32[]{:S(2)}) collective-permute-start(bf16[512,256]{1,0:T(8,128)(2,1)S(1)} %down_far_b.1), channel_id=1, source_target_pairs={{0,1},{1,0},{2,3},{3,2},{4,5},{5,4},{6,7},{7,6},{8,9},{9,8},{10,11... | collective-permute-start | bytes 786440 | tf_op jit(solution)/shard_map/ppermute | solution.py:223
  107.7 8.8 %collective-permute-done.33 = bf16[512,256]{1,0:T(8,128)(2,1)S(1)} collective-permute-done((bf16[512,256]{1,0:T(8,128)(2,1)S(1)}, bf16[512,256]{1,0:T(8,128)(2,1)S(1)}, u32[]{:S(2)}, u32[]{:S(2)}) %collective-permute-start.33) | collective-permute-done | bytes 262176 | tf_op jit(solution)/shard_map/ppermute | solution.py:223
  117.2 3.8 %down_own.1.own_ref = f32[1024,256]{1,0:T(8,128)S(1)} custom-call(bf16[1024,1024]{1,0:T(8,128)(2,1)S(1)} %copy-done.1, bf16[1024,1024]{1,0:T(8,128)(2,1)} %get-tuple-element.30.refs_1_, bf16[1024,256]{1,0:T(8,128)(2,1)S(1)} %constant_dynamic-update-slice_fusion.10.refs_2_, bf16[1024,256]{1,0:T(8,128)(2,1)S(1)} %constant_dynamic-update-slice_fusion.15.refs_3_), custom_call_target="tpu_custom_call" | custom-call | flops 1073741824 | bytes 6291456 | tf_op jit(solution)/shard_map/down_own/pallas_call | solution.py:29
  121.1 2.0 %collective-permute-done.34.xb_ref = bf16[512,256]{1,0:T(8,128)(2,1)S(1)} collective-permute-done((bf16[512,256]{1,0:T(8,128)(2,1)S(1)}, bf16[512,256]{1,0:T(8,128)(2,1)S(1)}, u32[]{:S(2)}, u32[]{:S(2)}) %collective-permute-start.34) | collective-permute-done | bytes 262176 | tf_op jit(solution)/shard_map/ppermute | solution.py:223
  (124 shorter events, 33.6 us)
Async XLA Ops:
  2.8 17.7 %collective-permute-start = (bf16[128,256]{1,0:T(8,128)(2,1)S(1)}, bf16[128,256]{1,0:T(8,128)(2,1)S(1)}, u32[]{:S(2)}, u32[]{:S(2)}) collective-permute-start(bf16[128,256]{1,0:T(8,128)(2,1)S(1)} %get-tuple-element.25), channel_id=1, source_target_pairs={{0,1},{1,2},{2,3},{3,4},{4,5},{5,6},{6,7},{7,8},{8,9},{9,10},{10,1... | collective-permute-start | bytes 196616 | tf_op jit(solution)/shard_map/ppermute | solution.py:238
  5.8 14.7 %collective-permute-start.1 = (bf16[128,256]{1,0:T(8,128)(2,1)S(1)}, bf16[128,256]{1,0:T(8,128)(2,1)S(1)}, u32[]{:S(2)}, u32[]{:S(2)}) collective-permute-start(bf16[128,256]{1,0:T(8,128)(2,1)S(1)} %get-tuple-element.26), channel_id=1, source_target_pairs={{1,0},{2,1},{3,2},{4,3},{5,4},{6,5},{7,6},{8,7},{9,8},{10,9},{11,1... | collective-permute-start | bytes 196616 | tf_op jit(solution)/shard_map/ppermute | solution.py:239
  28.5 12.5 %collective-permute-start.8 = (bf16[256,256]{1,0:T(8,128)(2,1)S(1)}, bf16[256,256]{1,0:T(8,128)(2,1)S(1)}, u32[]{:S(2)}, u32[]{:S(2)}) collective-permute-start(bf16[256,256]{1,0:T(8,128)(2,1)S(1)} %get-tuple-element.28), channel_id=1, source_target_pairs={{0,6},{1,7},{2,4},{3,5},{4,2},{5,3},{6,0},{7,1},{8,14},{9,15},{10,... | collective-permute-start | bytes 393224 | tf_op jit(solution)/shard_map/ppermute | solution.py:223
  30.1 10.9 %collective-permute-start.7 = (bf16[256,256]{1,0:T(8,128)(2,1)S(1)}, bf16[256,256]{1,0:T(8,128)(2,1)S(1)}, u32[]{:S(2)}, u32[]{:S(2)}) collective-permute-start(bf16[256,256]{1,0:T(8,128)(2,1)S(1)} %get-tuple-element.28), channel_id=1, source_target_pairs={{0,4},{1,5},{2,6},{3,7},{4,0},{5,1},{6,2},{7,3},{8,12},{9,13},{10,... | collective-permute-start | bytes 393224 | tf_op jit(solution)/shard_map/ppermute | solution.py:223
  30.1 9.5 %collective-permute-start.6 = (bf16[256,256]{1,0:T(8,128)(2,1)S(1)}, bf16[256,256]{1,0:T(8,128)(2,1)S(1)}, u32[]{:S(2)}, u32[]{:S(2)}) collective-permute-start(bf16[256,256]{1,0:T(8,128)(2,1)S(1)} %get-tuple-element.28), channel_id=1, source_target_pairs={{0,2},{1,3},{2,0},{3,1},{4,6},{5,7},{6,4},{7,5},{8,10},{9,11},{10,... | collective-permute-start | bytes 393224 | tf_op jit(solution)/shard_map/ppermute | solution.py:223
  33.0 10.3 %collective-permute-start.2 = (bf16[512,256]{1,0:T(8,128)(2,1)S(1)}, bf16[512,256]{1,0:T(8,128)(2,1)S(1)}, u32[]{:S(2)}, u32[]{:S(2)}) collective-permute-start(bf16[512,256]{1,0:T(8,128)(2,1)S(1)} %get-tuple-element.49), channel_id=1, source_target_pairs={{0,16},{8,24},{16,0},{24,8},{1,17},{9,25},{17,1},{25,9},{2,18},{10... | collective-permute-start | bytes 786440 | tf_op jit(solution)/shard_map/ppermute | solution.py:223
  34.9 8.6 %collective-permute-start.5 = (bf16[512,256]{1,0:T(8,128)(2,1)S(1)}, bf16[512,256]{1,0:T(8,128)(2,1)S(1)}, u32[]{:S(2)}, u32[]{:S(2)}) collective-permute-start(bf16[512,256]{1,0:T(8,128)(2,1)S(1)} %get-tuple-element.48), channel_id=1, source_target_pairs={{0,1},{1,0},{2,3},{3,2},{4,5},{5,4},{6,7},{7,6},{8,9},{9,8},{10,11... | collective-permute-start | bytes 786440 | tf_op jit(solution)/shard_map/ppermute | solution.py:223
  41.8 9.2 %collective-permute-start.3 = (bf16[512,256]{1,0:T(8,128)(2,1)S(1)}, bf16[512,256]{1,0:T(8,128)(2,1)S(1)}, u32[]{:S(2)}, u32[]{:S(2)}) collective-permute-start(bf16[512,256]{1,0:T(8,128)(2,1)S(1)} %get-tuple-element.48), channel_id=1, source_target_pairs={{0,16},{8,24},{16,0},{24,8},{1,17},{9,25},{17,1},{25,9},{2,18},{10... | collective-permute-start | bytes 786440 | tf_op jit(solution)/shard_map/ppermute | solution.py:223
  43.3 9.2 %collective-permute-start.4 = (bf16[512,256]{1,0:T(8,128)(2,1)S(1)}, bf16[512,256]{1,0:T(8,128)(2,1)S(1)}, u32[]{:S(2)}, u32[]{:S(2)}) collective-permute-start(bf16[512,256]{1,0:T(8,128)(2,1)S(1)} %get-tuple-element.49), channel_id=1, source_target_pairs={{0,1},{1,0},{2,3},{3,2},{4,5},{5,4},{6,7},{7,6},{8,9},{9,8},{10,11... | collective-permute-start | bytes 786440 | tf_op jit(solution)/shard_map/ppermute | solution.py:223
  43.5 20.6 %collective-permute-start.11 = (bf16[512,256]{1,0:T(8,128)(2,1)S(1)}, bf16[512,256]{1,0:T(8,128)(2,1)S(1)}, u32[]{:S(2)}, u32[]{:S(2)}) collective-permute-start(bf16[512,256]{1,0:T(8,128)(2,1)S(1)} %collective-permute-done.2.refs_1_), channel_id=1, source_target_pairs={{0,1},{1,0},{2,3},{3,2},{4,5},{5,4},{6,7},{7,6},{8,9},{9,8},{10,11... | collective-permute-start | bytes 786440 | tf_op jit(solution)/shard_map/ppermute | solution.py:223
  45.3 18.8 %collective-permute-start.12 = (bf16[512,256]{1,0:T(8,128)(2,1)S(1)}, bf16[512,256]{1,0:T(8,128)(2,1)S(1)}, u32[]{:S(2)}, u32[]{:S(2)}) collective-permute-start(bf16[512,256]{1,0:T(8,128)(2,1)S(1)} %collective-permute-done.5.refs_4_), channel_id=1, source_target_pairs={{0,16},{8,24},{16,0},{24,8},{1,17},{9,25},{17,1},{25,9},{2,18},{10... | collective-permute-start | bytes 786440 | tf_op jit(solution)/shard_map/ppermute | solution.py:223
  72.3 7.1 %collective-permute-start.15 = (bf16[128,256]{1,0:T(8,128)(2,1)S(1)}, bf16[128,256]{1,0:T(8,128)(2,1)S(1)}, u32[]{:S(2)}, u32[]{:S(2)}) collective-permute-start(bf16[128,256]{1,0:T(8,128)(2,1)S(1)} %get-tuple-element.55), channel_id=1, source_target_pairs={{0,4},{1,5},{2,6},{3,7},{4,0},{5,1},{6,2},{7,3},{8,12},{9,13},{10,... | collective-permute-start | bytes 196616 | tf_op jit(solution)/shard_map/ppermute | solution.py:223
  72.4 7.1 %collective-permute-start.14 = (bf16[128,256]{1,0:T(8,128)(2,1)S(1)}, bf16[128,256]{1,0:T(8,128)(2,1)S(1)}, u32[]{:S(2)}, u32[]{:S(2)}) collective-permute-start(bf16[128,256]{1,0:T(8,128)(2,1)S(1)} %get-tuple-element.53), channel_id=1, source_target_pairs={{0,2},{1,3},{2,0},{3,1},{4,6},{5,7},{6,4},{7,5},{8,10},{9,11},{10,... | collective-permute-start | bytes 196616 | tf_op jit(solution)/shard_map/ppermute | solution.py:223
  74.5 9.0 %collective-permute-start.24 = (bf16[128,256]{1,0:T(8,128)(2,1)S(1)}, bf16[128,256]{1,0:T(8,128)(2,1)S(1)}, u32[]{:S(2)}, u32[]{:S(2)}) collective-permute-start(bf16[128,256]{1,0:T(8,128)(2,1)S(1)} %get-tuple-element.51), channel_id=1, source_target_pairs={{0,6},{1,7},{2,4},{3,5},{4,2},{5,3},{6,0},{7,1},{8,14},{9,15},{10,... | collective-permute-start | bytes 196616 | tf_op jit(solution)/shard_map/ppermute | solution.py:223
  76.9 8.0 %collective-permute-start.23 = (bf16[128,256]{1,0:T(8,128)(2,1)S(1)}, bf16[128,256]{1,0:T(8,128)(2,1)S(1)}, u32[]{:S(2)}, u32[]{:S(2)}) collective-permute-start(bf16[128,256]{1,0:T(8,128)(2,1)S(1)} %get-tuple-element.52), channel_id=1, source_target_pairs={{0,4},{1,5},{2,6},{3,7},{4,0},{5,1},{6,2},{7,3},{8,12},{9,13},{10,... | collective-permute-start | bytes 196616 | tf_op jit(solution)/shard_map/ppermute | solution.py:223
  76.9 8.0 %collective-permute-start.22 = (bf16[128,256]{1,0:T(8,128)(2,1)S(1)}, bf16[128,256]{1,0:T(8,128)(2,1)S(1)}, u32[]{:S(2)}, u32[]{:S(2)}) collective-permute-start(bf16[128,256]{1,0:T(8,128)(2,1)S(1)} %get-tuple-element.50), channel_id=1, source_target_pairs={{0,2},{1,3},{2,0},{3,1},{4,6},{5,7},{6,4},{7,5},{8,10},{9,11},{10,... | collective-permute-start | bytes 196616 | tf_op jit(solution)/shard_map/ppermute | solution.py:223
  79.6 8.4 %collective-permute-start.17 = (bf16[128,256]{1,0:T(8,128)(2,1)S(1)}, bf16[128,256]{1,0:T(8,128)(2,1)S(1)}, u32[]{:S(2)}, u32[]{:S(2)}) collective-permute-start(bf16[128,256]{1,0:T(8,128)(2,1)S(1)} %get-tuple-element.73), channel_id=1, source_target_pairs={{0,2},{1,3},{2,0},{3,1},{4,6},{5,7},{6,4},{7,5},{8,10},{9,11},{10,... | collective-permute-start | bytes 196616 | tf_op jit(solution)/shard_map/ppermute | solution.py:223
  79.9 9.6 %collective-permute-start.18 = (bf16[128,256]{1,0:T(8,128)(2,1)S(1)}, bf16[128,256]{1,0:T(8,128)(2,1)S(1)}, u32[]{:S(2)}, u32[]{:S(2)}) collective-permute-start(bf16[128,256]{1,0:T(8,128)(2,1)S(1)} %get-tuple-element.73), channel_id=1, source_target_pairs={{0,4},{1,5},{2,6},{3,7},{4,0},{5,1},{6,2},{7,3},{8,12},{9,13},{10,... | collective-permute-start | bytes 196616 | tf_op jit(solution)/shard_map/ppermute | solution.py:223
  85.2 9.1 %collective-permute-start.26 = (bf16[128,256]{1,0:T(8,128)(2,1)S(1)}, bf16[128,256]{1,0:T(8,128)(2,1)S(1)}, u32[]{:S(2)}, u32[]{:S(2)}) collective-permute-start(bf16[128,256]{1,0:T(8,128)(2,1)S(1)} %get-tuple-element.75), channel_id=1, source_target_pairs={{0,4},{1,5},{2,6},{3,7},{4,0},{5,1},{6,2},{7,3},{8,12},{9,13},{10,... | collective-permute-start | bytes 196616 | tf_op jit(solution)/shard_map/ppermute | solution.py:223
  97.1 10.1 %collective-permute-start.30 = (bf16[512,256]{1,0:T(8,128)(2,1)S(1)}, bf16[512,256]{1,0:T(8,128)(2,1)S(1)}, u32[]{:S(2)}, u32[]{:S(2)}) collective-permute-start(bf16[512,256]{1,0:T(8,128)(2,1)S(1)} %down_far_a.1), channel_id=1, source_target_pairs={{0,16},{8,24},{16,0},{24,8},{1,17},{9,25},{17,1},{25,9},{2,18},{10... | collective-permute-start | bytes 786440 | tf_op jit(solution)/shard_map/ppermute | solution.py:223
  98.9 22.1 %collective-permute-start.29 = (bf16[512,256]{1,0:T(8,128)(2,1)S(1)}, bf16[512,256]{1,0:T(8,128)(2,1)S(1)}, u32[]{:S(2)}, u32[]{:S(2)}) collective-permute-start(bf16[512,256]{1,0:T(8,128)(2,1)S(1)} %down_x_a.1), channel_id=1, source_target_pairs={{0,16},{8,24},{16,0},{24,8},{1,17},{9,25},{17,1},{25,9},{2,18},{10... | collective-permute-start | bytes 786440 | tf_op jit(solution)/shard_map/ppermute | solution.py:223
  101.6 19.4 %collective-permute-start.32 = (bf16[512,256]{1,0:T(8,128)(2,1)S(1)}, bf16[512,256]{1,0:T(8,128)(2,1)S(1)}, u32[]{:S(2)}, u32[]{:S(2)}) collective-permute-start(bf16[512,256]{1,0:T(8,128)(2,1)S(1)} %down_y_b.1), channel_id=1, source_target_pairs={{0,1},{1,0},{2,3},{3,2},{4,5},{5,4},{6,7},{7,6},{8,9},{9,8},{10,11... | collective-permute-start | bytes 786440 | tf_op jit(solution)/shard_map/ppermute | solution.py:223
  103.2 13.4 %collective-permute-start.33 = (bf16[512,256]{1,0:T(8,128)(2,1)S(1)}, bf16[512,256]{1,0:T(8,128)(2,1)S(1)}, u32[]{:S(2)}, u32[]{:S(2)}) collective-permute-start(bf16[512,256]{1,0:T(8,128)(2,1)S(1)} %down_far_b.1), channel_id=1, source_target_pairs={{0,1},{1,0},{2,3},{3,2},{4,5},{5,4},{6,7},{7,6},{8,9},{9,8},{10,11... | collective-permute-start | bytes 786440 | tf_op jit(solution)/shard_map/ppermute | solution.py:223
  107.3 13.7 %collective-permute-start.31 = (bf16[512,256]{1,0:T(8,128)(2,1)S(1)}, bf16[512,256]{1,0:T(8,128)(2,1)S(1)}, u32[]{:S(2)}, u32[]{:S(2)}) collective-permute-start(bf16[512,256]{1,0:T(8,128)(2,1)S(1)} %add_convert_fusion.3), channel_id=1, source_target_pairs={{0,1},{1,0},{2,3},{3,2},{4,5},{5,4},{6,7},{7,6},{8,9},{9,8},{10,11... | collective-permute-start | bytes 786440 | tf_op jit(solution)/shard_map/ppermute | solution.py:223
  (27 other events, 190.9 us)

commit v3 on v2

--- a/solution.py
+++ b/solution.py
@@ -12,7 +12,8 @@
 F32 = jnp.float32
 BOTH = ("grp", "dom")
 EPS = 1e-06
-VMEM_LIMIT = 48 * 2**20
+VMEM_LIMIT = 24 * 2**20
+WIDE_LIMIT = 62 * 2**20
 
 
 def dot(a, b, ca=1, cb=0):
@@ -23,9 +24,7 @@
     return pl.BlockSpec(shape, lambda *_: (0,) * len(shape))
 
 
-def call(body, name, out_shape, in_specs, out_specs, args, grid=(1,), scratch=(), flops=0, exps=0, limit=VMEM_LIMIT):
-    outs = out_shape if isinstance(out_shape, (list, tuple)) else [out_shape]
-    moved = sum(a.size * a.dtype.itemsize for a in (*args, *outs))
+def call(body, name, out_shape, in_specs, out_specs, args, grid=(1,), scratch=(), cost=1, limit=VMEM_LIMIT):
     return pl.pallas_call(
         body,
         grid=grid,
@@ -35,7 +34,7 @@
         scratch_shapes=list(scratch),
         name=name,
         compiler_params=pltpu.CompilerParams(vmem_limit_bytes=limit),
-        cost_estimate=pl.CostEstimate(flops=flops, bytes_accessed=moved, transcendentals=exps),
+        cost_estimate=pl.CostEstimate(flops=cost, bytes_accessed=1, transcendentals=0),
     )(*args)
 
 
@@ -128,59 +127,75 @@
         keys_ref[...] = dot(keys, w_query_ref[...], 1, 1).astype(BF16)
 
 
-def smooth_up_body(count, scale, *refs):
-    nodes, keys_ref, tiles, sums_ref = refs[:count], refs[count], refs[count + 1 : -1], refs[-1]
+def smooth_up_body(count, starts, scale, *refs):
+    nodes, (side_ref, other_ref), refs = refs[:count], refs[count : count + 2], refs[count + 2 :]
+    tiles = refs[starts:-1]
+    keys = jnp.where(pl.program_id(0) % 2 == 0, side_ref[...], other_ref[...])
     total = 0.0
+    for start_ref in refs[:starts]:
+        total += start_ref[...].astype(F32)
     for node_ref, tile_ref in zip(nodes, tiles):
-        tile = jnp.exp2(dot(keys_ref[...], node_ref[...], 1, 1) * scale).astype(BF16)
+        tile = jnp.exp2(dot(keys, node_ref[...], 1, 1) * scale).astype(BF16)
         tile_ref[...] = tile
         total += dot(tile, node_ref[...])
-    sums_ref[...] = total.astype(BF16)
-
-
-def smooth_up(blocks, keys, name):
-    marks, c = keys.shape
-    step = min(marks, 512)
+    refs[-1][...] = total.astype(BF16)
+
+
+def smooth_up(blocks, side_keys, other_keys, starts, halves, name):
+    step, c = side_keys.shape[0] // 2, side_keys.shape[1]
     scale = 2.0 * c ** (-0.5) * math.log2(math.e)
     sizes = [b.shape[0] for b in blocks]
-    keys_spec = pl.BlockSpec((step, c), lambda j: (j, 0))
+    marks = 2 * step * len(halves)
+    first = halves[0]
+    keys_spec = pl.BlockSpec((step, c), lambda j: (first + j // 2, 0))
     out = call(
-        functools.partial(smooth_up_body, len(blocks), scale),
+        functools.partial(smooth_up_body, len(blocks), len(starts), scale),
         name,
         [jax.ShapeDtypeStruct((marks, n), BF16) for n in sizes]
         + [jax.ShapeDtypeStruct((marks, c), BF16)],
-        [whole(b.shape) for b in blocks] + [keys_spec],
-        [pl.BlockSpec((step, n), lambda j: (j, 0)) for n in sizes] + [keys_spec],
-        [*blocks, keys],
+        [whole(b.shape) for b in blocks]
+        + [keys_spec] * 2
+        + [pl.BlockSpec((step, c), lambda j: (j, 0))] * len(starts),
+        [pl.BlockSpec((step, n), lambda j: (j, 0)) for n in sizes]
+        + [pl.BlockSpec((step, c), lambda j: (j, 0))],
+        [*blocks, side_keys, other_keys, *starts],
         grid=(marks // step,),
-        flops=4 * marks * sum(sizes) * c,
-        exps=marks * sum(sizes),
+        cost=4 * marks * sum(sizes) * c,
     )
     return out[:-1], out[-1]
 
 
-def smooth_down_body(count, *refs):
-    tiles, sums, out_ref = refs[:count], refs[count:-1], refs[-1]
-    total = 0.0
-    for tile_ref, sum_ref in zip(tiles, sums):
-        total += dot(tile_ref[...], sum_ref[...], 0, 0)
-    out_ref[...] = total.astype(out_ref.dtype)
-
-
-def smooth_down(tiles, sums, out_dtype, name):
-    n = tiles[0].shape[1]
+def smooth_down_body(jobs, halves, *refs):
+    tiles, sums, outs = refs[: -len(jobs) - halves], refs[-len(jobs) - halves : -len(jobs)], refs[-len(jobs) :]
+    for (first, count), out_ref in zip(jobs, outs):
+        total = 0.0
+        for h, sum_ref in enumerate(sums):
+            marks = sum_ref.shape[0]
+            if count == 1:
+                tile = tiles[first][h * marks : (h + 1) * marks, :]
+            else:
+                tile = tiles[first + h][...]
+            total += dot(tile, sum_ref[...], 0, 0)
+        out_ref[...] = total.astype(out_ref.dtype)
+
+
+def smooth_down(jobs, sums, n, name):
     c = sums[0].shape[1]
     step = min(n, 256)
+    tiles, specs, where = [], [], []
+    for held, at, _ in jobs:
+        where.append((len(tiles), len(held)))
+        for tile in held:
+            tiles.append(tile)
+            specs.append(pl.BlockSpec((tile.shape[0], step), lambda j, at=at: (0, at // step + j)))
     return call(
-        functools.partial(smooth_down_body, len(tiles)),
+        functools.partial(smooth_down_body, where, len(sums)),
         name,
-        jax.ShapeDtypeStruct((n, c), out_dtype),
-        [pl.BlockSpec((t.shape[0], step), lambda j: (0, j)) for t in tiles]
-        + [whole(v.shape) for v in sums],
-        pl.BlockSpec((step, c), lambda j: (j, 0)),
+        [jax.ShapeDtypeStruct((n, c), dtype) for _, _, dtype in jobs],
+        specs + [whole(v.shape) for v in sums],
+        [pl.BlockSpec((step, c), lambda j: (j, 0))] * len(jobs),
         [*tiles, *sums],
         grid=(n // step,),
-        flops=sum(2 * t.shape[0] * n * c for t in tiles),
     )
 
 
@@ -233,7 +248,7 @@
         [whole((1, 2 * halo)), whole((rows, c))],
         [whole((halo, c))] * 2,
         [send_rows.reshape(1, 2 * halo), nodes],
-        flops=4 * halo * rows * c,
+        limit=WIDE_LIMIT,
     )
     from_prev = lax.ppermute(to_next, BOTH, [(i, (i + 1) % parts) for i in range(parts)])
     from_next = lax.ppermute(to_prev, BOTH, [((i + 1) % parts, i) for i in range(parts)])
@@ -253,7 +268,7 @@
         [links, nodes, nodes, w_src, w_dst, edge_bias.reshape(1, c)],
         grid=(steps,),
         scratch=[pltpu.VMEM((rows, c), BF16)],
-        flops=2 * slots * rows * rows * c,
+        limit=WIDE_LIMIT,
     )
     updated, normed, keys = call(
         edge_body,
@@ -290,27 +305,39 @@
         ],
         grid=(steps,),
         scratch=[pltpu.VMEM((2 * halo, c), BF16), pltpu.VMEM((rows, c), BF16)],
-        flops=4 * slots * rows * halo * c,
-        exps=slots * rows * c,
-    )
-
-    x_a, y_b = over_x(normed[:half]), over_y(normed[half:])
-    key_blocks = [keys] + [over_z[t](keys) for t in range(1, line)]
-    x_b, y_a = over_x(normed[half:]), over_y(normed[:half])
-    xy_a, xy_b = over_y(x_a), over_x(y_b)
+        limit=WIDE_LIMIT,
+    )
+
     part = mine // 2
     side = line * part
-    near = (normed, x_a, x_b, y_a, y_b)
-    tiles = [[] for _ in range(7)]
-    sums = []
+    key_blocks = [keys] + [over_z[t](keys) for t in range(1, line)]
+    from_x, from_y = over_x(normed), over_y(normed)
+    *key_blocks, from_x, from_y = lax.optimization_barrier((*key_blocks, from_x, from_y))
+    xy_a, xy_b = over_y(from_x[:half]), over_x(from_y[half:])
+    side_keys = jnp.concatenate(
+        [k[h * part : (h + 1) * part] for h in range(2) for k in key_blocks], axis=0
+    )
+    other_keys = over_core(side_keys)
+    own_tiles, own_sums = smooth_up([normed], side_keys, other_keys, (), (0, 1), "up_own")
+    x_tiles, y_tiles, far_a_tiles, far_b_tiles, sums = [], [], [], [], []
+    both = own_sums
     for h in range(2):
-        side_keys = jnp.concatenate([k[h * part : (h + 1) * part] for k in key_blocks], axis=0)
-        marks = jnp.concatenate([side_keys, over_core(side_keys)], axis=0)
-        near_tiles, near_sums = smooth_up(near, marks, f"up_near_{h}")
-        far_tiles, far_sums = smooth_up((xy_a, xy_b), marks, f"up_far_{h}")
-        for held, tile in zip(tiles, [*near_tiles, *far_tiles]):
+        from_x, from_y, _ = lax.optimization_barrier((from_x, from_y, both))
+        (x_half, y_half), near_sums = smooth_up(
+            [from_x, from_y], side_keys, other_keys, (), (h,), f"up_near_{h}"
+        )
+        (a_half, b_half), both = smooth_up(
+            [xy_a, xy_b],
+            side_keys,
+            other_keys,
+            (own_sums[h * 2 * side : (h + 1) * 2 * side], near_sums),
+            (h,),
+            f"up_far_{h}",
+        )
+        for held, tile in zip(
+            (x_tiles, y_tiles, far_a_tiles, far_b_tiles), (x_half, y_half, a_half, b_half)
+        ):
             held.append(tile)
-        both = (near_sums.astype(F32) + far_sums.astype(F32)).astype(BF16)
         core_sums = (both[:side].astype(F32) + over_core(both[side:]).astype(F32)).astype(BF16)
         blocks = [core_sums[t * part : (t + 1) * part] for t in range(line)]
         total = blocks[0].astype(F32)
@@ -320,19 +347,27 @@
         side_sums = jnp.concatenate([total] + [over_z[t](total) for t in range(1, line)], axis=0)
         sums.append(jnp.concatenate([side_sums, over_core(side_sums)], axis=0))
 
-    def down(block, dtype, name):
-        return smooth_down(tiles[block], sums, dtype, name)
-
-    own_tiles, x_a_tiles, x_b_tiles, y_a_tiles, y_b_tiles, xy_a_tiles, xy_b_tiles = range(7)
-    far_a = over_x(down(xy_a_tiles, BF16, "down_far_a"))
-    far_b = over_y(down(xy_b_tiles, BF16, "down_far_b"))
-    first_a = over_x(down(x_a_tiles, BF16, "down_x_a"))
-    first_b = over_y(down(y_b_tiles, BF16, "down_y_b"))
-    pass_a = down(y_a_tiles, F32, "down_y_a")
-    pass_b = down(x_b_tiles, F32, "down_x_b")
+    far_a, far_b = smooth_down(
+        [(far_a_tiles, 0, BF16), (far_b_tiles, 0, BF16)], sums, half, "down_far"
+    )
+    sums_0, sums_1, far_a, far_b = lax.optimization_barrier((*sums, far_a, far_b))
+    sums = [sums_0, sums_1]
+    first_a, first_b, pass_a, pass_b = smooth_down(
+        [
+            (x_tiles, 0, BF16),
+            (y_tiles, half, BF16),
+            (y_tiles, 0, F32),
+            (x_tiles, half, F32),
+        ],
+        sums,
+        half,
+        "down_near",
+    )
+    far_a, far_b = over_x(far_a), over_y(far_b)
+    first_a, first_b = over_x(first_a), over_y(first_b)
     second_a = over_y((pass_a + far_a.astype(F32)).astype(BF16))
     second_b = over_x((pass_b + far_b.astype(F32)).astype(BF16))
-    own = down(own_tiles, F32, "down_own")
+    (own,) = smooth_down([(own_tiles, 0, F32)], sums, rows, "down_own")
 
     return call(
         last_body,
@@ -341,7 +376,6 @@
         [whole((rows, c))] + [whole((half, c))] * 4 + [whole((rows, c)), whole((c, c))],
         [whole((rows, c))] * 2,
         [own, first_a, second_a, first_b, second_b, updated, w_out],
-        flops=2 * rows * c * c,
     )
 
 

time: 125 us -> 114 us (0.912)
  local copies, waits for them, and re-layouts: 6.37 us -> 2.63 us
  waiting for transfers between devices: 30.8 us -> 27.1 us
  starting transfers between devices: 41.4 us -> 38.5 us
    ppermute x33 -> x30, waiting for transfers between devices: 30.8 us -> 27.1 us  [pair(): return lambda v: lax.ppermute(v, axis, [(i, i ^ flip) for i in range(size)])]
    unnamed x38 -> x25, local copies, waits for them, and re-layouts: 6.12 us -> 2.41 us
    ppermute x33 -> x30, starting transfers between devices: 34.9 us -> 32.1 us  [pair(): return lambda v: lax.ppermute(v, axis, [(i, i ^ flip) for i in range(size)])]
    pallas_call x15 -> x12, Pallas kernels: 43.9 us -> 43.9 us  [call(): pl.pallas_call(body, grid=grid, in_specs=in_specs, out_specs=out_specs, o...]
  transfers between devices with their start and end apart: 35 -> 32, of which waited for: 11 -> 11; matrix products, arithmetic and copies ran while one was open for 1% -> 1% of each run, Pallas kernels for 25% -> 24%
where the time goes in v3:
time: 114 us
  Pallas kernels  43.9 us (39%)
  starting transfers between devices  38.5 us (34%)
  waiting for transfers between devices  27.1 us (24%)
  local copies, waits for them, and re-layouts  2.63 us (2%)
    pallas_call x12, Pallas kernels, call(): pl.pallas_call(body, grid=grid, in_specs=in_specs, out_specs=out_specs, o...  43.9 us
    ppermute x30, starting transfers between devices, pair(): return lambda v: lax.ppermute(v, axis, [(i, i ^ flip) for i in range(size)])  32.1 us
    ppermute x30, waiting for transfers between devices, pair(): return lambda v: lax.ppermute(v, axis, [(i, i ^ flip) for i in range(size)])  27.1 us
    ppermute x1, starting transfers between devices, shards(): lax.ppermute(to_prev, BOTH, [((i + 1) % parts, i) for i in range(parts)])  3.4 us
    ppermute x1, starting transfers between devices, shards(): lax.ppermute(to_next, BOTH, [(i, (i + 1) % parts) for i in range(parts)])  2.97 us
    unnamed x25, local copies, waits for them, and re-layouts  2.41 us
  transfers between devices with their start and end apart: 32, of which 11 were waited for; matrix products, arithmetic and copies ran while one was open for 1% of the time, Pallas kernels for 24%

profile of v3, /device:TPU:0, one launch (start us, length us, event | category | flops | bytes accessed | tf_op | source)
XLA Modules:
  0.0 113.7 jit_solution(4468491285886762789)
XLA Ops:
  0.6 2.1 %send_rows.1 = (bf16[128,256]{1,0:T(8,128)(2,1)}, bf16[128,256]{1,0:T(8,128)(2,1)}) custom-call(s32[1,256]{1,0:T(1,128)} %bitcast.8, bf16[1024,256]{1,0:T(8,128)(2,1)} %tile_ref.3), custom_call_target="tpu_custom_call" | custom-call | flops 1 | bytes 1 | tf_op jit(solution)/shard_map/send_rows/pallas_call | solution.py:28
  2.7 3.0 %collective-permute-start = (bf16[128,256]{1,0:T(8,128)(2,1)}, bf16[128,256]{1,0:T(8,128)(2,1)S(1)}, u32[]{:S(2)}, u32[]{:S(2)}) collective-permute-start(bf16[128,256]{1,0:T(8,128)(2,1)} %get-tuple-element.41), channel_id=1, source_target_pairs={{0,1},{1,2},{2,3},{3,4},{4,5},{5,6},{6,7},{7,8},{8,9},{9,10},{10,1... | collective-permute-start | bytes 196616 | tf_op jit(solution)/shard_map/ppermute | solution.py:253
  5.7 3.4 %collective-permute-start.1 = (bf16[128,256]{1,0:T(8,128)(2,1)}, bf16[128,256]{1,0:T(8,128)(2,1)S(1)}, u32[]{:S(2)}, u32[]{:S(2)}) collective-permute-start(bf16[128,256]{1,0:T(8,128)(2,1)} %get-tuple-element.42), channel_id=1, source_target_pairs={{1,0},{2,1},{3,2},{4,3},{5,4},{6,5},{7,6},{8,7},{9,8},{10,9},{11,1... | collective-permute-start | bytes 196616 | tf_op jit(solution)/shard_map/ppermute | solution.py:254
  9.1 8.2 %own_edges.1.pre_ref = f32[8,1024,256]{2,1,0:T(8,128)} custom-call(s32[8,1024]{1,0:T(8,128)} %bitcast.6, bf16[1024,256]{1,0:T(8,128)(2,1)} %tile_ref.3, bf16[1024,256]{1,0:T(8,128)(2,1)} %tile_ref.3, bf16[256,256]{1,0:T(8,128)(2,1)} %w_src_ref.3, bf16[256,256]{1,0:T(8,128)(2,1)} %w_dst_ref.1, f32[1,256]{1,0:T(1,128)} %bitcast.9), custom_call_target="tpu_custom_call" | custom-call | flops 1 | bytes 1 | tf_op jit(solution)/shard_map/own_edges/pallas_call | solution.py:28
  18.0 9.0 %edges.1 = (bf16[1024,256]{1,0:T(8,128)(2,1)}, bf16[1024,256]{1,0:T(8,128)(2,1)}, bf16[256,256]{1,0:T(8,128)(2,1)}) custom-call(s32[8,1024]{1,0:T(8,128)} %bitcast.7, f32[8,1024,256]{2,1,0:T(8,128)} %own_edges.1.pre_ref, bf16[128,256]{1,0:T(8,128)(2,1)} %copy-done.4, bf16[128,256]{1,0:T(8,128)(2,1)} %copy-done.5, bf16[1024,256]{1,0:T(8,128)(2,1)} %tile_ref.3, ...), custom_call_target="tpu_custom_call" | custom-call | flops 1 | bytes 1 | tf_op jit(solution)/shard_map/edges/pallas_call | solution.py:28
  27.1 2.0 %collective-permute-start.5 = (bf16[1024,256]{1,0:T(8,128)(2,1)}, bf16[1024,256]{1,0:T(8,128)(2,1)S(1)}, u32[]{:S(2)}, u32[]{:S(2)}) collective-permute-start(bf16[1024,256]{1,0:T(8,128)(2,1)} %get-tuple-element.43.refs_0_), channel_id=1, source_target_pairs={{0,16},{8,24},{16,0},{24,8},{1,17},{9,25},{17,1},{25,9},{2,18},{10... | collective-permute-start | bytes 1572872 | tf_op jit(solution)/shard_map/ppermute | solution.py:238
  30.8 2.6 %collective-permute-start.2 = (bf16[256,256]{1,0:T(8,128)(2,1)}, bf16[256,256]{1,0:T(8,128)(2,1)S(1)}, u32[]{:S(2)}, u32[]{:S(2)}) collective-permute-start(bf16[256,256]{1,0:T(8,128)(2,1)} %get-tuple-element.45), channel_id=1, source_target_pairs={{0,2},{1,3},{2,0},{3,1},{4,6},{5,7},{6,4},{7,5},{8,10},{9,11},{10,... | collective-permute-start | bytes 393224 | tf_op jit(solution)/shard_map/ppermute | solution.py:238
  33.4 4.1 %collective-permute-done.4 = bf16[256,256]{1,0:T(8,128)(2,1)S(1)} collective-permute-done((bf16[256,256]{1,0:T(8,128)(2,1)}, bf16[256,256]{1,0:T(8,128)(2,1)S(1)}, u32[]{:S(2)}, u32[]{:S(2)}) %collective-permute-start.4) | collective-permute-done | bytes 131104 | tf_op jit(solution)/shard_map/ppermute | solution.py:238
  37.5 4.3 %collective-permute-done.3 = bf16[256,256]{1,0:T(8,128)(2,1)S(1)} collective-permute-done((bf16[256,256]{1,0:T(8,128)(2,1)}, bf16[256,256]{1,0:T(8,128)(2,1)S(1)}, u32[]{:S(2)}, u32[]{:S(2)}) %collective-permute-start.3) | collective-permute-done | bytes 131104 | tf_op jit(solution)/shard_map/ppermute | solution.py:238
  46.1 3.4 %up_own.1 = (bf16[2048,1024]{1,0:T(8,128)(2,1)S(1)}, bf16[2048,256]{1,0:T(8,128)(2,1)S(1)}) custom-call(bf16[1024,256]{1,0:T(8,128)(2,1)S(1)} %copy-done.3, bf16[1024,256]{1,0:T(8,128)(2,1)S(1)} %slice_dynamic-update-slice_fusion.refs_1_.refs_2_, bf16[1024,256]{1,0:T(8,128)(2,1)S(1)} %collective-permute-done.7.refs_2_.refs_3_), custom_call_target="tpu_custom_call" | custom-call | flops 2147483648 | bytes 1 | tf_op jit(solution)/shard_map/up_own/pallas_call | solution.py:28
  49.5 3.9 %up_near_0.1 = (bf16[1024,1024]{1,0:T(8,128)(2,1)S(1)}, bf16[1024,1024]{1,0:T(8,128)(2,1)S(1)}, bf16[1024,256]{1,0:T(8,128)(2,1)S(1)}) custom-call(bf16[1024,256]{1,0:T(8,128)(2,1)S(1)} %collective-permute-done.5.refs_0_, bf16[1024,256]{1,0:T(8,128)(2,1)S(1)} %collective-permute-done.6.refs_1_, ...), custom_call_target="tpu_custom_call" | custom-call | flops 2147483648 | bytes 1 | tf_op jit(solution)/shard_map/up_near_0/pallas_call | solution.py:28
  53.5 1.7 %up_far_0.1 = (bf16[1024,512]{1,0:T(8,128)(2,1)S(1)}, bf16[1024,512]{1,0:T(8,128)(2,1)S(1)}, bf16[1024,256]{1,0:T(8,128)(2,1)S(1)}) custom-call(bf16[512,256]{1,0:T(8,128)(2,1)S(1)} %collective-permute-done.8.refs_0_, bf16[512,256]{1,0:T(8,128)(2,1)S(1)} %collective-permute-done.9.refs_1_, ...), custom_call_target="tpu_custom_call" | custom-call | flops 1073741824 | bytes 1 | tf_op jit(solution)/shard_map/up_far_0/pallas_call | solution.py:28
  55.4 3.9 %up_near_1.1 = (bf16[1024,1024]{1,0:T(8,128)(2,1)S(1)}, bf16[1024,1024]{1,0:T(8,128)(2,1)S(1)}, bf16[1024,256]{1,0:T(8,128)(2,1)S(1)}) custom-call(bf16[1024,256]{1,0:T(8,128)(2,1)S(1)} %collective-permute-done.5.refs_0_, bf16[1024,256]{1,0:T(8,128)(2,1)S(1)} %collective-permute-done.6.refs_1_, ...), custom_call_target="tpu_custom_call" | custom-call | flops 2147483648 | bytes 1 | tf_op jit(solution)/shard_map/up_near_1/pallas_call | solution.py:28
  59.3 1.7 %up_far_1.1 = (bf16[1024,512]{1,0:T(8,128)(2,1)S(1)}, bf16[1024,512]{1,0:T(8,128)(2,1)S(1)}, bf16[1024,256]{1,0:T(8,128)(2,1)S(1)}) custom-call(bf16[512,256]{1,0:T(8,128)(2,1)S(1)} %collective-permute-done.8.refs_0_, bf16[512,256]{1,0:T(8,128)(2,1)S(1)} %collective-permute-done.9.refs_1_, ...), custom_call_target="tpu_custom_call" | custom-call | flops 1073741824 | bytes 1 | tf_op jit(solution)/shard_map/up_far_1/pallas_call | solution.py:28
  61.8 1.9 %collective-permute-start.13 = (bf16[128,256]{1,0:T(8,128)(2,1)S(1)}, bf16[128,256]{1,0:T(8,128)(2,1)S(1)}, u32[]{:S(2)}, u32[]{:S(2)}) collective-permute-start(bf16[128,256]{1,0:T(8,128)(2,1)S(1)} %get-tuple-element.86), channel_id=1, source_target_pairs={{0,6},{1,7},{2,4},{3,5},{4,2},{5,3},{6,0},{7,1},{8,14},{9,15},{10,... | collective-permute-start | bytes 196616 | tf_op jit(solution)/shard_map/ppermute | solution.py:238
  66.4 1.8 %collective-permute-start.21 = (bf16[128,256]{1,0:T(8,128)(2,1)S(1)}, bf16[128,256]{1,0:T(8,128)(2,1)S(1)}, u32[]{:S(2)}, u32[]{:S(2)}) collective-permute-start(bf16[128,256]{1,0:T(8,128)(2,1)S(1)} %get-tuple-element.83), channel_id=1, source_target_pairs={{0,6},{1,7},{2,4},{3,5},{4,2},{5,3},{6,0},{7,1},{8,14},{9,15},{10,... | collective-permute-start | bytes 196616 | tf_op jit(solution)/shard_map/ppermute | solution.py:238
  68.9 5.8 %collective-permute-done.12 = bf16[128,256]{1,0:T(8,128)(2,1)S(1)} collective-permute-done((bf16[128,256]{1,0:T(8,128)(2,1)S(1)}, bf16[128,256]{1,0:T(8,128)(2,1)S(1)}, u32[]{:S(2)}, u32[]{:S(2)}) %collective-permute-start.12) | collective-permute-done | bytes 65568 | tf_op jit(solution)/shard_map/ppermute | solution.py:238
  76.6 2.7 %collective-permute-start.14 = (bf16[128,256]{1,0:T(8,128)(2,1)S(1)}, bf16[128,256]{1,0:T(8,128)(2,1)S(1)}, u32[]{:S(2)}, u32[]{:S(2)}) collective-permute-start(bf16[128,256]{1,0:T(8,128)(2,1)S(1)} %get-tuple-element.89), channel_id=1, source_target_pairs={{0,2},{1,3},{2,0},{3,1},{4,6},{5,7},{6,4},{7,5},{8,10},{9,11},{10,... | collective-permute-start | bytes 196616 | tf_op jit(solution)/shard_map/ppermute | solution.py:238
  81.2 2.7 %collective-permute-start.22 = (bf16[128,256]{1,0:T(8,128)(2,1)S(1)}, bf16[128,256]{1,0:T(8,128)(2,1)S(1)}, u32[]{:S(2)}, u32[]{:S(2)}) collective-permute-start(bf16[128,256]{1,0:T(8,128)(2,1)S(1)} %get-tuple-element.91), channel_id=1, source_target_pairs={{0,2},{1,3},{2,0},{3,1},{4,6},{5,7},{6,4},{7,5},{8,10},{9,11},{10,... | collective-permute-start | bytes 196616 | tf_op jit(solution)/shard_map/ppermute | solution.py:238
  85.7 2.3 %collective-permute-done.23 = bf16[128,256]{1,0:T(8,128)(2,1)S(1)} collective-permute-done((bf16[128,256]{1,0:T(8,128)(2,1)S(1)}, bf16[128,256]{1,0:T(8,128)(2,1)S(1)}, u32[]{:S(2)}, u32[]{:S(2)}) %collective-permute-start.23) | collective-permute-done | bytes 65568 | tf_op jit(solution)/shard_map/ppermute | solution.py:238
  89.7 2.0 %down_far.1 = (bf16[512,256]{1,0:T(8,128)(2,1)S(1)}, bf16[512,256]{1,0:T(8,128)(2,1)S(1)}) custom-call(bf16[1024,512]{1,0:T(8,128)(2,1)S(1)} %get-tuple-element.61.refs_0_, bf16[1024,512]{1,0:T(8,128)(2,1)S(1)} %get-tuple-element.62.refs_1_, bf16[1024,512]{1,0:T(8,128)(2,1)S(1)} %get-tuple-element.63.refs_2_, ...), custom_call_target="tpu_custom_call" | custom-call | flops 1 | bytes 1 | tf_op jit(solution)/shard_map/down_far/pallas_call | solution.py:28
  93.9 3.8 %down_near.1 = (bf16[512,256]{1,0:T(8,128)(2,1)S(1)}, bf16[512,256]{1,0:T(8,128)(2,1)S(1)}, f32[512,256]{1,0:T(8,128)S(1)}, f32[512,256]{1,0:T(8,128)S(1)}) custom-call(bf16[1024,1024]{1,0:T(8,128)(2,1)S(1)} %get-tuple-element.69.refs_0_.refs_6_, bf16[1024,1024]{1,0:T(8,128)(2,1)S(1)} %get-tuple-element.70.refs_1_.refs_7_, ...), custom_call_target="tpu_custom_call" | custom-call | flops 1 | bytes 1 | tf_op jit(solution)/shard_map/down_near/pallas_call | solution.py:28
  102.8 2.6 %down_own.1.own_ref = f32[1024,256]{1,0:T(8,128)S(1)} custom-call(bf16[2048,1024]{1,0:T(8,128)(2,1)S(1)} %get-tuple-element.49.refs_0_, bf16[1024,256]{1,0:T(8,128)(2,1)S(1)} %constant_dynamic-update-slice_fusion.refs_4_.refs_1_.refs_8_, bf16[1024,256]{1,0:T(8,128)(2,1)S(1)} %constant_dynamic-update-slice_fusion.5.refs_5_.refs_2_.refs_9_), custom_call_target="tpu_custom_call" | custom-call | flops 1 | bytes 1 | tf_op jit(solution)/shard_map/down_own/pallas_call | solution.py:28
  107.9 4.3 %collective-permute-done.28.ya_ref = bf16[512,256]{1,0:T(8,128)(2,1)S(1)} collective-permute-done((bf16[512,256]{1,0:T(8,128)(2,1)S(1)}, bf16[512,256]{1,0:T(8,128)(2,1)S(1)}, u32[]{:S(2)}, u32[]{:S(2)}) %collective-permute-start.28) | collective-permute-done | bytes 262176 | tf_op jit(solution)/shard_map/ppermute | solution.py:238
  (95 shorter events, 29.5 us)
Async XLA Ops:
  2.7 14.6 %collective-permute-start = (bf16[128,256]{1,0:T(8,128)(2,1)}, bf16[128,256]{1,0:T(8,128)(2,1)S(1)}, u32[]{:S(2)}, u32[]{:S(2)}) collective-permute-start(bf16[128,256]{1,0:T(8,128)(2,1)} %get-tuple-element.41), channel_id=1, source_target_pairs={{0,1},{1,2},{2,3},{3,4},{4,5},{5,6},{6,7},{7,8},{8,9},{9,10},{10,1... | collective-permute-start | bytes 196616 | tf_op jit(solution)/shard_map/ppermute | solution.py:253
  5.7 11.6 %collective-permute-start.1 = (bf16[128,256]{1,0:T(8,128)(2,1)}, bf16[128,256]{1,0:T(8,128)(2,1)S(1)}, u32[]{:S(2)}, u32[]{:S(2)}) collective-permute-start(bf16[128,256]{1,0:T(8,128)(2,1)} %get-tuple-element.42), channel_id=1, source_target_pairs={{1,0},{2,1},{3,2},{4,3},{5,4},{6,5},{7,6},{8,7},{9,8},{10,9},{11,1... | collective-permute-start | bytes 196616 | tf_op jit(solution)/shard_map/ppermute | solution.py:254
  27.0 14.8 %collective-permute-start.6 = (bf16[1024,256]{1,0:T(8,128)(2,1)}, bf16[1024,256]{1,0:T(8,128)(2,1)S(1)}, u32[]{:S(2)}, u32[]{:S(2)}) collective-permute-start(bf16[1024,256]{1,0:T(8,128)(2,1)} %get-tuple-element.43.refs_0_), channel_id=1, source_target_pairs={{0,1},{1,0},{2,3},{3,2},{4,5},{5,4},{6,7},{7,6},{8,9},{9,8},{10,11... | collective-permute-start | bytes 1572872 | tf_op jit(solution)/shard_map/ppermute | solution.py:238
  27.1 14.7 %collective-permute-start.5 = (bf16[1024,256]{1,0:T(8,128)(2,1)}, bf16[1024,256]{1,0:T(8,128)(2,1)S(1)}, u32[]{:S(2)}, u32[]{:S(2)}) collective-permute-start(bf16[1024,256]{1,0:T(8,128)(2,1)} %get-tuple-element.43.refs_0_), channel_id=1, source_target_pairs={{0,16},{8,24},{16,0},{24,8},{1,17},{9,25},{17,1},{25,9},{2,18},{10... | collective-permute-start | bytes 1572872 | tf_op jit(solution)/shard_map/ppermute | solution.py:238
  29.0 8.4 %collective-permute-start.4 = (bf16[256,256]{1,0:T(8,128)(2,1)}, bf16[256,256]{1,0:T(8,128)(2,1)S(1)}, u32[]{:S(2)}, u32[]{:S(2)}) collective-permute-start(bf16[256,256]{1,0:T(8,128)(2,1)} %get-tuple-element.45), channel_id=1, source_target_pairs={{0,6},{1,7},{2,4},{3,5},{4,2},{5,3},{6,0},{7,1},{8,14},{9,15},{10,... | collective-permute-start | bytes 393224 | tf_op jit(solution)/shard_map/ppermute | solution.py:238
  30.8 11.0 %collective-permute-start.3 = (bf16[256,256]{1,0:T(8,128)(2,1)}, bf16[256,256]{1,0:T(8,128)(2,1)S(1)}, u32[]{:S(2)}, u32[]{:S(2)}) collective-permute-start(bf16[256,256]{1,0:T(8,128)(2,1)} %get-tuple-element.45), channel_id=1, source_target_pairs={{0,4},{1,5},{2,6},{3,7},{4,0},{5,1},{6,2},{7,3},{8,12},{9,13},{10,... | collective-permute-start | bytes 393224 | tf_op jit(solution)/shard_map/ppermute | solution.py:238
  30.8 11.0 %collective-permute-start.2 = (bf16[256,256]{1,0:T(8,128)(2,1)}, bf16[256,256]{1,0:T(8,128)(2,1)S(1)}, u32[]{:S(2)}, u32[]{:S(2)}) collective-permute-start(bf16[256,256]{1,0:T(8,128)(2,1)} %get-tuple-element.45), channel_id=1, source_target_pairs={{0,2},{1,3},{2,0},{3,1},{4,6},{5,7},{6,4},{7,5},{8,10},{9,11},{10,... | collective-permute-start | bytes 393224 | tf_op jit(solution)/shard_map/ppermute | solution.py:238
  43.7 9.8 %collective-permute-start.9 = (bf16[512,256]{1,0:T(8,128)(2,1)S(1)}, bf16[512,256]{1,0:T(8,128)(2,1)S(1)}, u32[]{:S(2)}, u32[]{:S(2)}) collective-permute-start(bf16[512,256]{1,0:T(8,128)(2,1)S(1)} %slice.81), channel_id=1, source_target_pairs={{0,16},{8,24},{16,0},{24,8},{1,17},{9,25},{17,1},{25,9},{2,18},{10... | collective-permute-start | bytes 786440 | tf_op jit(solution)/shard_map/ppermute | solution.py:238
  44.4 9.1 %collective-permute-start.8 = (bf16[512,256]{1,0:T(8,128)(2,1)S(1)}, bf16[512,256]{1,0:T(8,128)(2,1)S(1)}, u32[]{:S(2)}, u32[]{:S(2)}) collective-permute-start(bf16[512,256]{1,0:T(8,128)(2,1)S(1)} %slice.80), channel_id=1, source_target_pairs={{0,1},{1,0},{2,3},{3,2},{4,5},{5,4},{6,7},{7,6},{8,9},{9,8},{10,11... | collective-permute-start | bytes 786440 | tf_op jit(solution)/shard_map/ppermute | solution.py:238
  61.8 7.1 %collective-permute-start.13 = (bf16[128,256]{1,0:T(8,128)(2,1)S(1)}, bf16[128,256]{1,0:T(8,128)(2,1)S(1)}, u32[]{:S(2)}, u32[]{:S(2)}) collective-permute-start(bf16[128,256]{1,0:T(8,128)(2,1)S(1)} %get-tuple-element.86), channel_id=1, source_target_pairs={{0,6},{1,7},{2,4},{3,5},{4,2},{5,3},{6,0},{7,1},{8,14},{9,15},{10,... | collective-permute-start | bytes 196616 | tf_op jit(solution)/shard_map/ppermute | solution.py:238
  63.6 11.1 %collective-permute-start.12 = (bf16[128,256]{1,0:T(8,128)(2,1)S(1)}, bf16[128,256]{1,0:T(8,128)(2,1)S(1)}, u32[]{:S(2)}, u32[]{:S(2)}) collective-permute-start(bf16[128,256]{1,0:T(8,128)(2,1)S(1)} %get-tuple-element.87), channel_id=1, source_target_pairs={{0,4},{1,5},{2,6},{3,7},{4,0},{5,1},{6,2},{7,3},{8,12},{9,13},{10,... | collective-permute-start | bytes 196616 | tf_op jit(solution)/shard_map/ppermute | solution.py:238
  65.3 11.2 %collective-permute-start.19 = (bf16[128,256]{1,0:T(8,128)(2,1)S(1)}, bf16[128,256]{1,0:T(8,128)(2,1)S(1)}, u32[]{:S(2)}, u32[]{:S(2)}) collective-permute-start(bf16[128,256]{1,0:T(8,128)(2,1)S(1)} %get-tuple-element.82), channel_id=1, source_target_pairs={{0,2},{1,3},{2,0},{3,1},{4,6},{5,7},{6,4},{7,5},{8,10},{9,11},{10,... | collective-permute-start | bytes 196616 | tf_op jit(solution)/shard_map/ppermute | solution.py:238
  66.4 12.9 %collective-permute-start.21 = (bf16[128,256]{1,0:T(8,128)(2,1)S(1)}, bf16[128,256]{1,0:T(8,128)(2,1)S(1)}, u32[]{:S(2)}, u32[]{:S(2)}) collective-permute-start(bf16[128,256]{1,0:T(8,128)(2,1)S(1)} %get-tuple-element.83), channel_id=1, source_target_pairs={{0,6},{1,7},{2,4},{3,5},{4,2},{5,3},{6,0},{7,1},{8,14},{9,15},{10,... | collective-permute-start | bytes 196616 | tf_op jit(solution)/shard_map/ppermute | solution.py:238
  68.2 11.1 %collective-permute-start.20 = (bf16[128,256]{1,0:T(8,128)(2,1)S(1)}, bf16[128,256]{1,0:T(8,128)(2,1)S(1)}, u32[]{:S(2)}, u32[]{:S(2)}) collective-permute-start(bf16[128,256]{1,0:T(8,128)(2,1)S(1)} %get-tuple-element.84), channel_id=1, source_target_pairs={{0,4},{1,5},{2,6},{3,7},{4,0},{5,1},{6,2},{7,3},{8,12},{9,13},{10,... | collective-permute-start | bytes 196616 | tf_op jit(solution)/shard_map/ppermute | solution.py:238
  76.6 8.1 %collective-permute-start.15 = (bf16[128,256]{1,0:T(8,128)(2,1)S(1)}, bf16[128,256]{1,0:T(8,128)(2,1)S(1)}, u32[]{:S(2)}, u32[]{:S(2)}) collective-permute-start(bf16[128,256]{1,0:T(8,128)(2,1)S(1)} %get-tuple-element.89), channel_id=1, source_target_pairs={{0,4},{1,5},{2,6},{3,7},{4,0},{5,1},{6,2},{7,3},{8,12},{9,13},{10,... | collective-permute-start | bytes 196616 | tf_op jit(solution)/shard_map/ppermute | solution.py:238
  76.6 8.1 %collective-permute-start.14 = (bf16[128,256]{1,0:T(8,128)(2,1)S(1)}, bf16[128,256]{1,0:T(8,128)(2,1)S(1)}, u32[]{:S(2)}, u32[]{:S(2)}) collective-permute-start(bf16[128,256]{1,0:T(8,128)(2,1)S(1)} %get-tuple-element.89), channel_id=1, source_target_pairs={{0,2},{1,3},{2,0},{3,1},{4,6},{5,7},{6,4},{7,5},{8,10},{9,11},{10,... | collective-permute-start | bytes 196616 | tf_op jit(solution)/shard_map/ppermute | solution.py:238
  81.2 6.8 %collective-permute-start.23 = (bf16[128,256]{1,0:T(8,128)(2,1)S(1)}, bf16[128,256]{1,0:T(8,128)(2,1)S(1)}, u32[]{:S(2)}, u32[]{:S(2)}) collective-permute-start(bf16[128,256]{1,0:T(8,128)(2,1)S(1)} %get-tuple-element.91), channel_id=1, source_target_pairs={{0,4},{1,5},{2,6},{3,7},{4,0},{5,1},{6,2},{7,3},{8,12},{9,13},{10,... | collective-permute-start | bytes 196616 | tf_op jit(solution)/shard_map/ppermute | solution.py:238
  81.2 6.8 %collective-permute-start.22 = (bf16[128,256]{1,0:T(8,128)(2,1)S(1)}, bf16[128,256]{1,0:T(8,128)(2,1)S(1)}, u32[]{:S(2)}, u32[]{:S(2)}) collective-permute-start(bf16[128,256]{1,0:T(8,128)(2,1)S(1)} %get-tuple-element.91), channel_id=1, source_target_pairs={{0,2},{1,3},{2,0},{3,1},{4,6},{5,7},{6,4},{7,5},{8,10},{9,11},{10,... | collective-permute-start | bytes 196616 | tf_op jit(solution)/shard_map/ppermute | solution.py:238
  91.7 8.6 %collective-permute-start.27 = (bf16[512,256]{1,0:T(8,128)(2,1)S(1)}, bf16[512,256]{1,0:T(8,128)(2,1)S(1)}, u32[]{:S(2)}, u32[]{:S(2)}) collective-permute-start(bf16[512,256]{1,0:T(8,128)(2,1)S(1)} %get-tuple-element.75), channel_id=1, source_target_pairs={{0,16},{8,24},{16,0},{24,8},{1,17},{9,25},{17,1},{25,9},{2,18},{10... | collective-permute-start | bytes 786440 | tf_op jit(solution)/shard_map/ppermute | solution.py:238
  93.0 8.5 %collective-permute-start.30 = (bf16[512,256]{1,0:T(8,128)(2,1)S(1)}, bf16[512,256]{1,0:T(8,128)(2,1)S(1)}, u32[]{:S(2)}, u32[]{:S(2)}) collective-permute-start(bf16[512,256]{1,0:T(8,128)(2,1)S(1)} %get-tuple-element.78), channel_id=1, source_target_pairs={{0,1},{1,0},{2,3},{3,2},{4,5},{5,4},{6,7},{7,6},{8,9},{9,8},{10,11... | collective-permute-start | bytes 786440 | tf_op jit(solution)/shard_map/ppermute | solution.py:238
  97.7 9.3 %collective-permute-start.26 = (bf16[512,256]{1,0:T(8,128)(2,1)S(1)}, bf16[512,256]{1,0:T(8,128)(2,1)S(1)}, u32[]{:S(2)}, u32[]{:S(2)}) collective-permute-start(bf16[512,256]{1,0:T(8,128)(2,1)S(1)} %get-tuple-element.73), channel_id=1, source_target_pairs={{0,16},{8,24},{16,0},{24,8},{1,17},{9,25},{17,1},{25,9},{2,18},{10... | collective-permute-start | bytes 786440 | tf_op jit(solution)/shard_map/ppermute | solution.py:238
  98.7 9.2 %collective-permute-start.29 = (bf16[512,256]{1,0:T(8,128)(2,1)S(1)}, bf16[512,256]{1,0:T(8,128)(2,1)S(1)}, u32[]{:S(2)}, u32[]{:S(2)}) collective-permute-start(bf16[512,256]{1,0:T(8,128)(2,1)S(1)} %get-tuple-element.76), channel_id=1, source_target_pairs={{0,1},{1,0},{2,3},{3,2},{4,5},{5,4},{6,7},{7,6},{8,9},{9,8},{10,11... | collective-permute-start | bytes 786440 | tf_op jit(solution)/shard_map/ppermute | solution.py:238
  100.4 11.9 %collective-permute-start.28 = (bf16[512,256]{1,0:T(8,128)(2,1)S(1)}, bf16[512,256]{1,0:T(8,128)(2,1)S(1)}, u32[]{:S(2)}, u32[]{:S(2)}) collective-permute-start(bf16[512,256]{1,0:T(8,128)(2,1)S(1)} %add_convert_fusion.1), channel_id=1, source_target_pairs={{0,1},{1,0},{2,3},{3,2},{4,5},{5,4},{6,7},{7,6},{8,9},{9,8},{10,11... | collective-permute-start | bytes 786440 | tf_op jit(solution)/shard_map/ppermute | solution.py:238
  101.5 10.8 %collective-permute-start.31 = (bf16[512,256]{1,0:T(8,128)(2,1)S(1)}, bf16[512,256]{1,0:T(8,128)(2,1)S(1)}, u32[]{:S(2)}, u32[]{:S(2)}) collective-permute-start(bf16[512,256]{1,0:T(8,128)(2,1)S(1)} %add_convert_fusion), channel_id=1, source_target_pairs={{0,16},{8,24},{16,0},{24,8},{1,17},{9,25},{17,1},{25,9},{2,18},{10... | collective-permute-start | bytes 786440 | tf_op jit(solution)/shard_map/ppermute | solution.py:238
  (14 other events, 150.5 us)

commit v4 on v2

--- a/solution.py
+++ b/solution.py
@@ -12,7 +12,8 @@
 F32 = jnp.float32
 BOTH = ("grp", "dom")
 EPS = 1e-06
-VMEM_LIMIT = 48 * 2**20
+VMEM_LIMIT = 24 * 2**20
+WIDE_LIMIT = 62 * 2**20
 
 
 def dot(a, b, ca=1, cb=0):
@@ -23,9 +24,7 @@
     return pl.BlockSpec(shape, lambda *_: (0,) * len(shape))
 
 
-def call(body, name, out_shape, in_specs, out_specs, args, grid=(1,), scratch=(), flops=0, exps=0, limit=VMEM_LIMIT):
-    outs = out_shape if isinstance(out_shape, (list, tuple)) else [out_shape]
-    moved = sum(a.size * a.dtype.itemsize for a in (*args, *outs))
+def call(body, name, out_shape, in_specs, out_specs, args, grid=(1,), scratch=(), cost=1, limit=VMEM_LIMIT):
     return pl.pallas_call(
         body,
         grid=grid,
@@ -35,7 +34,7 @@
         scratch_shapes=list(scratch),
         name=name,
         compiler_params=pltpu.CompilerParams(vmem_limit_bytes=limit),
-        cost_estimate=pl.CostEstimate(flops=flops, bytes_accessed=moved, transcendentals=exps),
+        cost_estimate=pl.CostEstimate(flops=cost, bytes_accessed=1, transcendentals=0),
     )(*args)
 
 
@@ -128,59 +127,86 @@
         keys_ref[...] = dot(keys, w_query_ref[...], 1, 1).astype(BF16)
 
 
-def smooth_up_body(count, scale, *refs):
-    nodes, keys_ref, tiles, sums_ref = refs[:count], refs[count], refs[count + 1 : -1], refs[-1]
+def smooth_up_body(count, groups, starts, scale, *refs):
+    nodes, keys, refs = refs[:count], refs[count : count + groups], refs[count + groups :]
+    (sums_ref, held), tiles = refs[-2:], refs[starts:-2]
+    step = sums_ref.shape[0]
+
+    @pl.when(pl.program_id(0) == 0)
+    def _():
+        first = 0
+        for key_ref in keys:
+            held[first : first + key_ref.shape[0], :] = key_ref[...]
+            first += key_ref.shape[0]
+
+    marks = held[pl.ds(pl.multiple_of(pl.program_id(0) * step, step), step), :]
     total = 0.0
+    for start_ref in refs[:starts]:
+        total += start_ref[...].astype(F32)
     for node_ref, tile_ref in zip(nodes, tiles):
-        tile = jnp.exp2(dot(keys_ref[...], node_ref[...], 1, 1) * scale).astype(BF16)
+        tile = jnp.exp2(dot(marks, node_ref[...], 1, 1) * scale).astype(BF16)
         tile_ref[...] = tile
         total += dot(tile, node_ref[...])
     sums_ref[...] = total.astype(BF16)
 
 
-def smooth_up(blocks, keys, name):
-    marks, c = keys.shape
+def smooth_up(blocks, keys, starts, name):
+    marks, c = sum(k.shape[0] for k in keys), keys[0].shape[1]
     step = min(marks, 512)
     scale = 2.0 * c ** (-0.5) * math.log2(math.e)
     sizes = [b.shape[0] for b in blocks]
-    keys_spec = pl.BlockSpec((step, c), lambda j: (j, 0))
+    rows_spec = pl.BlockSpec((step, c), lambda j: (j, 0))
     out = call(
-        functools.partial(smooth_up_body, len(blocks), scale),
+        functools.partial(smooth_up_body, len(blocks), len(keys), len(starts), scale),
         name,
         [jax.ShapeDtypeStruct((marks, n), BF16) for n in sizes]
         + [jax.ShapeDtypeStruct((marks, c), BF16)],
-        [whole(b.shape) for b in blocks] + [keys_spec],
-        [pl.BlockSpec((step, n), lambda j: (j, 0)) for n in sizes] + [keys_spec],
-        [*blocks, keys],
+        [whole(v.shape) for v in (*blocks, *keys)] + [rows_spec] * len(starts),
+        [pl.BlockSpec((step, n), lambda j: (j, 0)) for n in sizes] + [rows_spec],
+        [*blocks, *keys, *starts],
         grid=(marks // step,),
-        flops=4 * marks * sum(sizes) * c,
-        exps=marks * sum(sizes),
+        scratch=[pltpu.VMEM((marks, c), BF16)],
+        cost=marks * sum(sizes) * c,
     )
     return out[:-1], out[-1]
 
 
-def smooth_down_body(count, *refs):
-    tiles, sums, out_ref = refs[:count], refs[count:-1], refs[-1]
-    total = 0.0
-    for tile_ref, sum_ref in zip(tiles, sums):
-        total += dot(tile_ref[...], sum_ref[...], 0, 0)
-    out_ref[...] = total.astype(out_ref.dtype)
-
-
-def smooth_down(tiles, sums, out_dtype, name):
-    n = tiles[0].shape[1]
+def smooth_down_body(count, halves, starts, *refs):
+    tiles, sums = refs[: 2 * count], refs[2 * count : 2 * count + 2 * halves]
+    begun, outs = refs[2 * count + 2 * halves : -count], refs[-count:]
+    for b, out_ref in enumerate(outs):
+        total = begun[b][...] if starts else 0.0
+        for side, tile_ref in enumerate(tiles[2 * b : 2 * b + 2]):
+            line, mine, n = tile_ref.shape
+            part = mine // halves
+            for h in range(halves):
+                tile = tile_ref[:, h * part : (h + 1) * part, :].reshape(line * part, n)
+                total += dot(tile, sums[2 * h + side][...], 0, 0)
+        out_ref[...] = total.astype(out_ref.dtype)
+
+
+def smooth_down(jobs, sums, n, name, half=None, starts=()):
     c = sums[0].shape[1]
     step = min(n, 256)
+    rows_spec = pl.BlockSpec((step, c), lambda j: (j, 0))
+    args, specs = [], []
+    for tiles, at, _ in jobs:
+        for tile in tiles:
+            line, mine, _ = tile.shape
+            args.append(tile)
+            if half is None:
+                shape, place = (line, mine, step), 0
+            else:
+                shape, place = (line, mine // 2, step), half
+            specs.append(pl.BlockSpec(shape, lambda j, at=at, place=place: (0, place, at // step + j)))
     return call(
-        functools.partial(smooth_down_body, len(tiles)),
+        functools.partial(smooth_down_body, len(jobs), len(sums) // 2, len(starts)),
         name,
-        jax.ShapeDtypeStruct((n, c), out_dtype),
-        [pl.BlockSpec((t.shape[0], step), lambda j: (0, j)) for t in tiles]
-        + [whole(v.shape) for v in sums],
-        pl.BlockSpec((step, c), lambda j: (j, 0)),
-        [*tiles, *sums],
+        [jax.ShapeDtypeStruct((n, c), dtype) for _, _, dtype in jobs],
+        specs + [whole(v.shape) for v in sums] + [rows_spec] * len(starts),
+        [rows_spec] * len(jobs),
+        [*args, *sums, *starts],
         grid=(n // step,),
-        flops=sum(2 * t.shape[0] * n * c for t in tiles),
     )
 
 
@@ -233,7 +259,7 @@
         [whole((1, 2 * halo)), whole((rows, c))],
         [whole((halo, c))] * 2,
         [send_rows.reshape(1, 2 * halo), nodes],
-        flops=4 * halo * rows * c,
+        limit=WIDE_LIMIT,
     )
     from_prev = lax.ppermute(to_next, BOTH, [(i, (i + 1) % parts) for i in range(parts)])
     from_next = lax.ppermute(to_prev, BOTH, [((i + 1) % parts, i) for i in range(parts)])
@@ -253,7 +279,7 @@
         [links, nodes, nodes, w_src, w_dst, edge_bias.reshape(1, c)],
         grid=(steps,),
         scratch=[pltpu.VMEM((rows, c), BF16)],
-        flops=2 * slots * rows * rows * c,
+        limit=WIDE_LIMIT,
     )
     updated, normed, keys = call(
         edge_body,
@@ -290,49 +316,52 @@
         ],
         grid=(steps,),
         scratch=[pltpu.VMEM((2 * halo, c), BF16), pltpu.VMEM((rows, c), BF16)],
-        flops=4 * slots * rows * halo * c,
-        exps=slots * rows * c,
-    )
-
-    x_a, y_b = over_x(normed[:half]), over_y(normed[half:])
+        limit=WIDE_LIMIT,
+    )
+
     key_blocks = [keys] + [over_z[t](keys) for t in range(1, line)]
-    x_b, y_a = over_x(normed[half:]), over_y(normed[:half])
-    xy_a, xy_b = over_y(x_a), over_x(y_b)
+    from_x, from_y = over_x(normed), over_y(normed)
+    *key_blocks, from_x, from_y = lax.optimization_barrier((*key_blocks, from_x, from_y))
+    other_keys = [over_core(jnp.concatenate(key_blocks, axis=0))]
+    far = (over_y(from_x[:half]), over_x(from_y[half:]))
+    near = (normed, from_x, from_y)
+    near_side, side_sums = smooth_up(near, key_blocks, (), "up_near_side")
+    *near, side_sums = lax.optimization_barrier((*near, side_sums))
+    near_other, other_sums = smooth_up(near, other_keys, (), "up_near_other")
+    far_other, other_sums = smooth_up(far, other_keys, (other_sums,), "up_far_other")
+    *far, other_sums = lax.optimization_barrier((*far, other_sums))
+    far_side, side_sums = smooth_up(far, key_blocks, (side_sums,), "up_far_side")
+    core_sums = (side_sums.astype(F32) + over_core(other_sums).astype(F32)).astype(BF16)
+
     part = mine // 2
-    side = line * part
-    near = (normed, x_a, x_b, y_a, y_b)
-    tiles = [[] for _ in range(7)]
     sums = []
     for h in range(2):
-        side_keys = jnp.concatenate([k[h * part : (h + 1) * part] for k in key_blocks], axis=0)
-        marks = jnp.concatenate([side_keys, over_core(side_keys)], axis=0)
-        near_tiles, near_sums = smooth_up(near, marks, f"up_near_{h}")
-        far_tiles, far_sums = smooth_up((xy_a, xy_b), marks, f"up_far_{h}")
-        for held, tile in zip(tiles, [*near_tiles, *far_tiles]):
-            held.append(tile)
-        both = (near_sums.astype(F32) + far_sums.astype(F32)).astype(BF16)
-        core_sums = (both[:side].astype(F32) + over_core(both[side:]).astype(F32)).astype(BF16)
-        blocks = [core_sums[t * part : (t + 1) * part] for t in range(line)]
+        blocks = [core_sums[t * mine + h * part : t * mine + (h + 1) * part] for t in range(line)]
         total = blocks[0].astype(F32)
         for t in range(1, line):
             total = total + over_z[t](blocks[t]).astype(F32)
         total = dot(total.astype(BF16), w_value).astype(BF16)
-        side_sums = jnp.concatenate([total] + [over_z[t](total) for t in range(1, line)], axis=0)
-        sums.append(jnp.concatenate([side_sums, over_core(side_sums)], axis=0))
-
-    def down(block, dtype, name):
-        return smooth_down(tiles[block], sums, dtype, name)
-
-    own_tiles, x_a_tiles, x_b_tiles, y_a_tiles, y_b_tiles, xy_a_tiles, xy_b_tiles = range(7)
-    far_a = over_x(down(xy_a_tiles, BF16, "down_far_a"))
-    far_b = over_y(down(xy_b_tiles, BF16, "down_far_b"))
-    first_a = over_x(down(x_a_tiles, BF16, "down_x_a"))
-    first_b = over_y(down(y_b_tiles, BF16, "down_y_b"))
-    pass_a = down(y_a_tiles, F32, "down_y_a")
-    pass_b = down(x_b_tiles, F32, "down_x_b")
+        side = jnp.concatenate([total] + [over_z[t](total) for t in range(1, line)], axis=0)
+        sums.append((side, over_core(side)))
+
+    tiles = [
+        tuple(v.reshape(line, mine, v.shape[1]) for v in pair)
+        for pair in zip((*near_side, *far_side), (*near_other, *far_other))
+    ]
+    own_tiles, x_tiles, y_tiles, a_tiles, b_tiles = tiles
+    far_jobs = [(a_tiles, 0), (b_tiles, 0)]
+    near_jobs = [(x_tiles, 0), (y_tiles, half), (y_tiles, 0), (x_tiles, half)]
+    begun = smooth_down([(*j, F32) for j in far_jobs], sums[0], half, "down_far_first", 0)
+    far_a, far_b = smooth_down([(*j, BF16) for j in far_jobs], sums[1], half, "down_far", 1, begun)
+    *both, far_a, far_b = lax.optimization_barrier((*sums[0], *sums[1], far_a, far_b))
+    first_a, first_b, pass_a, pass_b = smooth_down(
+        [(*j, dtype) for j, dtype in zip(near_jobs, (BF16, BF16, F32, F32))], both, half, "down_near"
+    )
+    far_a, far_b = over_x(far_a), over_y(far_b)
+    first_a, first_b = over_x(first_a), over_y(first_b)
     second_a = over_y((pass_a + far_a.astype(F32)).astype(BF16))
     second_b = over_x((pass_b + far_b.astype(F32)).astype(BF16))
-    own = down(own_tiles, F32, "down_own")
+    (own,) = smooth_down([(own_tiles, 0, F32)], both, rows, "down_own")
 
     return call(
         last_body,
@@ -341,7 +370,6 @@
         [whole((rows, c))] + [whole((half, c))] * 4 + [whole((rows, c)), whole((c, c))],
         [whole((rows, c))] * 2,
         [own, first_a, second_a, first_b, second_b, updated, w_out],
-        flops=2 * rows * c * c,
     )
 
 

time: 125 us -> 110 us (0.88)
  starting transfers between devices: 41.4 us -> 35.7 us
  local copies, waits for them, and re-layouts: 6.37 us -> 0.73 us
  waiting for transfers between devices: 30.8 us -> 28.1 us
    ppermute x33 -> x29, starting transfers between devices: 34.9 us -> 29.3 us  [pair(): return lambda v: lax.ppermute(v, axis, [(i, i ^ flip) for i in range(size)])]
    unnamed x38 -> x14, local copies, waits for them, and re-layouts: 6.12 us -> 0.66 us
    ppermute x33 -> x29, waiting for transfers between devices: 30.8 us -> 28.1 us  [pair(): return lambda v: lax.ppermute(v, axis, [(i, i ^ flip) for i in range(size)])]
    pallas_call x15 -> x12, Pallas kernels: 43.9 us -> 43.2 us  [call(): pl.pallas_call(body, grid=grid, in_specs=in_specs, out_specs=out_specs, o...]
  transfers between devices with their start and end apart: 35 -> 31, of which waited for: 11 -> 15; matrix products, arithmetic and copies ran while one was open for 1% -> 0% of each run, Pallas kernels for 25% -> 25%
where the time goes in v4:
time: 110 us
  Pallas kernels  43.2 us (39%)
  starting transfers between devices  35.7 us (32%)
  waiting for transfers between devices  28.1 us (26%)
  other arithmetic  1.22 us (1%)
    pallas_call x12, Pallas kernels, call(): pl.pallas_call(body, grid=grid, in_specs=in_specs, out_specs=out_specs, o...  43.2 us
    ppermute x29, starting transfers between devices, pair(): return lambda v: lax.ppermute(v, axis, [(i, i ^ flip) for i in range(size)])  29.3 us
    ppermute x29, waiting for transfers between devices, pair(): return lambda v: lax.ppermute(v, axis, [(i, i ^ flip) for i in range(size)])  28.1 us
    ppermute x1, starting transfers between devices, shards(): lax.ppermute(to_prev, BOTH, [((i + 1) % parts, i) for i in range(parts)])  3.4 us
    ppermute x1, starting transfers between devices, shards(): lax.ppermute(to_next, BOTH, [(i, (i + 1) % parts) for i in range(parts)])  2.97 us
  transfers between devices with their start and end apart: 31, of which 15 were waited for; matrix products, arithmetic and copies ran while one was open for 0% of the time, Pallas kernels for 25%

profile of v4, /device:TPU:0, one launch (start us, length us, event | category | flops | bytes accessed | tf_op | source)
XLA Modules:
  0.0 110.1 jit_solution(12885112115906712985)
XLA Ops:
  0.6 2.1 %send_rows.1 = (bf16[128,256]{1,0:T(8,128)(2,1)}, bf16[128,256]{1,0:T(8,128)(2,1)}) custom-call(s32[1,256]{1,0:T(1,128)} %bitcast.36, bf16[1024,256]{1,0:T(8,128)(2,1)} %tile_ref.3), custom_call_target="tpu_custom_call" | custom-call | flops 1 | bytes 1 | tf_op jit(solution)/shard_map/send_rows/pallas_call | solution.py:28
  2.7 3.0 %collective-permute-start = (bf16[128,256]{1,0:T(8,128)(2,1)}, bf16[128,256]{1,0:T(8,128)(2,1)S(1)}, u32[]{:S(2)}, u32[]{:S(2)}) collective-permute-start(bf16[128,256]{1,0:T(8,128)(2,1)} %get-tuple-element.48), channel_id=1, source_target_pairs={{0,1},{1,2},{2,3},{3,4},{4,5},{5,6},{6,7},{7,8},{8,9},{9,10},{10,1... | collective-permute-start | bytes 196616 | tf_op jit(solution)/shard_map/ppermute | solution.py:264
  5.7 3.4 %collective-permute-start.1 = (bf16[128,256]{1,0:T(8,128)(2,1)}, bf16[128,256]{1,0:T(8,128)(2,1)S(1)}, u32[]{:S(2)}, u32[]{:S(2)}) collective-permute-start(bf16[128,256]{1,0:T(8,128)(2,1)} %get-tuple-element.49), channel_id=1, source_target_pairs={{1,0},{2,1},{3,2},{4,3},{5,4},{6,5},{7,6},{8,7},{9,8},{10,9},{11,1... | collective-permute-start | bytes 196616 | tf_op jit(solution)/shard_map/ppermute | solution.py:265
  9.1 8.2 %own_edges.1.pre_ref = f32[8,1024,256]{2,1,0:T(8,128)} custom-call(s32[8,1024]{1,0:T(8,128)} %bitcast.34, bf16[1024,256]{1,0:T(8,128)(2,1)} %tile_ref.3, bf16[1024,256]{1,0:T(8,128)(2,1)} %tile_ref.3, bf16[256,256]{1,0:T(8,128)(2,1)} %w_src_ref.3, bf16[256,256]{1,0:T(8,128)(2,1)} %w_dst_ref.1, f32[1,256]{1,0:T(1,128)} %bitcast.37), custom_call_target="tpu_custom_call" | custom-call | flops 1 | bytes 1 | tf_op jit(solution)/shard_map/own_edges/pallas_call | solution.py:28
  17.9 9.0 %edges.1 = (bf16[1024,256]{1,0:T(8,128)(2,1)}, bf16[1024,256]{1,0:T(8,128)(2,1)}, bf16[256,256]{1,0:T(8,128)(2,1)}) custom-call(s32[8,1024]{1,0:T(8,128)} %bitcast.35, f32[8,1024,256]{2,1,0:T(8,128)} %own_edges.1.pre_ref, bf16[128,256]{1,0:T(8,128)(2,1)} %copy-done.5, bf16[128,256]{1,0:T(8,128)(2,1)} %copy-done.6, bf16[1024,256]{1,0:T(8,128)(2,1)} %tile_ref.3, ...), custom_call_target="tpu_custom_call" | custom-call | flops 1 | bytes 1 | tf_op jit(solution)/shard_map/edges/pallas_call | solution.py:28
  27.1 2.0 %collective-permute-start.5 = (bf16[1024,256]{1,0:T(8,128)(2,1)}, bf16[1024,256]{1,0:T(8,128)(2,1)S(1)}, u32[]{:S(2)}, u32[]{:S(2)}) collective-permute-start(bf16[1024,256]{1,0:T(8,128)(2,1)} %get-tuple-element.60.refs_0_), channel_id=1, source_target_pairs={{0,16},{8,24},{16,0},{24,8},{1,17},{9,25},{17,1},{25,9},{2,18},{10... | collective-permute-start | bytes 1572872 | tf_op jit(solution)/shard_map/ppermute | solution.py:249
  30.8 2.6 %collective-permute-start.2 = (bf16[256,256]{1,0:T(8,128)(2,1)}, bf16[256,256]{1,0:T(8,128)(2,1)S(1)}, u32[]{:S(2)}, u32[]{:S(2)}) collective-permute-start(bf16[256,256]{1,0:T(8,128)(2,1)} %get-tuple-element.54.refs_3_.refs_2_), channel_id=1, source_target_pairs={{0,2},{1,3},{2,0},{3,1},{4,6},{5,7},{6,4},{7,5},{8,10},{9,11},{10,... | collective-permute-start | bytes 393224 | tf_op jit(solution)/shard_map/ppermute | solution.py:249
  33.4 4.1 %collective-permute-done.4.refs_6_.refs_5_ = bf16[256,256]{1,0:T(8,128)(2,1)S(1)} collective-permute-done((bf16[256,256]{1,0:T(8,128)(2,1)}, bf16[256,256]{1,0:T(8,128)(2,1)S(1)}, u32[]{:S(2)}, u32[]{:S(2)}) %collective-permute-start.4) | collective-permute-done | bytes 131104 | tf_op jit(solution)/shard_map/ppermute | solution.py:249
  37.5 4.3 %collective-permute-done.3.refs_5_.refs_4_ = bf16[256,256]{1,0:T(8,128)(2,1)S(1)} collective-permute-done((bf16[256,256]{1,0:T(8,128)(2,1)}, bf16[256,256]{1,0:T(8,128)(2,1)S(1)}, u32[]{:S(2)}, u32[]{:S(2)}) %collective-permute-start.3) | collective-permute-done | bytes 131104 | tf_op jit(solution)/shard_map/ppermute | solution.py:249
  45.2 5.0 %up_near_side.1 = (bf16[1024,1024]{1,0:T(8,128)(2,1)S(1)}, bf16[1024,1024]{1,0:T(8,128)(2,1)S(1)}, bf16[1024,1024]{1,0:T(8,128)(2,1)S(1)}, bf16[1024,256]{1,0:T(8,128)(2,1)S(1)}) custom-call(bf16[1024,256]{1,0:T(8,128)(2,1)S(1)} %copy-done.4, bf16[1024,256]{1,0:T(8,128)(2,1)S(1)} %collective-permute-done.5.refs_1_, ...), custom_call_target="tpu_custom_call" | custom-call | flops 805306368 | bytes 1 | tf_op jit(solution)/shard_map/up_near_side/pallas_call | solution.py:28
  50.3 5.0 %up_near_other.1 = (bf16[1024,1024]{1,0:T(8,128)(2,1)S(1)}, bf16[1024,1024]{1,0:T(8,128)(2,1)S(1)}, bf16[1024,1024]{1,0:T(8,128)(2,1)S(1)}, bf16[1024,256]{1,0:T(8,128)(2,1)S(1)}) custom-call(bf16[1024,256]{1,0:T(8,128)(2,1)S(1)} %copy-done.4, bf16[1024,256]{1,0:T(8,128)(2,1)S(1)} %collective-permute-done.5.refs_1_, ...), custom_call_target="tpu_custom_call" | custom-call | flops 805306368 | bytes 1 | tf_op jit(solution)/shard_map/up_near_other/pallas_call | solution.py:28
  57.2 1.8 %up_far_side.1 = (bf16[1024,512]{1,0:T(8,128)(2,1)S(1)}, bf16[1024,512]{1,0:T(8,128)(2,1)S(1)}, bf16[1024,256]{1,0:T(8,128)(2,1)S(1)}) custom-call(bf16[512,256]{1,0:T(8,128)(2,1)S(1)} %collective-permute-done.8.refs_0_, bf16[512,256]{1,0:T(8,128)(2,1)S(1)} %collective-permute-done.9.refs_1_, bf16[256,256]{1,0:T(8,128)(2,1)S(1)} %copy-done.2, ...), custom_call_target="tpu_custom_call" | custom-call | flops 268435456 | bytes 1 | tf_op jit(solution)/shard_map/up_far_side/pallas_call | solution.py:28
  59.3 1.9 %collective-permute-start.13 = (bf16[128,256]{1,0:T(8,128)(2,1)S(1)}, bf16[128,256]{1,0:T(8,128)(2,1)S(1)}, u32[]{:S(2)}, u32[]{:S(2)}) collective-permute-start(bf16[128,256]{1,0:T(8,128)(2,1)S(1)} %get-tuple-element.97), channel_id=1, source_target_pairs={{0,6},{1,7},{2,4},{3,5},{4,2},{5,3},{6,0},{7,1},{8,14},{9,15},{10,... | collective-permute-start | bytes 196616 | tf_op jit(solution)/shard_map/ppermute | solution.py:249
  61.2 2.6 %collective-permute-start.11 = (bf16[128,256]{1,0:T(8,128)(2,1)S(1)}, bf16[128,256]{1,0:T(8,128)(2,1)S(1)}, u32[]{:S(2)}, u32[]{:S(2)}) collective-permute-start(bf16[128,256]{1,0:T(8,128)(2,1)S(1)} %get-tuple-element.99), channel_id=1, source_target_pairs={{0,2},{1,3},{2,0},{3,1},{4,6},{5,7},{6,4},{7,5},{8,10},{9,11},{10,... | collective-permute-start | bytes 196616 | tf_op jit(solution)/shard_map/ppermute | solution.py:249
  63.8 1.8 %collective-permute-start.20 = (bf16[128,256]{1,0:T(8,128)(2,1)S(1)}, bf16[128,256]{1,0:T(8,128)(2,1)S(1)}, u32[]{:S(2)}, u32[]{:S(2)}) collective-permute-start(bf16[128,256]{1,0:T(8,128)(2,1)S(1)} %get-tuple-element.95), channel_id=1, source_target_pairs={{0,6},{1,7},{2,4},{3,5},{4,2},{5,3},{6,0},{7,1},{8,14},{9,15},{10,... | collective-permute-start | bytes 196616 | tf_op jit(solution)/shard_map/ppermute | solution.py:249
  68.6 1.9 %collective-permute-start.16 = (bf16[128,256]{1,0:T(8,128)(2,1)S(1)}, bf16[128,256]{1,0:T(8,128)(2,1)S(1)}, u32[]{:S(2)}, u32[]{:S(2)}) collective-permute-start(bf16[128,256]{1,0:T(8,128)(2,1)S(1)} %convolution_convert_fusion.1), channel_id=1, source_target_pairs={{0,6},{1,7},{2,4},{3,5},{4,2},{5,3},{6,0},{7,1},{8,14},{9,15},{10,... | collective-permute-start | bytes 196616 | tf_op jit(solution)/shard_map/ppermute | solution.py:249
  71.1 2.0 %collective-permute-start.14 = (bf16[128,256]{1,0:T(8,128)(2,1)S(1)}, bf16[128,256]{1,0:T(8,128)(2,1)S(1)}, u32[]{:S(2)}, u32[]{:S(2)}) collective-permute-start(bf16[128,256]{1,0:T(8,128)(2,1)S(1)} %convolution_convert_fusion.1), channel_id=1, source_target_pairs={{0,2},{1,3},{2,0},{3,1},{4,6},{5,7},{6,4},{7,5},{8,10},{9,11},{10,... | collective-permute-start | bytes 196616 | tf_op jit(solution)/shard_map/ppermute | solution.py:249
  73.1 4.2 %collective-permute-done.19 = bf16[128,256]{1,0:T(8,128)(2,1)S(1)} collective-permute-done((bf16[128,256]{1,0:T(8,128)(2,1)S(1)}, bf16[128,256]{1,0:T(8,128)(2,1)S(1)}, u32[]{:S(2)}, u32[]{:S(2)}) %collective-permute-start.19) | collective-permute-done | bytes 65568 | tf_op jit(solution)/shard_map/ppermute | solution.py:249
  77.4 1.9 %collective-permute-start.23 = (bf16[128,256]{1,0:T(8,128)(2,1)S(1)}, bf16[128,256]{1,0:T(8,128)(2,1)S(1)}, u32[]{:S(2)}, u32[]{:S(2)}) collective-permute-start(bf16[128,256]{1,0:T(8,128)(2,1)S(1)} %convolution_convert_fusion), channel_id=1, source_target_pairs={{0,6},{1,7},{2,4},{3,5},{4,2},{5,3},{6,0},{7,1},{8,14},{9,15},{10,... | collective-permute-start | bytes 196616 | tf_op jit(solution)/shard_map/ppermute | solution.py:249
  79.3 2.6 %collective-permute-start.21 = (bf16[128,256]{1,0:T(8,128)(2,1)S(1)}, bf16[128,256]{1,0:T(8,128)(2,1)S(1)}, u32[]{:S(2)}, u32[]{:S(2)}) collective-permute-start(bf16[128,256]{1,0:T(8,128)(2,1)S(1)} %convolution_convert_fusion), channel_id=1, source_target_pairs={{0,2},{1,3},{2,0},{3,1},{4,6},{5,7},{6,4},{7,5},{8,10},{9,11},{10,... | collective-permute-start | bytes 196616 | tf_op jit(solution)/shard_map/ppermute | solution.py:249
  82.0 1.9 %collective-permute-done.23 = bf16[128,256]{1,0:T(8,128)(2,1)S(1)} collective-permute-done((bf16[128,256]{1,0:T(8,128)(2,1)S(1)}, bf16[128,256]{1,0:T(8,128)(2,1)S(1)}, u32[]{:S(2)}, u32[]{:S(2)}) %collective-permute-start.23) | collective-permute-done | bytes 65568 | tf_op jit(solution)/shard_map/ppermute | solution.py:249
  89.9 3.8 %down_near.1 = (bf16[512,256]{1,0:T(8,128)(2,1)S(1)}, bf16[512,256]{1,0:T(8,128)(2,1)S(1)}, f32[512,256]{1,0:T(8,128)S(1)}, f32[512,256]{1,0:T(8,128)S(1)}) custom-call(bf16[4,256,1024]{2,1,0:T(8,128)(2,1)S(1)} %bitcast.16, bf16[4,256,1024]{2,1,0:T(8,128)(2,1)S(1)} %bitcast.20, bf16[4,256,1024]{2,1,0:T(8,128)(2,1)S(1)} %bitcast.18, ...), custom_call_target="tpu_custom_call" | custom-call | flops 1 | bytes 1 | tf_op jit(solution)/shard_map/down_near/pallas_call | solution.py:28
  98.8 2.6 %down_own.1.own_ref = f32[1024,256]{1,0:T(8,128)S(1)} custom-call(bf16[4,256,1024]{2,1,0:T(8,128)(2,1)S(1)} %bitcast.32, bf16[4,256,1024]{2,1,0:T(8,128)(2,1)S(1)} %bitcast.33, bf16[512,256]{1,0:T(8,128)(2,1)S(1)} %pad_maximum_fusion.1.refs_4_.refs_2_.refs_8_, bf16[512,256]{1,0:T(8,128)(2,1)S(1)} %collective-permute-done.17.refs_5_.refs_3_.refs_9_, ...), custom_call_target="tpu_custom_call" | custom-call | flops 1 | bytes 1 | tf_op jit(solution)/shard_map/down_own/pallas_call | solution.py:28
  104.1 4.5 %collective-permute-done.27.ya_ref = bf16[512,256]{1,0:T(8,128)(2,1)S(1)} collective-permute-done((bf16[512,256]{1,0:T(8,128)(2,1)S(1)}, bf16[512,256]{1,0:T(8,128)(2,1)S(1)}, u32[]{:S(2)}, u32[]{:S(2)}) %collective-permute-start.27) | collective-permute-done | bytes 262176 | tf_op jit(solution)/shard_map/ppermute | solution.py:249
  (75 shorter events, 27.2 us)
Async XLA Ops:
  2.7 14.6 %collective-permute-start = (bf16[128,256]{1,0:T(8,128)(2,1)}, bf16[128,256]{1,0:T(8,128)(2,1)S(1)}, u32[]{:S(2)}, u32[]{:S(2)}) collective-permute-start(bf16[128,256]{1,0:T(8,128)(2,1)} %get-tuple-element.48), channel_id=1, source_target_pairs={{0,1},{1,2},{2,3},{3,4},{4,5},{5,6},{6,7},{7,8},{8,9},{9,10},{10,1... | collective-permute-start | bytes 196616 | tf_op jit(solution)/shard_map/ppermute | solution.py:264
  5.7 11.6 %collective-permute-start.1 = (bf16[128,256]{1,0:T(8,128)(2,1)}, bf16[128,256]{1,0:T(8,128)(2,1)S(1)}, u32[]{:S(2)}, u32[]{:S(2)}) collective-permute-start(bf16[128,256]{1,0:T(8,128)(2,1)} %get-tuple-element.49), channel_id=1, source_target_pairs={{1,0},{2,1},{3,2},{4,3},{5,4},{6,5},{7,6},{8,7},{9,8},{10,9},{11,1... | collective-permute-start | bytes 196616 | tf_op jit(solution)/shard_map/ppermute | solution.py:265
  27.0 14.8 %collective-permute-start.6 = (bf16[1024,256]{1,0:T(8,128)(2,1)}, bf16[1024,256]{1,0:T(8,128)(2,1)S(1)}, u32[]{:S(2)}, u32[]{:S(2)}) collective-permute-start(bf16[1024,256]{1,0:T(8,128)(2,1)} %get-tuple-element.60.refs_0_), channel_id=1, source_target_pairs={{0,1},{1,0},{2,3},{3,2},{4,5},{5,4},{6,7},{7,6},{8,9},{9,8},{10,11... | collective-permute-start | bytes 1572872 | tf_op jit(solution)/shard_map/ppermute | solution.py:249
  27.1 14.7 %collective-permute-start.5 = (bf16[1024,256]{1,0:T(8,128)(2,1)}, bf16[1024,256]{1,0:T(8,128)(2,1)S(1)}, u32[]{:S(2)}, u32[]{:S(2)}) collective-permute-start(bf16[1024,256]{1,0:T(8,128)(2,1)} %get-tuple-element.60.refs_0_), channel_id=1, source_target_pairs={{0,16},{8,24},{16,0},{24,8},{1,17},{9,25},{17,1},{25,9},{2,18},{10... | collective-permute-start | bytes 1572872 | tf_op jit(solution)/shard_map/ppermute | solution.py:249
  29.0 8.4 %collective-permute-start.4 = (bf16[256,256]{1,0:T(8,128)(2,1)}, bf16[256,256]{1,0:T(8,128)(2,1)S(1)}, u32[]{:S(2)}, u32[]{:S(2)}) collective-permute-start(bf16[256,256]{1,0:T(8,128)(2,1)} %get-tuple-element.54.refs_3_.refs_2_), channel_id=1, source_target_pairs={{0,6},{1,7},{2,4},{3,5},{4,2},{5,3},{6,0},{7,1},{8,14},{9,15},{10,... | collective-permute-start | bytes 393224 | tf_op jit(solution)/shard_map/ppermute | solution.py:249
  30.8 11.0 %collective-permute-start.3 = (bf16[256,256]{1,0:T(8,128)(2,1)}, bf16[256,256]{1,0:T(8,128)(2,1)S(1)}, u32[]{:S(2)}, u32[]{:S(2)}) collective-permute-start(bf16[256,256]{1,0:T(8,128)(2,1)} %get-tuple-element.54.refs_3_.refs_2_), channel_id=1, source_target_pairs={{0,4},{1,5},{2,6},{3,7},{4,0},{5,1},{6,2},{7,3},{8,12},{9,13},{10,... | collective-permute-start | bytes 393224 | tf_op jit(solution)/shard_map/ppermute | solution.py:249
  30.8 11.0 %collective-permute-start.2 = (bf16[256,256]{1,0:T(8,128)(2,1)}, bf16[256,256]{1,0:T(8,128)(2,1)S(1)}, u32[]{:S(2)}, u32[]{:S(2)}) collective-permute-start(bf16[256,256]{1,0:T(8,128)(2,1)} %get-tuple-element.54.refs_3_.refs_2_), channel_id=1, source_target_pairs={{0,2},{1,3},{2,0},{3,1},{4,6},{5,7},{6,4},{7,5},{8,10},{9,11},{10,... | collective-permute-start | bytes 393224 | tf_op jit(solution)/shard_map/ppermute | solution.py:249
  42.7 7.5 %collective-permute-start.7 = (bf16[1024,256]{1,0:T(8,128)(2,1)S(1)}, bf16[1024,256]{1,0:T(8,128)(2,1)S(1)}, u32[]{:S(2)}, u32[]{:S(2)}) collective-permute-start(bf16[1024,256]{1,0:T(8,128)(2,1)S(1)} %pad_maximum_fusion), channel_id=1, source_target_pairs={{0,8},{8,0},{16,24},{24,16},{1,9},{9,1},{17,25},{25,17},{2,10},{10... | collective-permute-start | bytes 1572872 | tf_op jit(solution)/shard_map/ppermute | solution.py:249
  42.9 12.5 %collective-permute-start.9 = (bf16[512,256]{1,0:T(8,128)(2,1)S(1)}, bf16[512,256]{1,0:T(8,128)(2,1)S(1)}, u32[]{:S(2)}, u32[]{:S(2)}) collective-permute-start(bf16[512,256]{1,0:T(8,128)(2,1)S(1)} %slice.31), channel_id=1, source_target_pairs={{0,16},{8,24},{16,0},{24,8},{1,17},{9,25},{17,1},{25,9},{2,18},{10... | collective-permute-start | bytes 786440 | tf_op jit(solution)/shard_map/ppermute | solution.py:249
  43.6 11.8 %collective-permute-start.8 = (bf16[512,256]{1,0:T(8,128)(2,1)S(1)}, bf16[512,256]{1,0:T(8,128)(2,1)S(1)}, u32[]{:S(2)}, u32[]{:S(2)}) collective-permute-start(bf16[512,256]{1,0:T(8,128)(2,1)S(1)} %slice.30), channel_id=1, source_target_pairs={{0,1},{1,0},{2,3},{3,2},{4,5},{5,4},{6,7},{7,6},{8,9},{9,8},{10,11... | collective-permute-start | bytes 786440 | tf_op jit(solution)/shard_map/ppermute | solution.py:249
  61.2 7.3 %collective-permute-start.12 = (bf16[128,256]{1,0:T(8,128)(2,1)S(1)}, bf16[128,256]{1,0:T(8,128)(2,1)S(1)}, u32[]{:S(2)}, u32[]{:S(2)}) collective-permute-start(bf16[128,256]{1,0:T(8,128)(2,1)S(1)} %get-tuple-element.98), channel_id=1, source_target_pairs={{0,4},{1,5},{2,6},{3,7},{4,0},{5,1},{6,2},{7,3},{8,12},{9,13},{10,... | collective-permute-start | bytes 196616 | tf_op jit(solution)/shard_map/ppermute | solution.py:249
  61.2 7.3 %collective-permute-start.11 = (bf16[128,256]{1,0:T(8,128)(2,1)S(1)}, bf16[128,256]{1,0:T(8,128)(2,1)S(1)}, u32[]{:S(2)}, u32[]{:S(2)}) collective-permute-start(bf16[128,256]{1,0:T(8,128)(2,1)S(1)} %get-tuple-element.99), channel_id=1, source_target_pairs={{0,2},{1,3},{2,0},{3,1},{4,6},{5,7},{6,4},{7,5},{8,10},{9,11},{10,... | collective-permute-start | bytes 196616 | tf_op jit(solution)/shard_map/ppermute | solution.py:249
  63.8 7.3 %collective-permute-start.18 = (bf16[128,256]{1,0:T(8,128)(2,1)S(1)}, bf16[128,256]{1,0:T(8,128)(2,1)S(1)}, u32[]{:S(2)}, u32[]{:S(2)}) collective-permute-start(bf16[128,256]{1,0:T(8,128)(2,1)S(1)} %get-tuple-element.94), channel_id=1, source_target_pairs={{0,2},{1,3},{2,0},{3,1},{4,6},{5,7},{6,4},{7,5},{8,10},{9,11},{10,... | collective-permute-start | bytes 196616 | tf_op jit(solution)/shard_map/ppermute | solution.py:249
  63.8 9.3 %collective-permute-start.20 = (bf16[128,256]{1,0:T(8,128)(2,1)S(1)}, bf16[128,256]{1,0:T(8,128)(2,1)S(1)}, u32[]{:S(2)}, u32[]{:S(2)}) collective-permute-start(bf16[128,256]{1,0:T(8,128)(2,1)S(1)} %get-tuple-element.95), channel_id=1, source_target_pairs={{0,6},{1,7},{2,4},{3,5},{4,2},{5,3},{6,0},{7,1},{8,14},{9,15},{10,... | collective-permute-start | bytes 196616 | tf_op jit(solution)/shard_map/ppermute | solution.py:249
  66.2 11.1 %collective-permute-start.19 = (bf16[128,256]{1,0:T(8,128)(2,1)S(1)}, bf16[128,256]{1,0:T(8,128)(2,1)S(1)}, u32[]{:S(2)}, u32[]{:S(2)}) collective-permute-start(bf16[128,256]{1,0:T(8,128)(2,1)S(1)} %get-tuple-element.96), channel_id=1, source_target_pairs={{0,4},{1,5},{2,6},{3,7},{4,0},{5,1},{6,2},{7,3},{8,12},{9,13},{10,... | collective-permute-start | bytes 196616 | tf_op jit(solution)/shard_map/ppermute | solution.py:249
  68.6 10.7 %collective-permute-start.16 = (bf16[128,256]{1,0:T(8,128)(2,1)S(1)}, bf16[128,256]{1,0:T(8,128)(2,1)S(1)}, u32[]{:S(2)}, u32[]{:S(2)}) collective-permute-start(bf16[128,256]{1,0:T(8,128)(2,1)S(1)} %convolution_convert_fusion.1), channel_id=1, source_target_pairs={{0,6},{1,7},{2,4},{3,5},{4,2},{5,3},{6,0},{7,1},{8,14},{9,15},{10,... | collective-permute-start | bytes 196616 | tf_op jit(solution)/shard_map/ppermute | solution.py:249
  70.5 11.4 %collective-permute-start.15 = (bf16[128,256]{1,0:T(8,128)(2,1)S(1)}, bf16[128,256]{1,0:T(8,128)(2,1)S(1)}, u32[]{:S(2)}, u32[]{:S(2)}) collective-permute-start(bf16[128,256]{1,0:T(8,128)(2,1)S(1)} %convolution_convert_fusion.1), channel_id=1, source_target_pairs={{0,4},{1,5},{2,6},{3,7},{4,0},{5,1},{6,2},{7,3},{8,12},{9,13},{10,... | collective-permute-start | bytes 196616 | tf_op jit(solution)/shard_map/ppermute | solution.py:249
  71.1 10.8 %collective-permute-start.14 = (bf16[128,256]{1,0:T(8,128)(2,1)S(1)}, bf16[128,256]{1,0:T(8,128)(2,1)S(1)}, u32[]{:S(2)}, u32[]{:S(2)}) collective-permute-start(bf16[128,256]{1,0:T(8,128)(2,1)S(1)} %convolution_convert_fusion.1), channel_id=1, source_target_pairs={{0,2},{1,3},{2,0},{3,1},{4,6},{5,7},{6,4},{7,5},{8,10},{9,11},{10,... | collective-permute-start | bytes 196616 | tf_op jit(solution)/shard_map/ppermute | solution.py:249
  88.0 8.9 %collective-permute-start.26 = (bf16[512,256]{1,0:T(8,128)(2,1)S(1)}, bf16[512,256]{1,0:T(8,128)(2,1)S(1)}, u32[]{:S(2)}, u32[]{:S(2)}) collective-permute-start(bf16[512,256]{1,0:T(8,128)(2,1)S(1)} %get-tuple-element.89), channel_id=1, source_target_pairs={{0,16},{8,24},{16,0},{24,8},{1,17},{9,25},{17,1},{25,9},{2,18},{10... | collective-permute-start | bytes 786440 | tf_op jit(solution)/shard_map/ppermute | solution.py:249
  89.3 9.2 %collective-permute-start.29 = (bf16[512,256]{1,0:T(8,128)(2,1)S(1)}, bf16[512,256]{1,0:T(8,128)(2,1)S(1)}, u32[]{:S(2)}, u32[]{:S(2)}) collective-permute-start(bf16[512,256]{1,0:T(8,128)(2,1)S(1)} %get-tuple-element.92), channel_id=1, source_target_pairs={{0,1},{1,0},{2,3},{3,2},{4,5},{5,4},{6,7},{7,6},{8,9},{9,8},{10,11... | collective-permute-start | bytes 786440 | tf_op jit(solution)/shard_map/ppermute | solution.py:249
  93.7 9.3 %collective-permute-start.25 = (bf16[512,256]{1,0:T(8,128)(2,1)S(1)}, bf16[512,256]{1,0:T(8,128)(2,1)S(1)}, u32[]{:S(2)}, u32[]{:S(2)}) collective-permute-start(bf16[512,256]{1,0:T(8,128)(2,1)S(1)} %get-tuple-element.87), channel_id=1, source_target_pairs={{0,16},{8,24},{16,0},{24,8},{1,17},{9,25},{17,1},{25,9},{2,18},{10... | collective-permute-start | bytes 786440 | tf_op jit(solution)/shard_map/ppermute | solution.py:249
  94.3 9.8 %collective-permute-start.28 = (bf16[512,256]{1,0:T(8,128)(2,1)S(1)}, bf16[512,256]{1,0:T(8,128)(2,1)S(1)}, u32[]{:S(2)}, u32[]{:S(2)}) collective-permute-start(bf16[512,256]{1,0:T(8,128)(2,1)S(1)} %get-tuple-element.90), channel_id=1, source_target_pairs={{0,1},{1,0},{2,3},{3,2},{4,5},{5,4},{6,7},{7,6},{8,9},{9,8},{10,11... | collective-permute-start | bytes 786440 | tf_op jit(solution)/shard_map/ppermute | solution.py:249
  97.0 11.7 %collective-permute-start.27 = (bf16[512,256]{1,0:T(8,128)(2,1)S(1)}, bf16[512,256]{1,0:T(8,128)(2,1)S(1)}, u32[]{:S(2)}, u32[]{:S(2)}) collective-permute-start(bf16[512,256]{1,0:T(8,128)(2,1)S(1)} %add_convert_fusion.2), channel_id=1, source_target_pairs={{0,1},{1,0},{2,3},{3,2},{4,5},{5,4},{6,7},{7,6},{8,9},{9,8},{10,11... | collective-permute-start | bytes 786440 | tf_op jit(solution)/shard_map/ppermute | solution.py:249
  98.6 10.1 %collective-permute-start.30 = (bf16[512,256]{1,0:T(8,128)(2,1)S(1)}, bf16[512,256]{1,0:T(8,128)(2,1)S(1)}, u32[]{:S(2)}, u32[]{:S(2)}) collective-permute-start(bf16[512,256]{1,0:T(8,128)(2,1)S(1)} %add_convert_fusion.1), channel_id=1, source_target_pairs={{0,16},{8,24},{16,0},{24,8},{1,17},{9,25},{17,1},{25,9},{2,18},{10... | collective-permute-start | bytes 786440 | tf_op jit(solution)/shard_map/ppermute | solution.py:249
  (14 other events, 157.6 us)

commit v5 on v4

v5 whole, which is shorter than its diff:
```python
import functools
import math

import jax
import jax.numpy as jnp
from jax import lax
from jax.experimental import pallas as pl
from jax.experimental.pallas import tpu as pltpu
from jax.sharding import PartitionSpec as P

BF16 = jnp.bfloat16
F32 = jnp.float32
BOTH = ("grp", "dom")
EPS = 1e-06
VMEM_LIMIT = 24 * 2**20


def dot(a, b, ca=1, cb=0):
    return lax.dot_general(a, b, (((ca,), (cb,)), ((), ())), preferred_element_type=F32)


def whole(shape):
    return pl.BlockSpec(shape, lambda *_: (0,) * len(shape))


def call(body, name, out_shape, in_specs, out_specs, args, grid=(1,), scratch=(), cost=1, limit=VMEM_LIMIT):
    return pl.pallas_call(
        body,
        grid=grid,
        in_specs=in_specs,
        out_specs=out_specs,
        out_shape=out_shape,
        scratch_shapes=list(scratch),
        name=name,
        compiler_params=pltpu.CompilerParams(vmem_limit_bytes=limit),
        cost_estimate=pl.CostEstimate(flops=cost, bytes_accessed=1, transcendentals=0),
    )(*args)


VMEM = pl.BlockSpec(memory_space=pltpu.VMEM)
HBM = pl.BlockSpec(memory_space=pltpu.HBM)


def call_flat(body, name, out_shape, args, in_specs=None, scratch=(), cost=1, limit=VMEM_LIMIT):
    return pl.pallas_call(
        body,
        in_specs=in_specs or [VMEM] * len(args),
        out_specs=[VMEM] * len(out_shape),
        out_shape=out_shape,
        scratch_shapes=list(scratch),
        name=name,
        compiler_params=pltpu.CompilerParams(vmem_limit_bytes=limit),
        cost_estimate=pl.CostEstimate(flops=cost, bytes_accessed=1, transcendentals=0),
    )(*args)


def picked(ids, table):
    rows = table.shape[0]
    place = lax.broadcasted_iota(jnp.int32, (rows, ids.shape[1]), 0)
    hot = jnp.where(place == ids, 1.0, 0.0).astype(BF16)
    return dot(hot, table, 0, 0).astype(BF16)


def send_body(count, *refs):
    given, (twin_ref, rest_ref), kept = refs[:count], refs[count : count + 2], refs[count + 2 : -2]
    ids, arrived = refs[-2:]
    copies = [
        pltpu.make_async_copy(src, dst, arrived.at[i])
        for i, (src, dst) in enumerate(zip(given, (ids, *kept)))
    ]
    for copy in copies:
        copy.start()
    copies[0].wait()
    copies[1].wait()
    rows = picked(ids[...], kept[0][...])
    half = rows.shape[0] // 2
    odd = lax.rem(lax.axis_index("dom"), 2) == 1
    twin_ref[...] = jnp.where(odd, rows[:half], rows[half:])
    rest_ref[...] = jnp.where(odd, rows[half:], rows[:half])
    for copy in copies[2:]:
        copy.wait()


def hot_rows(ids, first, width):
    n = ids.shape[1]
    spread = jnp.transpose(jnp.broadcast_to(ids, (128, n)))
    lane = lax.broadcasted_iota(jnp.int32, (n, 128), 1)
    parts = [
        jnp.where(spread == lane + (first + 128 * c), 1.0, 0.0).astype(BF16)
        for c in range(width // 128)
    ]
    return jnp.concatenate(parts, axis=1)


def own_body(nodes, w_src, links, w_dst, bias, pre_ref, source):
    source[...] = dot(nodes[...], w_src[...]).astype(BF16)
    slots, rows = links.shape
    tile = min(rows, 256)
    for first in range(0, rows, tile):
        at = slice(first, first + tile)
        target = dot(nodes[at, :], w_dst[...]) + bias[...]
        for k in range(slots):
            hot = hot_rows(links[k : k + 1, at], 0, rows)
            pre_ref[k, at, :] = dot(hot, source[...]) + target


def twice_gelu(x):
    slope = math.sqrt(2.0 / math.pi)
    return x * (1.0 + jnp.tanh(x * (slope + (0.044715 * slope) * (x * x))))


def edge_body(
    nodes,
    w_src,
    links,
    ids,
    w_msg,
    w_key,
    w_query,
    pre,
    twin,
    rest,
    updated_ref,
    normed_ref,
    keys_ref,
    source,
):
    halo = twin.shape[0]
    slots, rows = links.shape
    odd = lax.rem(lax.axis_index("dom"), 2) == 1
    source[:halo] = dot(jnp.where(odd, twin[...], rest[...]), w_src[...]).astype(BF16)
    source[halo:] = dot(jnp.where(odd, rest[...], twin[...]), w_src[...]).astype(BF16)
    tile = min(rows, 256)
    for first in range(0, rows, tile):
        at = slice(first, first + tile)
        total = 0.0
        for k in range(slots):
            hot = hot_rows(links[k : k + 1, at], rows, 2 * halo)
            total += twice_gelu(pre[k, at, :] + dot(hot, source[...]))
        messages = (total * (0.5 / slots)).astype(BF16)
        updated = (nodes[at, :].astype(F32) + dot(messages, w_msg[...])).astype(BF16)
        updated_ref[at, :] = updated
        wide = updated.astype(F32)
        normed = wide * lax.rsqrt(jnp.mean(wide * wide, axis=1, keepdims=True) + EPS)
        normed_ref[at, :] = normed.astype(BF16)
    keys = dot(picked(ids[...], normed_ref[...]), w_key[...]).astype(BF16)
    keys_ref[...] = dot(keys, w_query[...], 1, 1).astype(BF16)


def smooth_up_body(count, groups, starts, scale, *refs):
    nodes, keys, refs = refs[:count], refs[count : count + groups], refs[count + groups :]
    (sums_ref, held), tiles = refs[-2:], refs[starts:-2]
    first = 0
    for key_ref in keys:
        held[first : first + key_ref.shape[0], :] = key_ref[...]
        first += key_ref.shape[0]
    step = min(first, 512)
    for first in range(0, first, step):
        at = slice(first, first + step)
        total = 0.0
        for start_ref in refs[:starts]:
            total += start_ref[at, :].astype(F32)
        for node_ref, tile_ref in zip(nodes, tiles):
            tile = jnp.exp2(dot(held[at, :], node_ref[...], 1, 1) * scale).astype(BF16)
            tile_ref[at, :] = tile
            total += dot(tile, node_ref[...])
        sums_ref[at, :] = total.astype(BF16)


def smooth_up(blocks, keys, starts, name):
    marks, c = sum(k.shape[0] for k in keys), keys[0].shape[1]
    sizes = [b.shape[0] for b in blocks]
    out = call_flat(
        functools.partial(
            smooth_up_body, len(blocks), len(keys), len(starts), 2.0 * c ** (-0.5) * math.log2(math.e)
        ),
        name,
        [jax.ShapeDtypeStruct((marks, n), BF16) for n in sizes]
        + [jax.ShapeDtypeStruct((marks, c), BF16)],
        [*blocks, *keys, *starts],
        scratch=[pltpu.VMEM((marks, c), BF16)],
        cost=marks * sum(sizes) * c,
    )
    return out[:-1], out[-1]


def smooth_down_body(places, n, halves, starts, *refs):
    count = len(places)
    tiles, sums = refs[: 2 * count], refs[2 * count : 2 * count + 2 * len(halves)]
    begun, outs = refs[2 * count + 2 * len(halves) : -count], refs[-count:]
    for b, out_ref in enumerate(outs):
        total = begun[b][...] if starts else 0.0
        for side, tile_ref in enumerate(tiles[2 * b : 2 * b + 2]):
            line, mine, _ = tile_ref.shape
            part = mine // 2
            for i, h in enumerate(halves):
                tile = tile_ref[:, h * part : (h + 1) * part, places[b] : places[b] + n]
                total += dot(tile.reshape(line * part, n), sums[2 * i + side][...], 0, 0)
        out_ref[...] = total.astype(out_ref.dtype)


def smooth_down(jobs, sums, n, name, halves=(0, 1), starts=()):
    c = sums[0].shape[1]
    return call_flat(
        functools.partial(smooth_down_body, [at for _, at, _ in jobs], n, halves, len(starts)),
        name,
        [jax.ShapeDtypeStruct((n, c), dtype) for _, _, dtype in jobs],
        [*(tile for tiles, _, _ in jobs for tile in tiles), *sums, *starts],
    )


def last_body(own_ref, xa_ref, ya_ref, yb_ref, xb_ref, updated_ref, w_out_ref, result_ref, term_ref):
    half = own_ref.shape[0] // 2
    for h, first, second in ((0, xa_ref, ya_ref), (1, yb_ref, xb_ref)):
        at = slice(h * half, (h + 1) * half)
        smooth = own_ref[at, :] + first[...].astype(F32) + second[...].astype(F32)
        term = smooth * lax.rsqrt(jnp.mean(smooth * smooth, axis=1, keepdims=True) + EPS)
        term_ref[at, :] = term
        result = updated_ref[at, :].astype(F32) + dot(term.astype(BF16), w_out_ref[...])
        result_ref[at, :] = result.astype(BF16)


def shards(
    groups,
    domains,
    nodes,
    neighbours,
    send_rows,
    landmark_ids,
    w_dst,
    w_src,
    w_msg,
    edge_bias,
    w_query,
    w_key,
    w_value,
    w_out,
):
    rows, c = nodes.shape
    halo = send_rows.shape[0] // 2
    mine = landmark_ids.shape[0]
    slots = neighbours.shape[1]
    line = domains // 2
    parts = groups * domains
    half = rows // 2

    def pair(axis, size, flip):
        return lambda v: lax.ppermute(v, axis, [(i, i ^ flip) for i in range(size)])

    over_core = pair("grp", groups, 1)
    over_x = pair("grp", groups, 2)
    over_y = pair("dom", domains, 1)
    over_z = [pair("dom", domains, 2 * t) for t in range(line)]
    given = [
        send_rows.reshape(1, 2 * halo),
        nodes,
        w_src,
        neighbours.T,
        w_dst,
        edge_bias.reshape(1, c),
        landmark_ids.reshape(1, mine),
        w_msg,
        w_key,
        w_query,
    ]
    to_twin, to_rest, *kept = call_flat(
        functools.partial(send_body, len(given)),
        "send_rows",
        [jax.ShapeDtypeStruct((halo, c), BF16)] * 2
        + [pltpu.VMEM(v.shape, v.dtype) for v in given[1:]],
        [pltpu.with_memory_space_constraint(v, pltpu.HBM) for v in given],
        in_specs=[HBM] * len(given),
        scratch=[
            pltpu.VMEM((1, 2 * halo), jnp.int32),
            pltpu.SemaphoreType.DMA((len(given),)),
        ],
    )
    twin = over_y(to_twin)
    rest = lax.ppermute(
        to_rest, BOTH, [(p, (p + (1 if p % 2 else -1)) % parts) for p in range(parts)]
    )
    (pre,) = call_flat(
        own_body,
        "own_edges",
        [jax.ShapeDtypeStruct((slots, rows, c), F32)],
        kept[:5],
        scratch=[pltpu.VMEM((rows, c), BF16)],
    )
    updated, normed, keys = call_flat(
        edge_body,
        "edges",
        [
            jax.ShapeDtypeStruct((rows, c), BF16),
            jax.ShapeDtypeStruct((rows, c), BF16),
            jax.ShapeDtypeStruct((mine, c), BF16),
        ],
        [*kept[:3], *kept[5:], pre, twin, rest],
        scratch=[pltpu.VMEM((2 * halo, c), BF16)],
    )

    key_blocks = [keys] + [over_z[t](keys) for t in range(1, line)]
    from_x, from_y = over_x(normed), over_y(normed)
    *key_blocks, from_x, from_y = lax.optimization_barrier((*key_blocks, from_x, from_y))
    other_keys = [over_core(jnp.concatenate(key_blocks, axis=0))]
    far = (over_y(from_x[:half]), over_x(from_y[half:]))
    near = (normed, from_x, from_y)
    near_side, side_sums = smooth_up(near, key_blocks, (), "up_near_side")
    *near, side_sums = lax.optimization_barrier((*near, side_sums))
    near_other, other_sums = smooth_up(near, other_keys, (), "up_near_other")
    far_other, other_sums = smooth_up(far, other_keys, (other_sums,), "up_far_other")
    *far, other_sums = lax.optimization_barrier((*far, other_sums))
    far_side, side_sums = smooth_up(far, key_blocks, (side_sums,), "up_far_side")
    core_sums = (side_sums.astype(F32) + over_core(other_sums).astype(F32)).astype(BF16)

    part = mine // 2
    sums = []
    for h in range(2):
        blocks = [core_sums[t * mine + h * part : t * mine + (h + 1) * part] for t in range(line)]
        total = blocks[0].astype(F32)
        for t in range(1, line):
            total = total + over_z[t](blocks[t]).astype(F32)
        total = dot(total.astype(BF16), w_value).astype(BF16)
        side = jnp.concatenate([total] + [over_z[t](total) for t in range(1, line)], axis=0)
        sums.append((side, over_core(side)))

    tiles = [
        tuple(v.reshape(line, mine, v.shape[1]) for v in pair)
        for pair in zip((*near_side, *far_side), (*near_other, *far_other))
    ]
    own_tiles, x_tiles, y_tiles, a_tiles, b_tiles = tiles
    far_jobs = [(a_tiles, 0), (b_tiles, 0)]
    near_jobs = [(x_tiles, 0), (y_tiles, half), (y_tiles, 0), (x_tiles, half)]
    begun = smooth_down([(*j, F32) for j in far_jobs], sums[0], half, "down_far_first", (0,))
    far_a, far_b = smooth_down([(*j, BF16) for j in far_jobs], sums[1], half, "down_far", (1,), begun)
    *both, far_a, far_b = lax.optimization_barrier((*sums[0], *sums[1], far_a, far_b))
    first_a, first_b, pass_a, pass_b = smooth_down(
        [(*j, dtype) for j, dtype in zip(near_jobs, (BF16, BF16, F32, F32))], both, half, "down_near"
    )
    far_a, far_b = over_x(far_a), over_y(far_b)
    first_a, first_b = over_x(first_a), over_y(first_b)
    second_a = over_y((pass_a + far_a.astype(F32)).astype(BF16))
    second_b = over_x((pass_b + far_b.astype(F32)).astype(BF16))
    (own,) = smooth_down([(own_tiles, 0, F32)], both, rows, "down_own")

    return call(
        last_body,
        "last",
        [jax.ShapeDtypeStruct((rows, c), BF16), jax.ShapeDtypeStruct((rows, c), F32)],
        [whole((rows, c))] + [whole((half, c))] * 4 + [whole((rows, c)), whole((c, c))],
        [whole((rows, c))] * 2,
        [own, first_a, second_a, first_b, second_b, updated, w_out],
    )


def solution(mesh):
    split = P(BOTH, None)
    return jax.shard_map(
        functools.partial(shards, mesh.shape["grp"], mesh.shape["dom"]),
        mesh=mesh,
        in_specs=(split, split, P(BOTH), P(BOTH)) + (P(),) * 8,
        out_specs=(split, split),
        check_vma=False,
    )
```

time: 110 us -> 98.4 us (0.89)
  Pallas kernels: 43.2 us -> 30 us
  waiting for transfers between devices: 28.1 us -> 30.4 us
    pallas_call x12 -> x1, Pallas kernels: 43.2 us -> 1.47 us  [call(): pl.pallas_call(body, grid=grid, in_specs=in_specs, out_specs=out_specs, o...]
    pallas_call x0 -> x11, Pallas kernels: none -> 28.5 us  [call_flat(): pl.pallas_call(body, in_specs=in_specs or [VMEM] * len(args), out_specs=[...]
    ppermute x29 -> x30, starting transfers between devices: 29.3 us -> 32.7 us  [pair(): return lambda v: lax.ppermute(v, axis, [(i, i ^ flip) for i in range(size)])]
    ppermute x2 -> x1, starting transfers between devices: 6.37 us -> 3.62 us  [shards(): lax.ppermute(to_rest, BOTH, [(p, (p + (1 if p % 2 else -1)) % parts) for...]
    ppermute x29 -> x30, waiting for transfers between devices: 28.1 us -> 30.4 us  [pair(): return lambda v: lax.ppermute(v, axis, [(i, i ^ flip) for i in range(size)])]
  transfers between devices with their start and end apart: 31 -> 31, of which waited for: 15 -> 15; matrix products, arithmetic and copies ran while one was open for 0% -> 1% of each run, Pallas kernels for 25% -> 20%
where the time goes in v5:
time: 98.4 us; the launch traced here: 98.3 us
  starting transfers between devices  36.3 us (37%)
  waiting for transfers between devices  30.4 us (31%)
  Pallas kernels  30 us (30%)
    ppermute x30, starting transfers between devices, pair(): return lambda v: lax.ppermute(v, axis, [(i, i ^ flip) for i in range(size)])  32.7 us
    ppermute x30, waiting for transfers between devices, pair(): return lambda v: lax.ppermute(v, axis, [(i, i ^ flip) for i in range(size)])  30.4 us
    pallas_call x11, Pallas kernels, call_flat(): pl.pallas_call(body, in_specs=in_specs or [VMEM] * len(args), out_specs=[...  28.5 us
    ppermute x1, starting transfers between devices, shards(): lax.ppermute(to_rest, BOTH, [(p, (p + (1 if p % 2 else -1)) % parts) for...  3.62 us
  transfers between devices with their start and end apart: 31, of which 15 were waited for; matrix products, arithmetic and copies ran while one was open for 1% of the time, Pallas kernels for 20%

profile of v5, /device:TPU:0, one launch (start us, length us, event | category | flops | bytes accessed | tf_op | source)
XLA Modules:
  0.0 98.3 jit_solution(4168047107661053996)
XLA Ops:
  0.6 1.6 %send_rows.1 = (bf16[128,256]{1,0:T(8,128)(2,1)S(1)}, bf16[128,256]{1,0:T(8,128)(2,1)S(1)}, bf16[1024,256]{1,0:T(8,128)(2,1)S(1)}, bf16[256,256]{1,0:T(8,128)(2,...) custom-call(s32[1,256]{1,0:T(1,128)} %bitcast.35, ...), custom_call_target="tpu_custom_call" | custom-call | flops 1 | bytes 1 | tf_op jit(solution)/shard_map/send_rows/pallas_call | solution.py:45
  2.2 3.0 %collective-permute-start = (bf16[128,256]{1,0:T(8,128)(2,1)S(1)}, bf16[128,256]{1,0:T(8,128)(2,1)S(1)}, u32[]{:S(2)}, u32[]{:S(2)}) collective-permute-start(bf16[128,256]{1,0:T(8,128)(2,1)S(1)} %get-tuple-element.66), channel_id=1, source_target_pairs={{0,1},{1,0},{2,3},{3,2},{4,5},{5,4},{6,7},{7,6},{8,9},{9,8},{10,11... | collective-permute-start | bytes 196616 | tf_op jit(solution)/shard_map/ppermute | solution.py:248
  5.3 3.6 %collective-permute-start.1 = (bf16[128,256]{1,0:T(8,128)(2,1)S(1)}, bf16[128,256]{1,0:T(8,128)(2,1)S(1)}, u32[]{:S(2)}, u32[]{:S(2)}) collective-permute-start(bf16[128,256]{1,0:T(8,128)(2,1)S(1)} %get-tuple-element.67), channel_id=1, source_target_pairs={{0,31},{1,2},{2,1},{3,4},{4,3},{5,6},{6,5},{7,8},{8,7},{9,10},{10,... | collective-permute-start | bytes 196616 | tf_op jit(solution)/shard_map/ppermute | solution.py:279
  8.9 5.5 %own_edges.1.pre = f32[8,1024,256]{2,1,0:T(8,128)S(1)} custom-call(bf16[1024,256]{1,0:T(8,128)(2,1)S(1)} %get-tuple-element.57.nodes, bf16[256,256]{1,0:T(8,128)(2,1)S(1)} %get-tuple-element.58.w_src, s32[8,1024]{1,0:T(8,128)S(1)} %get-tuple-element.59.links, bf16[256,256]{1,0:T(8,128)(2,1)S(1)} %get-tuple-element.64.w_dst, f32[1,256]{1,0:T(1,128)S(1)} %get-tuple-element.65.bias), custom_call_target="tpu_custom_call" | custom-call | flops 1 | bytes 1 | tf_op jit(solution)/shard_map/own_edges/pallas_call | solution.py:45
  14.4 4.6 %edges.1 = (bf16[1024,256]{1,0:T(8,128)(2,1)S(1)}, bf16[1024,256]{1,0:T(8,128)(2,1)S(1)}, bf16[256,256]{1,0:T(8,128)(2,1)S(1)}) custom-call(bf16[1024,256]{1,0:T(8,128)(2,1)S(1)} %get-tuple-element.57.nodes, bf16[256,256]{1,0:T(8,128)(2,1)S(1)} %get-tuple-element.58.w_src, s32[8,1024]{1,0:T(8,128)S(1)} %get-tuple-element.59.links, ...), custom_call_target="tpu_custom_call" | custom-call | flops 1 | bytes 1 | tf_op jit(solution)/shard_map/edges/pallas_call | solution.py:45
  20.0 2.7 %collective-permute-start.4 = (bf16[256,256]{1,0:T(8,128)(2,1)S(1)}, bf16[256,256]{1,0:T(8,128)(2,1)S(1)}, u32[]{:S(2)}, u32[]{:S(2)}) collective-permute-start(bf16[256,256]{1,0:T(8,128)(2,1)S(1)} %get-tuple-element.72.refs_3_.refs_2_), channel_id=1, source_target_pairs={{0,6},{1,7},{2,4},{3,5},{4,2},{5,3},{6,0},{7,1},{8,14},{9,15},{10,... | collective-permute-start | bytes 393224 | tf_op jit(solution)/shard_map/ppermute | solution.py:248
  24.4 3.9 %collective-permute-done.4.refs_6_.refs_5_ = bf16[256,256]{1,0:T(8,128)(2,1)S(1)} collective-permute-done((bf16[256,256]{1,0:T(8,128)(2,1)S(1)}, bf16[256,256]{1,0:T(8,128)(2,1)S(1)}, u32[]{:S(2)}, u32[]{:S(2)}) %collective-permute-start.4) | collective-permute-done | bytes 131104 | tf_op jit(solution)/shard_map/ppermute | solution.py:248
  28.2 6.2 %collective-permute-done.3.refs_5_.refs_4_ = bf16[256,256]{1,0:T(8,128)(2,1)S(1)} collective-permute-done((bf16[256,256]{1,0:T(8,128)(2,1)S(1)}, bf16[256,256]{1,0:T(8,128)(2,1)S(1)}, u32[]{:S(2)}, u32[]{:S(2)}) %collective-permute-start.3) | collective-permute-done | bytes 131104 | tf_op jit(solution)/shard_map/ppermute | solution.py:248
  36.4 4.4 %up_near_side.1 = (bf16[1024,1024]{1,0:T(8,128)(2,1)S(1)}, bf16[1024,1024]{1,0:T(8,128)(2,1)S(1)}, bf16[1024,1024]{1,0:T(8,128)(2,1)S(1)}, bf16[1024,256]{1,0:T(8,128)(2,1)S(1)}) custom-call(bf16[1024,256]{1,0:T(8,128)(2,1)S(1)} %get-tuple-element.78.refs_0_, bf16[1024,256]{1,0:T(8,128)(2,1)S(1)} %collective-permute-done.5.refs_1_, ...), custom_call_target="tpu_custom_call" | custom-call | flops 805306368 | bytes 1 | tf_op jit(solution)/shard_map/up_near_side/pallas_call | solution.py:45
  40.8 4.2 %up_near_other.1 = (bf16[1024,1024]{1,0:T(8,128)(2,1)S(1)}, bf16[1024,1024]{1,0:T(8,128)(2,1)S(1)}, bf16[1024,1024]{1,0:T(8,128)(2,1)S(1)}, bf16[1024,256]{1,0:T(8,128)(2,1)S(1)}) custom-call(bf16[1024,256]{1,0:T(8,128)(2,1)S(1)} %get-tuple-element.78.refs_0_, bf16[1024,256]{1,0:T(8,128)(2,1)S(1)} %collective-permute-done.5.refs_1_, ...), custom_call_target="tpu_custom_call" | custom-call | flops 805306368 | bytes 1 | tf_op jit(solution)/shard_map/up_near_other/pallas_call | solution.py:45
  45.0 1.4 %up_far_other.1 = (bf16[1024,512]{1,0:T(8,128)(2,1)S(1)}, bf16[1024,512]{1,0:T(8,128)(2,1)S(1)}, bf16[1024,256]{1,0:T(8,128)(2,1)S(1)}) custom-call(bf16[512,256]{1,0:T(8,128)(2,1)S(1)} %collective-permute-done.8.refs_0_, bf16[512,256]{1,0:T(8,128)(2,1)S(1)} %collective-permute-done.9.refs_1_, bf16[1024,256]{1,0:T(8,128)(2,1)S(1)} %collective-permute-done.7.refs_3_.refs_2_, ...), custom_call_target="tpu_custom_call" | custom-call | flops 268435456 | bytes 1 | tf_op jit(solution)/shard_map/up_far_other/pallas_call | solution.py:45
  49.9 3.1 %collective-permute-start.11 = (bf16[128,256]{1,0:T(8,128)(2,1)S(1)}, bf16[128,256]{1,0:T(8,128)(2,1)S(1)}, u32[]{:S(2)}, u32[]{:S(2)}) collective-permute-start(bf16[128,256]{1,0:T(8,128)(2,1)S(1)} %get-tuple-element.117), channel_id=1, source_target_pairs={{0,2},{1,3},{2,0},{3,1},{4,6},{5,7},{6,4},{7,5},{8,10},{9,11},{10,... | collective-permute-start | bytes 196616 | tf_op jit(solution)/shard_map/ppermute | solution.py:248
  53.0 1.4 %collective-permute-start.20 = (bf16[128,256]{1,0:T(8,128)(2,1)S(1)}, bf16[128,256]{1,0:T(8,128)(2,1)S(1)}, u32[]{:S(2)}, u32[]{:S(2)}) collective-permute-start(bf16[128,256]{1,0:T(8,128)(2,1)S(1)} %get-tuple-element.113), channel_id=1, source_target_pairs={{0,6},{1,7},{2,4},{3,5},{4,2},{5,3},{6,0},{7,1},{8,14},{9,15},{10,... | collective-permute-start | bytes 196616 | tf_op jit(solution)/shard_map/ppermute | solution.py:248
  57.9 1.6 %collective-permute-start.16 = (bf16[128,256]{1,0:T(8,128)(2,1)S(1)}, bf16[128,256]{1,0:T(8,128)(2,1)S(1)}, u32[]{:S(2)}, u32[]{:S(2)}) collective-permute-start(bf16[128,256]{1,0:T(8,128)(2,1)S(1)} %convolution_convert_fusion.1), channel_id=1, source_target_pairs={{0,6},{1,7},{2,4},{3,5},{4,2},{5,3},{6,0},{7,1},{8,14},{9,15},{10,... | collective-permute-start | bytes 196616 | tf_op jit(solution)/shard_map/ppermute | solution.py:248
  60.1 2.3 %collective-permute-start.14 = (bf16[128,256]{1,0:T(8,128)(2,1)S(1)}, bf16[128,256]{1,0:T(8,128)(2,1)S(1)}, u32[]{:S(2)}, u32[]{:S(2)}) collective-permute-start(bf16[128,256]{1,0:T(8,128)(2,1)S(1)} %convolution_convert_fusion.1), channel_id=1, source_target_pairs={{0,2},{1,3},{2,0},{3,1},{4,6},{5,7},{6,4},{7,5},{8,10},{9,11},{10,... | collective-permute-start | bytes 196616 | tf_op jit(solution)/shard_map/ppermute | solution.py:248
  62.3 4.2 %collective-permute-done.19 = bf16[128,256]{1,0:T(8,128)(2,1)S(1)} collective-permute-done((bf16[128,256]{1,0:T(8,128)(2,1)S(1)}, bf16[128,256]{1,0:T(8,128)(2,1)S(1)}, u32[]{:S(2)}, u32[]{:S(2)}) %collective-permute-start.19) | collective-permute-done | bytes 65568 | tf_op jit(solution)/shard_map/ppermute | solution.py:248
  67.9 3.2 %collective-permute-start.21 = (bf16[128,256]{1,0:T(8,128)(2,1)S(1)}, bf16[128,256]{1,0:T(8,128)(2,1)S(1)}, u32[]{:S(2)}, u32[]{:S(2)}) collective-permute-start(bf16[128,256]{1,0:T(8,128)(2,1)S(1)} %convolution_convert_fusion), channel_id=1, source_target_pairs={{0,2},{1,3},{2,0},{3,1},{4,6},{5,7},{6,4},{7,5},{8,10},{9,11},{10,... | collective-permute-start | bytes 196616 | tf_op jit(solution)/shard_map/ppermute | solution.py:248
  71.2 1.6 %collective-permute-done.23 = bf16[128,256]{1,0:T(8,128)(2,1)S(1)} collective-permute-done((bf16[128,256]{1,0:T(8,128)(2,1)S(1)}, bf16[128,256]{1,0:T(8,128)(2,1)S(1)}, u32[]{:S(2)}, u32[]{:S(2)}) %collective-permute-start.23) | collective-permute-done | bytes 65568 | tf_op jit(solution)/shard_map/ppermute | solution.py:248
  77.4 1.8 %collective-permute-start.29 = (bf16[512,256]{1,0:T(8,128)(2,1)S(1)}, bf16[512,256]{1,0:T(8,128)(2,1)S(1)}, u32[]{:S(2)}, u32[]{:S(2)}) collective-permute-start(bf16[512,256]{1,0:T(8,128)(2,1)S(1)} %get-tuple-element.110), channel_id=1, source_target_pairs={{0,1},{1,0},{2,3},{3,2},{4,5},{5,4},{6,7},{7,6},{8,9},{9,8},{10,11... | collective-permute-start | bytes 786440 | tf_op jit(solution)/shard_map/ppermute | solution.py:248
  79.2 2.4 %down_near.1 = (bf16[512,256]{1,0:T(8,128)(2,1)S(1)}, bf16[512,256]{1,0:T(8,128)(2,1)S(1)}, f32[512,256]{1,0:T(8,128)S(1)}, f32[512,256]{1,0:T(8,128)S(1)}) custom-call(bf16[4,256,1024]{2,1,0:T(8,128)(2,1)S(1)} %bitcast.16, bf16[4,256,1024]{2,1,0:T(8,128)(2,1)S(1)} %bitcast.20, bf16[4,256,1024]{2,1,0:T(8,128)(2,1)S(1)} %bitcast.18, ...), custom_call_target="tpu_custom_call" | custom-call | flops 1 | bytes 1 | tf_op jit(solution)/shard_map/down_near/pallas_call | solution.py:45
  83.4 2.6 %collective-permute-done.26 = bf16[512,256]{1,0:T(8,128)(2,1)S(1)} collective-permute-done((bf16[512,256]{1,0:T(8,128)(2,1)S(1)}, bf16[512,256]{1,0:T(8,128)(2,1)S(1)}, u32[]{:S(2)}, u32[]{:S(2)}) %collective-permute-start.26) | collective-permute-done | bytes 262176 | tf_op jit(solution)/shard_map/ppermute | solution.py:248
  90.0 1.7 %collective-permute-done.25.xa_ref = bf16[512,256]{1,0:T(8,128)(2,1)S(1)} collective-permute-done((bf16[512,256]{1,0:T(8,128)(2,1)S(1)}, bf16[512,256]{1,0:T(8,128)(2,1)S(1)}, u32[]{:S(2)}, u32[]{:S(2)}) %collective-permute-start.25) | collective-permute-done | bytes 262176 | tf_op jit(solution)/shard_map/ppermute | solution.py:248
  92.2 4.5 %collective-permute-done.27.ya_ref = bf16[512,256]{1,0:T(8,128)(2,1)S(1)} collective-permute-done((bf16[512,256]{1,0:T(8,128)(2,1)S(1)}, bf16[512,256]{1,0:T(8,128)(2,1)S(1)}, u32[]{:S(2)}, u32[]{:S(2)}) %collective-permute-start.27) | collective-permute-done | bytes 262176 | tf_op jit(solution)/shard_map/ppermute | solution.py:248
  96.8 1.5 %last.1 = (bf16[1024,256]{1,0:T(8,128)(2,1)}, f32[1024,256]{1,0:T(8,128)}) custom-call(f32[1024,256]{1,0:T(8,128)S(1)} %down_own.1.own_ref, bf16[512,256]{1,0:T(8,128)(2,1)S(1)} %collective-permute-done.25.xa_ref, bf16[512,256]{1,0:T(8,128)(2,1)S(1)} %collective-permute-done.27.ya_ref, bf16[512,256]{1,0:T(8,128)(2,1)S(1)} %collective-permute-done.28.yb_ref, ...), custom_call_target="tpu_custom_call" | custom-call | flops 1 | bytes 1 | tf_op jit(solution)/shard_map/last/pallas_call | solution.py:27
  (65 shorter events, 24.4 us)
Async XLA Ops:
  2.2 12.2 %collective-permute-start = (bf16[128,256]{1,0:T(8,128)(2,1)S(1)}, bf16[128,256]{1,0:T(8,128)(2,1)S(1)}, u32[]{:S(2)}, u32[]{:S(2)}) collective-permute-start(bf16[128,256]{1,0:T(8,128)(2,1)S(1)} %get-tuple-element.66), channel_id=1, source_target_pairs={{0,1},{1,0},{2,3},{3,2},{4,5},{5,4},{6,7},{7,6},{8,9},{9,8},{10,11... | collective-permute-start | bytes 196616 | tf_op jit(solution)/shard_map/ppermute | solution.py:248
  5.3 9.1 %collective-permute-start.1 = (bf16[128,256]{1,0:T(8,128)(2,1)S(1)}, bf16[128,256]{1,0:T(8,128)(2,1)S(1)}, u32[]{:S(2)}, u32[]{:S(2)}) collective-permute-start(bf16[128,256]{1,0:T(8,128)(2,1)S(1)} %get-tuple-element.67), channel_id=1, source_target_pairs={{0,31},{1,2},{2,1},{3,4},{4,3},{5,6},{6,5},{7,8},{8,7},{9,10},{10,... | collective-permute-start | bytes 196616 | tf_op jit(solution)/shard_map/ppermute | solution.py:279
  19.0 15.4 %collective-permute-start.6 = (bf16[1024,256]{1,0:T(8,128)(2,1)S(1)}, bf16[1024,256]{1,0:T(8,128)(2,1)S(1)}, u32[]{:S(2)}, u32[]{:S(2)}) collective-permute-start(bf16[1024,256]{1,0:T(8,128)(2,1)S(1)} %get-tuple-element.78.refs_0_), channel_id=1, source_target_pairs={{0,1},{1,0},{2,3},{3,2},{4,5},{5,4},{6,7},{7,6},{8,9},{9,8},{10,11... | collective-permute-start | bytes 1572872 | tf_op jit(solution)/shard_map/ppermute | solution.py:248
  19.1 15.3 %collective-permute-start.5 = (bf16[1024,256]{1,0:T(8,128)(2,1)S(1)}, bf16[1024,256]{1,0:T(8,128)(2,1)S(1)}, u32[]{:S(2)}, u32[]{:S(2)}) collective-permute-start(bf16[1024,256]{1,0:T(8,128)(2,1)S(1)} %get-tuple-element.78.refs_0_), channel_id=1, source_target_pairs={{0,16},{8,24},{16,0},{24,8},{1,17},{9,25},{17,1},{25,9},{2,18},{10... | collective-permute-start | bytes 1572872 | tf_op jit(solution)/shard_map/ppermute | solution.py:248
  20.0 8.2 %collective-permute-start.4 = (bf16[256,256]{1,0:T(8,128)(2,1)S(1)}, bf16[256,256]{1,0:T(8,128)(2,1)S(1)}, u32[]{:S(2)}, u32[]{:S(2)}) collective-permute-start(bf16[256,256]{1,0:T(8,128)(2,1)S(1)} %get-tuple-element.72.refs_3_.refs_2_), channel_id=1, source_target_pairs={{0,6},{1,7},{2,4},{3,5},{4,2},{5,3},{6,0},{7,1},{8,14},{9,15},{10,... | collective-permute-start | bytes 393224 | tf_op jit(solution)/shard_map/ppermute | solution.py:248
  22.7 11.8 %collective-permute-start.3 = (bf16[256,256]{1,0:T(8,128)(2,1)S(1)}, bf16[256,256]{1,0:T(8,128)(2,1)S(1)}, u32[]{:S(2)}, u32[]{:S(2)}) collective-permute-start(bf16[256,256]{1,0:T(8,128)(2,1)S(1)} %get-tuple-element.72.refs_3_.refs_2_), channel_id=1, source_target_pairs={{0,4},{1,5},{2,6},{3,7},{4,0},{5,1},{6,2},{7,3},{8,12},{9,13},{10,... | collective-permute-start | bytes 393224 | tf_op jit(solution)/shard_map/ppermute | solution.py:248
  23.0 11.4 %collective-permute-start.2 = (bf16[256,256]{1,0:T(8,128)(2,1)S(1)}, bf16[256,256]{1,0:T(8,128)(2,1)S(1)}, u32[]{:S(2)}, u32[]{:S(2)}) collective-permute-start(bf16[256,256]{1,0:T(8,128)(2,1)S(1)} %get-tuple-element.72.refs_3_.refs_2_), channel_id=1, source_target_pairs={{0,2},{1,3},{2,0},{3,1},{4,6},{5,7},{6,4},{7,5},{8,10},{9,11},{10,... | collective-permute-start | bytes 393224 | tf_op jit(solution)/shard_map/ppermute | solution.py:248
  34.6 10.3 %collective-permute-start.9 = (bf16[512,256]{1,0:T(8,128)(2,1)S(1)}, bf16[512,256]{1,0:T(8,128)(2,1)S(1)}, u32[]{:S(2)}, u32[]{:S(2)}) collective-permute-start(bf16[512,256]{1,0:T(8,128)(2,1)S(1)} %slice.31), channel_id=1, source_target_pairs={{0,16},{8,24},{16,0},{24,8},{1,17},{9,25},{17,1},{25,9},{2,18},{10... | collective-permute-start | bytes 786440 | tf_op jit(solution)/shard_map/ppermute | solution.py:248
  35.2 9.8 %collective-permute-start.8 = (bf16[512,256]{1,0:T(8,128)(2,1)S(1)}, bf16[512,256]{1,0:T(8,128)(2,1)S(1)}, u32[]{:S(2)}, u32[]{:S(2)}) collective-permute-start(bf16[512,256]{1,0:T(8,128)(2,1)S(1)} %slice.30), channel_id=1, source_target_pairs={{0,1},{1,0},{2,3},{3,2},{4,5},{5,4},{6,7},{7,6},{8,9},{9,8},{10,11... | collective-permute-start | bytes 786440 | tf_op jit(solution)/shard_map/ppermute | solution.py:248
  48.5 6.8 %collective-permute-start.13 = (bf16[128,256]{1,0:T(8,128)(2,1)S(1)}, bf16[128,256]{1,0:T(8,128)(2,1)S(1)}, u32[]{:S(2)}, u32[]{:S(2)}) collective-permute-start(bf16[128,256]{1,0:T(8,128)(2,1)S(1)} %get-tuple-element.115), channel_id=1, source_target_pairs={{0,6},{1,7},{2,4},{3,5},{4,2},{5,3},{6,0},{7,1},{8,14},{9,15},{10,... | collective-permute-start | bytes 196616 | tf_op jit(solution)/shard_map/ppermute | solution.py:248
  49.9 7.5 %collective-permute-start.12 = (bf16[128,256]{1,0:T(8,128)(2,1)S(1)}, bf16[128,256]{1,0:T(8,128)(2,1)S(1)}, u32[]{:S(2)}, u32[]{:S(2)}) collective-permute-start(bf16[128,256]{1,0:T(8,128)(2,1)S(1)} %get-tuple-element.116), channel_id=1, source_target_pairs={{0,4},{1,5},{2,6},{3,7},{4,0},{5,1},{6,2},{7,3},{8,12},{9,13},{10,... | collective-permute-start | bytes 196616 | tf_op jit(solution)/shard_map/ppermute | solution.py:248
  49.9 7.8 %collective-permute-start.11 = (bf16[128,256]{1,0:T(8,128)(2,1)S(1)}, bf16[128,256]{1,0:T(8,128)(2,1)S(1)}, u32[]{:S(2)}, u32[]{:S(2)}) collective-permute-start(bf16[128,256]{1,0:T(8,128)(2,1)S(1)} %get-tuple-element.117), channel_id=1, source_target_pairs={{0,2},{1,3},{2,0},{3,1},{4,6},{5,7},{6,4},{7,5},{8,10},{9,11},{10,... | collective-permute-start | bytes 196616 | tf_op jit(solution)/shard_map/ppermute | solution.py:248
  53.0 7.1 %collective-permute-start.18 = (bf16[128,256]{1,0:T(8,128)(2,1)S(1)}, bf16[128,256]{1,0:T(8,128)(2,1)S(1)}, u32[]{:S(2)}, u32[]{:S(2)}) collective-permute-start(bf16[128,256]{1,0:T(8,128)(2,1)S(1)} %get-tuple-element.112), channel_id=1, source_target_pairs={{0,2},{1,3},{2,0},{3,1},{4,6},{5,7},{6,4},{7,5},{8,10},{9,11},{10,... | collective-permute-start | bytes 196616 | tf_op jit(solution)/shard_map/ppermute | solution.py:248
  53.0 9.3 %collective-permute-start.20 = (bf16[128,256]{1,0:T(8,128)(2,1)S(1)}, bf16[128,256]{1,0:T(8,128)(2,1)S(1)}, u32[]{:S(2)}, u32[]{:S(2)}) collective-permute-start(bf16[128,256]{1,0:T(8,128)(2,1)S(1)} %get-tuple-element.113), channel_id=1, source_target_pairs={{0,6},{1,7},{2,4},{3,5},{4,2},{5,3},{6,0},{7,1},{8,14},{9,15},{10,... | collective-permute-start | bytes 196616 | tf_op jit(solution)/shard_map/ppermute | solution.py:248
  55.4 11.1 %collective-permute-start.19 = (bf16[128,256]{1,0:T(8,128)(2,1)S(1)}, bf16[128,256]{1,0:T(8,128)(2,1)S(1)}, u32[]{:S(2)}, u32[]{:S(2)}) collective-permute-start(bf16[128,256]{1,0:T(8,128)(2,1)S(1)} %get-tuple-element.114), channel_id=1, source_target_pairs={{0,4},{1,5},{2,6},{3,7},{4,0},{5,1},{6,2},{7,3},{8,12},{9,13},{10,... | collective-permute-start | bytes 196616 | tf_op jit(solution)/shard_map/ppermute | solution.py:248
  57.9 10.0 %collective-permute-start.16 = (bf16[128,256]{1,0:T(8,128)(2,1)S(1)}, bf16[128,256]{1,0:T(8,128)(2,1)S(1)}, u32[]{:S(2)}, u32[]{:S(2)}) collective-permute-start(bf16[128,256]{1,0:T(8,128)(2,1)S(1)} %convolution_convert_fusion.1), channel_id=1, source_target_pairs={{0,6},{1,7},{2,4},{3,5},{4,2},{5,3},{6,0},{7,1},{8,14},{9,15},{10,... | collective-permute-start | bytes 196616 | tf_op jit(solution)/shard_map/ppermute | solution.py:248
  59.5 11.6 %collective-permute-start.15 = (bf16[128,256]{1,0:T(8,128)(2,1)S(1)}, bf16[128,256]{1,0:T(8,128)(2,1)S(1)}, u32[]{:S(2)}, u32[]{:S(2)}) collective-permute-start(bf16[128,256]{1,0:T(8,128)(2,1)S(1)} %convolution_convert_fusion.1), channel_id=1, source_target_pairs={{0,4},{1,5},{2,6},{3,7},{4,0},{5,1},{6,2},{7,3},{8,12},{9,13},{10,... | collective-permute-start | bytes 196616 | tf_op jit(solution)/shard_map/ppermute | solution.py:248
  60.1 11.1 %collective-permute-start.14 = (bf16[128,256]{1,0:T(8,128)(2,1)S(1)}, bf16[128,256]{1,0:T(8,128)(2,1)S(1)}, u32[]{:S(2)}, u32[]{:S(2)}) collective-permute-start(bf16[128,256]{1,0:T(8,128)(2,1)S(1)} %convolution_convert_fusion.1), channel_id=1, source_target_pairs={{0,2},{1,3},{2,0},{3,1},{4,6},{5,7},{6,4},{7,5},{8,10},{9,11},{10,... | collective-permute-start | bytes 196616 | tf_op jit(solution)/shard_map/ppermute | solution.py:248
  76.8 9.2 %collective-permute-start.26 = (bf16[512,256]{1,0:T(8,128)(2,1)S(1)}, bf16[512,256]{1,0:T(8,128)(2,1)S(1)}, u32[]{:S(2)}, u32[]{:S(2)}) collective-permute-start(bf16[512,256]{1,0:T(8,128)(2,1)S(1)} %get-tuple-element.107), channel_id=1, source_target_pairs={{0,16},{8,24},{16,0},{24,8},{1,17},{9,25},{17,1},{25,9},{2,18},{10... | collective-permute-start | bytes 786440 | tf_op jit(solution)/shard_map/ppermute | solution.py:248
  77.4 9.7 %collective-permute-start.29 = (bf16[512,256]{1,0:T(8,128)(2,1)S(1)}, bf16[512,256]{1,0:T(8,128)(2,1)S(1)}, u32[]{:S(2)}, u32[]{:S(2)}) collective-permute-start(bf16[512,256]{1,0:T(8,128)(2,1)S(1)} %get-tuple-element.110), channel_id=1, source_target_pairs={{0,1},{1,0},{2,3},{3,2},{4,5},{5,4},{6,7},{7,6},{8,9},{9,8},{10,11... | collective-permute-start | bytes 786440 | tf_op jit(solution)/shard_map/ppermute | solution.py:248
  81.6 10.0 %collective-permute-start.25 = (bf16[512,256]{1,0:T(8,128)(2,1)S(1)}, bf16[512,256]{1,0:T(8,128)(2,1)S(1)}, u32[]{:S(2)}, u32[]{:S(2)}) collective-permute-start(bf16[512,256]{1,0:T(8,128)(2,1)S(1)} %get-tuple-element.105), channel_id=1, source_target_pairs={{0,16},{8,24},{16,0},{24,8},{1,17},{9,25},{17,1},{25,9},{2,18},{10... | collective-permute-start | bytes 786440 | tf_op jit(solution)/shard_map/ppermute | solution.py:248
  82.4 9.8 %collective-permute-start.28 = (bf16[512,256]{1,0:T(8,128)(2,1)S(1)}, bf16[512,256]{1,0:T(8,128)(2,1)S(1)}, u32[]{:S(2)}, u32[]{:S(2)}) collective-permute-start(bf16[512,256]{1,0:T(8,128)(2,1)S(1)} %get-tuple-element.108), channel_id=1, source_target_pairs={{0,1},{1,0},{2,3},{3,2},{4,5},{5,4},{6,7},{7,6},{8,9},{9,8},{10,11... | collective-permute-start | bytes 786440 | tf_op jit(solution)/shard_map/ppermute | solution.py:248
  86.1 10.7 %collective-permute-start.27 = (bf16[512,256]{1,0:T(8,128)(2,1)S(1)}, bf16[512,256]{1,0:T(8,128)(2,1)S(1)}, u32[]{:S(2)}, u32[]{:S(2)}) collective-permute-start(bf16[512,256]{1,0:T(8,128)(2,1)S(1)} %add_convert_fusion.2), channel_id=1, source_target_pairs={{0,1},{1,0},{2,3},{3,2},{4,5},{5,4},{6,7},{7,6},{8,9},{9,8},{10,11... | collective-permute-start | bytes 786440 | tf_op jit(solution)/shard_map/ppermute | solution.py:248
  87.2 9.5 %collective-permute-start.30 = (bf16[512,256]{1,0:T(8,128)(2,1)S(1)}, bf16[512,256]{1,0:T(8,128)(2,1)S(1)}, u32[]{:S(2)}, u32[]{:S(2)}) collective-permute-start(bf16[512,256]{1,0:T(8,128)(2,1)S(1)} %add_convert_fusion.1), channel_id=1, source_target_pairs={{0,16},{8,24},{16,0},{24,8},{1,17},{9,25},{17,1},{25,9},{2,18},{10... | collective-permute-start | bytes 786440 | tf_op jit(solution)/shard_map/ppermute | solution.py:248
  (9 other events, 97.1 us)

commit v6 on v5

--- a/solution.py
+++ b/solution.py
@@ -13,43 +13,26 @@
 BOTH = ("grp", "dom")
 EPS = 1e-06
 VMEM_LIMIT = 24 * 2**20
+LAST_STEPS = 4
 
 
 def dot(a, b, ca=1, cb=0):
     return lax.dot_general(a, b, (((ca,), (cb,)), ((), ())), preferred_element_type=F32)
 
 
-def whole(shape):
-    return pl.BlockSpec(shape, lambda *_: (0,) * len(shape))
-
-
-def call(body, name, out_shape, in_specs, out_specs, args, grid=(1,), scratch=(), cost=1, limit=VMEM_LIMIT):
+VMEM = pl.BlockSpec(memory_space=pltpu.VMEM)
+HBM = pl.BlockSpec(memory_space=pltpu.HBM)
+
+
+def call_flat(body, name, out_shape, args, in_specs=None, out_specs=None, scratch=(), cost=1):
     return pl.pallas_call(
         body,
-        grid=grid,
-        in_specs=in_specs,
-        out_specs=out_specs,
+        in_specs=in_specs or [VMEM] * len(args),
+        out_specs=out_specs or [VMEM] * len(out_shape),
         out_shape=out_shape,
         scratch_shapes=list(scratch),
         name=name,
-        compiler_params=pltpu.CompilerParams(vmem_limit_bytes=limit),
-        cost_estimate=pl.CostEstimate(flops=cost, bytes_accessed=1, transcendentals=0),
-    )(*args)
-
-
-VMEM = pl.BlockSpec(memory_space=pltpu.VMEM)
-HBM = pl.BlockSpec(memory_space=pltpu.HBM)
-
-
-def call_flat(body, name, out_shape, args, in_specs=None, scratch=(), cost=1, limit=VMEM_LIMIT):
-    return pl.pallas_call(
-        body,
-        in_specs=in_specs or [VMEM] * len(args),
-        out_specs=[VMEM] * len(out_shape),
-        out_shape=out_shape,
-        scratch_shapes=list(scratch),
-        name=name,
-        compiler_params=pltpu.CompilerParams(vmem_limit_bytes=limit),
+        compiler_params=pltpu.CompilerParams(vmem_limit_bytes=VMEM_LIMIT),
         cost_estimate=pl.CostEstimate(flops=cost, bytes_accessed=1, transcendentals=0),
     )(*args)
 
@@ -161,9 +144,12 @@
         for start_ref in refs[:starts]:
             total += start_ref[at, :].astype(F32)
         for node_ref, tile_ref in zip(nodes, tiles):
-            tile = jnp.exp2(dot(held[at, :], node_ref[...], 1, 1) * scale).astype(BF16)
-            tile_ref[at, :] = tile
-            total += dot(tile, node_ref[...])
+            width = min(node_ref.shape[0], 512)
+            for start in range(0, node_ref.shape[0], width):
+                block = node_ref[start : start + width, :]
+                tile = jnp.exp2(dot(held[at, :], block, 1, 1) * scale).astype(BF16)
+                tile_ref[at, start : start + width] = tile
+                total += dot(tile, block)
         sums_ref[at, :] = total.astype(BF16)
 
 
@@ -184,40 +170,65 @@
     return out[:-1], out[-1]
 
 
-def smooth_down_body(places, n, halves, starts, *refs):
+def smooth_down_body(places, n, given, starts, *refs):
     count = len(places)
-    tiles, sums = refs[: 2 * count], refs[2 * count : 2 * count + 2 * len(halves)]
-    begun, outs = refs[2 * count + 2 * len(halves) : -count], refs[-count:]
+    tiles, sums = refs[: 2 * count], refs[2 * count : 2 * count + len(given)]
+    begun, outs = refs[2 * count + len(given) : -count], refs[-count:]
     for b, out_ref in enumerate(outs):
         total = begun[b][...] if starts else 0.0
-        for side, tile_ref in enumerate(tiles[2 * b : 2 * b + 2]):
+        for place, sum_ref in zip(given, sums):
+            tile_ref = tiles[2 * b + place % 2]
             line, mine, _ = tile_ref.shape
             part = mine // 2
-            for i, h in enumerate(halves):
-                tile = tile_ref[:, h * part : (h + 1) * part, places[b] : places[b] + n]
-                total += dot(tile.reshape(line * part, n), sums[2 * i + side][...], 0, 0)
+            h = place // 2
+            tile = tile_ref[:, h * part : (h + 1) * part, places[b] : places[b] + n]
+            total += dot(tile.reshape(line * part, n), sum_ref[...], 0, 0)
         out_ref[...] = total.astype(out_ref.dtype)
 
 
-def smooth_down(jobs, sums, n, name, halves=(0, 1), starts=()):
-    c = sums[0].shape[1]
+def smooth_down(jobs, sums, n, name, starts=()):
+    given = [i for i, v in enumerate(sums) if v is not None]
+    c = sums[given[0]].shape[1]
     return call_flat(
-        functools.partial(smooth_down_body, [at for _, at, _ in jobs], n, halves, len(starts)),
+        functools.partial(smooth_down_body, [at for _, at, _ in jobs], n, given, len(starts)),
         name,
         [jax.ShapeDtypeStruct((n, c), dtype) for _, _, dtype in jobs],
-        [*(tile for tiles, _, _ in jobs for tile in tiles), *sums, *starts],
-    )
-
-
-def last_body(own_ref, xa_ref, ya_ref, yb_ref, xb_ref, updated_ref, w_out_ref, result_ref, term_ref):
-    half = own_ref.shape[0] // 2
-    for h, first, second in ((0, xa_ref, ya_ref), (1, yb_ref, xb_ref)):
-        at = slice(h * half, (h + 1) * half)
-        smooth = own_ref[at, :] + first[...].astype(F32) + second[...].astype(F32)
+        [*(tile for tiles, _, _ in jobs for tile in tiles), *(sums[i] for i in given), *starts],
+    )
+
+
+def last_body(
+    own,
+    xa,
+    ya,
+    yb,
+    xb,
+    updated,
+    w_out,
+    result_hbm,
+    term_hbm,
+    result_ref,
+    term_ref,
+    sent,
+):
+    rows = own.shape[0]
+    step = rows // LAST_STEPS
+    copies = []
+    for i in range(LAST_STEPS):
+        at = slice(i * step, (i + 1) * step)
+        first, second = (xa, ya) if 2 * i < LAST_STEPS else (yb, xb)
+        there = slice(i * step % (rows // 2), i * step % (rows // 2) + step)
+        smooth = own[at, :] + first[there, :].astype(F32) + second[there, :].astype(F32)
         term = smooth * lax.rsqrt(jnp.mean(smooth * smooth, axis=1, keepdims=True) + EPS)
         term_ref[at, :] = term
-        result = updated_ref[at, :].astype(F32) + dot(term.astype(BF16), w_out_ref[...])
+        copies.append(pltpu.make_async_copy(term_ref.at[at], term_hbm.at[at], sent.at[2 * i]))
+        copies[-1].start()
+        result = updated[at, :].astype(F32) + dot(term.astype(BF16), w_out[...])
         result_ref[at, :] = result.astype(BF16)
+        copies.append(pltpu.make_async_copy(result_ref.at[at], result_hbm.at[at], sent.at[2 * i + 1]))
+        copies[-1].start()
+    for copy in copies:
+        copy.wait()
 
 
 def shards(
@@ -330,8 +341,10 @@
     own_tiles, x_tiles, y_tiles, a_tiles, b_tiles = tiles
     far_jobs = [(a_tiles, 0), (b_tiles, 0)]
     near_jobs = [(x_tiles, 0), (y_tiles, half), (y_tiles, 0), (x_tiles, half)]
-    begun = smooth_down([(*j, F32) for j in far_jobs], sums[0], half, "down_far_first", (0,))
-    far_a, far_b = smooth_down([(*j, BF16) for j in far_jobs], sums[1], half, "down_far", (1,), begun)
+    begun = smooth_down([(*j, F32) for j in far_jobs], [*sums[0], sums[1][0]], half, "down_far_first")
+    far_a, far_b = smooth_down(
+        [(*j, BF16) for j in far_jobs], [None, None, None, sums[1][1]], half, "down_far", begun
+    )
     *both, far_a, far_b = lax.optimization_barrier((*sums[0], *sums[1], far_a, far_b))
     first_a, first_b, pass_a, pass_b = smooth_down(
         [(*j, dtype) for j, dtype in zip(near_jobs, (BF16, BF16, F32, F32))], both, half, "down_near"
@@ -342,13 +355,17 @@
     second_b = over_x((pass_b + far_b.astype(F32)).astype(BF16))
     (own,) = smooth_down([(own_tiles, 0, F32)], both, rows, "down_own")
 
-    return call(
+    return call_flat(
         last_body,
         "last",
-        [jax.ShapeDtypeStruct((rows, c), BF16), jax.ShapeDtypeStruct((rows, c), F32)],
-        [whole((rows, c))] + [whole((half, c))] * 4 + [whole((rows, c)), whole((c, c))],
-        [whole((rows, c))] * 2,
+        [pltpu.HBM((rows, c), BF16), pltpu.HBM((rows, c), F32)],
         [own, first_a, second_a, first_b, second_b, updated, w_out],
+        out_specs=[HBM] * 2,
+        scratch=[
+            pltpu.VMEM((rows, c), BF16),
+            pltpu.VMEM((rows, c), F32),
+            pltpu.SemaphoreType.DMA((2 * LAST_STEPS,)),
+        ],
     )
 
 

time: 98.4 us -> 97.9 us (level)
  no operation moved by 1% of the time
where the time goes in v6:
time: 97.9 us; the launch traced here: 97.8 us
  starting transfers between devices  36.6 us (37%)
  waiting for transfers between devices  30 us (31%)
  Pallas kernels  29.4 us (30%)
  between operations  1.07 us (1%)
    ppermute x30, starting transfers between devices, pair(): return lambda v: lax.ppermute(v, axis, [(i, i ^ flip) for i in range(size)])  33 us
    ppermute x30, waiting for transfers between devices, pair(): return lambda v: lax.ppermute(v, axis, [(i, i ^ flip) for i in range(size)])  30 us
    pallas_call x12, Pallas kernels, call_flat(): pl.pallas_call(body, in_specs=in_specs or [VMEM] * len(args), out_specs=o...  29.4 us
    ppermute x1, starting transfers between devices, shards(): lax.ppermute(to_rest, BOTH, [(p, (p + (1 if p % 2 else -1)) % parts) for...  3.62 us
  transfers between devices with their start and end apart: 31, of which 15 were waited for; matrix products, arithmetic and copies ran while one was open for 1% of the time, Pallas kernels for 20%

profile of v6, /device:TPU:0, one launch (start us, length us, event | category | flops | bytes accessed | tf_op | source)
XLA Modules:
  0.0 97.8 jit_solution(3689558331816500741)
XLA Ops:
  0.6 1.6 %send_rows.1 = (bf16[128,256]{1,0:T(8,128)(2,1)S(1)}, bf16[128,256]{1,0:T(8,128)(2,1)S(1)}, bf16[1024,256]{1,0:T(8,128)(2,1)S(1)}, bf16[256,256]{1,0:T(8,128)(2,...) custom-call(s32[1,256]{1,0:T(1,128)} %bitcast.35, ...), custom_call_target="tpu_custom_call" | custom-call | flops 1 | bytes 1 | tf_op jit(solution)/shard_map/send_rows/pallas_call | solution.py:28
  2.2 3.0 %collective-permute-start = (bf16[128,256]{1,0:T(8,128)(2,1)S(1)}, bf16[128,256]{1,0:T(8,128)(2,1)S(1)}, u32[]{:S(2)}, u32[]{:S(2)}) collective-permute-start(bf16[128,256]{1,0:T(8,128)(2,1)S(1)} %get-tuple-element.66), channel_id=1, source_target_pairs={{0,1},{1,0},{2,3},{3,2},{4,5},{5,4},{6,7},{7,6},{8,9},{9,8},{10,11... | collective-permute-start | bytes 196616 | tf_op jit(solution)/shard_map/ppermute | solution.py:259
  5.3 3.6 %collective-permute-start.1 = (bf16[128,256]{1,0:T(8,128)(2,1)S(1)}, bf16[128,256]{1,0:T(8,128)(2,1)S(1)}, u32[]{:S(2)}, u32[]{:S(2)}) collective-permute-start(bf16[128,256]{1,0:T(8,128)(2,1)S(1)} %get-tuple-element.67), channel_id=1, source_target_pairs={{0,31},{1,2},{2,1},{3,4},{4,3},{5,6},{6,5},{7,8},{8,7},{9,10},{10,... | collective-permute-start | bytes 196616 | tf_op jit(solution)/shard_map/ppermute | solution.py:290
  8.9 5.5 %own_edges.1.pre = f32[8,1024,256]{2,1,0:T(8,128)S(1)} custom-call(bf16[1024,256]{1,0:T(8,128)(2,1)S(1)} %get-tuple-element.57.nodes, bf16[256,256]{1,0:T(8,128)(2,1)S(1)} %get-tuple-element.58.w_src, s32[8,1024]{1,0:T(8,128)S(1)} %get-tuple-element.59.links, bf16[256,256]{1,0:T(8,128)(2,1)S(1)} %get-tuple-element.64.w_dst, f32[1,256]{1,0:T(1,128)S(1)} %get-tuple-element.65.bias), custom_call_target="tpu_custom_call" | custom-call | flops 1 | bytes 1 | tf_op jit(solution)/shard_map/own_edges/pallas_call | solution.py:28
  14.4 4.6 %edges.1 = (bf16[1024,256]{1,0:T(8,128)(2,1)S(1)}, bf16[1024,256]{1,0:T(8,128)(2,1)S(1)}, bf16[256,256]{1,0:T(8,128)(2,1)S(1)}) custom-call(bf16[1024,256]{1,0:T(8,128)(2,1)S(1)} %get-tuple-element.57.nodes, bf16[256,256]{1,0:T(8,128)(2,1)S(1)} %get-tuple-element.58.w_src, s32[8,1024]{1,0:T(8,128)S(1)} %get-tuple-element.59.links, ...), custom_call_target="tpu_custom_call" | custom-call | flops 1 | bytes 1 | tf_op jit(solution)/shard_map/edges/pallas_call | solution.py:28
  20.0 2.7 %collective-permute-start.4 = (bf16[256,256]{1,0:T(8,128)(2,1)S(1)}, bf16[256,256]{1,0:T(8,128)(2,1)S(1)}, u32[]{:S(2)}, u32[]{:S(2)}) collective-permute-start(bf16[256,256]{1,0:T(8,128)(2,1)S(1)} %get-tuple-element.72.refs_3_.refs_2_), channel_id=1, source_target_pairs={{0,6},{1,7},{2,4},{3,5},{4,2},{5,3},{6,0},{7,1},{8,14},{9,15},{10,... | collective-permute-start | bytes 393224 | tf_op jit(solution)/shard_map/ppermute | solution.py:259
  24.4 3.9 %collective-permute-done.4.refs_6_.refs_5_ = bf16[256,256]{1,0:T(8,128)(2,1)S(1)} collective-permute-done((bf16[256,256]{1,0:T(8,128)(2,1)S(1)}, bf16[256,256]{1,0:T(8,128)(2,1)S(1)}, u32[]{:S(2)}, u32[]{:S(2)}) %collective-permute-start.4) | collective-permute-done | bytes 131104 | tf_op jit(solution)/shard_map/ppermute | solution.py:259
  28.2 6.2 %collective-permute-done.3.refs_5_.refs_4_ = bf16[256,256]{1,0:T(8,128)(2,1)S(1)} collective-permute-done((bf16[256,256]{1,0:T(8,128)(2,1)S(1)}, bf16[256,256]{1,0:T(8,128)(2,1)S(1)}, u32[]{:S(2)}, u32[]{:S(2)}) %collective-permute-start.3) | collective-permute-done | bytes 131104 | tf_op jit(solution)/shard_map/ppermute | solution.py:259
  36.4 4.1 %up_near_side.1 = (bf16[1024,1024]{1,0:T(8,128)(2,1)S(1)}, bf16[1024,1024]{1,0:T(8,128)(2,1)S(1)}, bf16[1024,1024]{1,0:T(8,128)(2,1)S(1)}, bf16[1024,256]{1,0:T(8,128)(2,1)S(1)}) custom-call(bf16[1024,256]{1,0:T(8,128)(2,1)S(1)} %get-tuple-element.78.refs_0_, bf16[1024,256]{1,0:T(8,128)(2,1)S(1)} %collective-permute-done.5.refs_1_, ...), custom_call_target="tpu_custom_call" | custom-call | flops 805306368 | bytes 1 | tf_op jit(solution)/shard_map/up_near_side/pallas_call | solution.py:28
  40.5 3.9 %up_near_other.1 = (bf16[1024,1024]{1,0:T(8,128)(2,1)S(1)}, bf16[1024,1024]{1,0:T(8,128)(2,1)S(1)}, bf16[1024,1024]{1,0:T(8,128)(2,1)S(1)}, bf16[1024,256]{1,0:T(8,128)(2,1)S(1)}) custom-call(bf16[1024,256]{1,0:T(8,128)(2,1)S(1)} %get-tuple-element.78.refs_0_, bf16[1024,256]{1,0:T(8,128)(2,1)S(1)} %collective-permute-done.5.refs_1_, ...), custom_call_target="tpu_custom_call" | custom-call | flops 805306368 | bytes 1 | tf_op jit(solution)/shard_map/up_near_other/pallas_call | solution.py:28
  48.0 1.8 %collective-permute-start.13 = (bf16[128,256]{1,0:T(8,128)(2,1)S(1)}, bf16[128,256]{1,0:T(8,128)(2,1)S(1)}, u32[]{:S(2)}, u32[]{:S(2)}) collective-permute-start(bf16[128,256]{1,0:T(8,128)(2,1)S(1)} %get-tuple-element.115), channel_id=1, source_target_pairs={{0,6},{1,7},{2,4},{3,5},{4,2},{5,3},{6,0},{7,1},{8,14},{9,15},{10,... | collective-permute-start | bytes 196616 | tf_op jit(solution)/shard_map/ppermute | solution.py:259
  49.7 2.7 %collective-permute-start.11 = (bf16[128,256]{1,0:T(8,128)(2,1)S(1)}, bf16[128,256]{1,0:T(8,128)(2,1)S(1)}, u32[]{:S(2)}, u32[]{:S(2)}) collective-permute-start(bf16[128,256]{1,0:T(8,128)(2,1)S(1)} %get-tuple-element.117), channel_id=1, source_target_pairs={{0,2},{1,3},{2,0},{3,1},{4,6},{5,7},{6,4},{7,5},{8,10},{9,11},{10,... | collective-permute-start | bytes 196616 | tf_op jit(solution)/shard_map/ppermute | solution.py:259
  52.5 1.7 %collective-permute-start.20 = (bf16[128,256]{1,0:T(8,128)(2,1)S(1)}, bf16[128,256]{1,0:T(8,128)(2,1)S(1)}, u32[]{:S(2)}, u32[]{:S(2)}) collective-permute-start(bf16[128,256]{1,0:T(8,128)(2,1)S(1)} %get-tuple-element.113), channel_id=1, source_target_pairs={{0,6},{1,7},{2,4},{3,5},{4,2},{5,3},{6,0},{7,1},{8,14},{9,15},{10,... | collective-permute-start | bytes 196616 | tf_op jit(solution)/shard_map/ppermute | solution.py:259
  57.3 1.8 %collective-permute-start.16 = (bf16[128,256]{1,0:T(8,128)(2,1)S(1)}, bf16[128,256]{1,0:T(8,128)(2,1)S(1)}, u32[]{:S(2)}, u32[]{:S(2)}) collective-permute-start(bf16[128,256]{1,0:T(8,128)(2,1)S(1)} %convolution_convert_fusion.1), channel_id=1, source_target_pairs={{0,6},{1,7},{2,4},{3,5},{4,2},{5,3},{6,0},{7,1},{8,14},{9,15},{10,... | collective-permute-start | bytes 196616 | tf_op jit(solution)/shard_map/ppermute | solution.py:259
  59.5 2.3 %collective-permute-start.14 = (bf16[128,256]{1,0:T(8,128)(2,1)S(1)}, bf16[128,256]{1,0:T(8,128)(2,1)S(1)}, u32[]{:S(2)}, u32[]{:S(2)}) collective-permute-start(bf16[128,256]{1,0:T(8,128)(2,1)S(1)} %convolution_convert_fusion.1), channel_id=1, source_target_pairs={{0,2},{1,3},{2,0},{3,1},{4,6},{5,7},{6,4},{7,5},{8,10},{9,11},{10,... | collective-permute-start | bytes 196616 | tf_op jit(solution)/shard_map/ppermute | solution.py:259
  61.8 4.1 %collective-permute-done.19 = bf16[128,256]{1,0:T(8,128)(2,1)S(1)} collective-permute-done((bf16[128,256]{1,0:T(8,128)(2,1)S(1)}, bf16[128,256]{1,0:T(8,128)(2,1)S(1)}, u32[]{:S(2)}, u32[]{:S(2)}) %collective-permute-start.19) | collective-permute-done | bytes 65568 | tf_op jit(solution)/shard_map/ppermute | solution.py:259
  66.1 1.8 %collective-permute-start.23 = (bf16[128,256]{1,0:T(8,128)(2,1)S(1)}, bf16[128,256]{1,0:T(8,128)(2,1)S(1)}, u32[]{:S(2)}, u32[]{:S(2)}) collective-permute-start(bf16[128,256]{1,0:T(8,128)(2,1)S(1)} %convolution_convert_fusion), channel_id=1, source_target_pairs={{0,6},{1,7},{2,4},{3,5},{4,2},{5,3},{6,0},{7,1},{8,14},{9,15},{10,... | collective-permute-start | bytes 196616 | tf_op jit(solution)/shard_map/ppermute | solution.py:259
  67.9 2.7 %collective-permute-start.21 = (bf16[128,256]{1,0:T(8,128)(2,1)S(1)}, bf16[128,256]{1,0:T(8,128)(2,1)S(1)}, u32[]{:S(2)}, u32[]{:S(2)}) collective-permute-start(bf16[128,256]{1,0:T(8,128)(2,1)S(1)} %convolution_convert_fusion), channel_id=1, source_target_pairs={{0,2},{1,3},{2,0},{3,1},{4,6},{5,7},{6,4},{7,5},{8,10},{9,11},{10,... | collective-permute-start | bytes 196616 | tf_op jit(solution)/shard_map/ppermute | solution.py:259
  70.7 1.6 %collective-permute-done.23 = bf16[128,256]{1,0:T(8,128)(2,1)S(1)} collective-permute-done((bf16[128,256]{1,0:T(8,128)(2,1)S(1)}, bf16[128,256]{1,0:T(8,128)(2,1)S(1)}, u32[]{:S(2)}, u32[]{:S(2)}) %collective-permute-start.23) | collective-permute-done | bytes 65568 | tf_op jit(solution)/shard_map/ppermute | solution.py:259
  76.8 1.6 %collective-permute-start.29 = (bf16[512,256]{1,0:T(8,128)(2,1)S(1)}, bf16[512,256]{1,0:T(8,128)(2,1)S(1)}, u32[]{:S(2)}, u32[]{:S(2)}) collective-permute-start(bf16[512,256]{1,0:T(8,128)(2,1)S(1)} %get-tuple-element.110), channel_id=1, source_target_pairs={{0,1},{1,0},{2,3},{3,2},{4,5},{5,4},{6,7},{7,6},{8,9},{9,8},{10,11... | collective-permute-start | bytes 786440 | tf_op jit(solution)/shard_map/ppermute | solution.py:259
  78.4 2.4 %down_near.1 = (bf16[512,256]{1,0:T(8,128)(2,1)S(1)}, bf16[512,256]{1,0:T(8,128)(2,1)S(1)}, f32[512,256]{1,0:T(8,128)S(1)}, f32[512,256]{1,0:T(8,128)S(1)}) custom-call(bf16[4,256,1024]{2,1,0:T(8,128)(2,1)S(1)} %bitcast.16, bf16[4,256,1024]{2,1,0:T(8,128)(2,1)S(1)} %bitcast.20, bf16[4,256,1024]{2,1,0:T(8,128)(2,1)S(1)} %bitcast.18, ...), custom_call_target="tpu_custom_call" | custom-call | flops 1 | bytes 1 | tf_op jit(solution)/shard_map/down_near/pallas_call | solution.py:28
  82.6 2.6 %collective-permute-done.26 = bf16[512,256]{1,0:T(8,128)(2,1)S(1)} collective-permute-done((bf16[512,256]{1,0:T(8,128)(2,1)S(1)}, bf16[512,256]{1,0:T(8,128)(2,1)S(1)}, u32[]{:S(2)}, u32[]{:S(2)}) %collective-permute-start.26) | collective-permute-done | bytes 262176 | tf_op jit(solution)/shard_map/ppermute | solution.py:259
  89.1 1.7 %collective-permute-done.25.xa = bf16[512,256]{1,0:T(8,128)(2,1)S(1)} collective-permute-done((bf16[512,256]{1,0:T(8,128)(2,1)S(1)}, bf16[512,256]{1,0:T(8,128)(2,1)S(1)}, u32[]{:S(2)}, u32[]{:S(2)}) %collective-permute-start.25) | collective-permute-done | bytes 262176 | tf_op jit(solution)/shard_map/ppermute | solution.py:259
  91.6 4.5 %collective-permute-done.27.ya = bf16[512,256]{1,0:T(8,128)(2,1)S(1)} collective-permute-done((bf16[512,256]{1,0:T(8,128)(2,1)S(1)}, bf16[512,256]{1,0:T(8,128)(2,1)S(1)}, u32[]{:S(2)}, u32[]{:S(2)}) %collective-permute-start.27) | collective-permute-done | bytes 262176 | tf_op jit(solution)/shard_map/ppermute | solution.py:259
  (65 shorter events, 24.4 us)
Async XLA Ops:
  2.2 12.2 %collective-permute-start = (bf16[128,256]{1,0:T(8,128)(2,1)S(1)}, bf16[128,256]{1,0:T(8,128)(2,1)S(1)}, u32[]{:S(2)}, u32[]{:S(2)}) collective-permute-start(bf16[128,256]{1,0:T(8,128)(2,1)S(1)} %get-tuple-element.66), channel_id=1, source_target_pairs={{0,1},{1,0},{2,3},{3,2},{4,5},{5,4},{6,7},{7,6},{8,9},{9,8},{10,11... | collective-permute-start | bytes 196616 | tf_op jit(solution)/shard_map/ppermute | solution.py:259
  5.3 9.1 %collective-permute-start.1 = (bf16[128,256]{1,0:T(8,128)(2,1)S(1)}, bf16[128,256]{1,0:T(8,128)(2,1)S(1)}, u32[]{:S(2)}, u32[]{:S(2)}) collective-permute-start(bf16[128,256]{1,0:T(8,128)(2,1)S(1)} %get-tuple-element.67), channel_id=1, source_target_pairs={{0,31},{1,2},{2,1},{3,4},{4,3},{5,6},{6,5},{7,8},{8,7},{9,10},{10,... | collective-permute-start | bytes 196616 | tf_op jit(solution)/shard_map/ppermute | solution.py:290
  19.0 15.4 %collective-permute-start.6 = (bf16[1024,256]{1,0:T(8,128)(2,1)S(1)}, bf16[1024,256]{1,0:T(8,128)(2,1)S(1)}, u32[]{:S(2)}, u32[]{:S(2)}) collective-permute-start(bf16[1024,256]{1,0:T(8,128)(2,1)S(1)} %get-tuple-element.78.refs_0_), channel_id=1, source_target_pairs={{0,1},{1,0},{2,3},{3,2},{4,5},{5,4},{6,7},{7,6},{8,9},{9,8},{10,11... | collective-permute-start | bytes 1572872 | tf_op jit(solution)/shard_map/ppermute | solution.py:259
  19.1 15.3 %collective-permute-start.5 = (bf16[1024,256]{1,0:T(8,128)(2,1)S(1)}, bf16[1024,256]{1,0:T(8,128)(2,1)S(1)}, u32[]{:S(2)}, u32[]{:S(2)}) collective-permute-start(bf16[1024,256]{1,0:T(8,128)(2,1)S(1)} %get-tuple-element.78.refs_0_), channel_id=1, source_target_pairs={{0,16},{8,24},{16,0},{24,8},{1,17},{9,25},{17,1},{25,9},{2,18},{10... | collective-permute-start | bytes 1572872 | tf_op jit(solution)/shard_map/ppermute | solution.py:259
  20.0 8.2 %collective-permute-start.4 = (bf16[256,256]{1,0:T(8,128)(2,1)S(1)}, bf16[256,256]{1,0:T(8,128)(2,1)S(1)}, u32[]{:S(2)}, u32[]{:S(2)}) collective-permute-start(bf16[256,256]{1,0:T(8,128)(2,1)S(1)} %get-tuple-element.72.refs_3_.refs_2_), channel_id=1, source_target_pairs={{0,6},{1,7},{2,4},{3,5},{4,2},{5,3},{6,0},{7,1},{8,14},{9,15},{10,... | collective-permute-start | bytes 393224 | tf_op jit(solution)/shard_map/ppermute | solution.py:259
  22.7 11.8 %collective-permute-start.3 = (bf16[256,256]{1,0:T(8,128)(2,1)S(1)}, bf16[256,256]{1,0:T(8,128)(2,1)S(1)}, u32[]{:S(2)}, u32[]{:S(2)}) collective-permute-start(bf16[256,256]{1,0:T(8,128)(2,1)S(1)} %get-tuple-element.72.refs_3_.refs_2_), channel_id=1, source_target_pairs={{0,4},{1,5},{2,6},{3,7},{4,0},{5,1},{6,2},{7,3},{8,12},{9,13},{10,... | collective-permute-start | bytes 393224 | tf_op jit(solution)/shard_map/ppermute | solution.py:259
  23.0 11.4 %collective-permute-start.2 = (bf16[256,256]{1,0:T(8,128)(2,1)S(1)}, bf16[256,256]{1,0:T(8,128)(2,1)S(1)}, u32[]{:S(2)}, u32[]{:S(2)}) collective-permute-start(bf16[256,256]{1,0:T(8,128)(2,1)S(1)} %get-tuple-element.72.refs_3_.refs_2_), channel_id=1, source_target_pairs={{0,2},{1,3},{2,0},{3,1},{4,6},{5,7},{6,4},{7,5},{8,10},{9,11},{10,... | collective-permute-start | bytes 393224 | tf_op jit(solution)/shard_map/ppermute | solution.py:259
  34.6 9.8 %collective-permute-start.9 = (bf16[512,256]{1,0:T(8,128)(2,1)S(1)}, bf16[512,256]{1,0:T(8,128)(2,1)S(1)}, u32[]{:S(2)}, u32[]{:S(2)}) collective-permute-start(bf16[512,256]{1,0:T(8,128)(2,1)S(1)} %slice.31), channel_id=1, source_target_pairs={{0,16},{8,24},{16,0},{24,8},{1,17},{9,25},{17,1},{25,9},{2,18},{10... | collective-permute-start | bytes 786440 | tf_op jit(solution)/shard_map/ppermute | solution.py:259
  35.2 9.2 %collective-permute-start.8 = (bf16[512,256]{1,0:T(8,128)(2,1)S(1)}, bf16[512,256]{1,0:T(8,128)(2,1)S(1)}, u32[]{:S(2)}, u32[]{:S(2)}) collective-permute-start(bf16[512,256]{1,0:T(8,128)(2,1)S(1)} %slice.30), channel_id=1, source_target_pairs={{0,1},{1,0},{2,3},{3,2},{4,5},{5,4},{6,7},{7,6},{8,9},{9,8},{10,11... | collective-permute-start | bytes 786440 | tf_op jit(solution)/shard_map/ppermute | solution.py:259
  48.0 6.8 %collective-permute-start.13 = (bf16[128,256]{1,0:T(8,128)(2,1)S(1)}, bf16[128,256]{1,0:T(8,128)(2,1)S(1)}, u32[]{:S(2)}, u32[]{:S(2)}) collective-permute-start(bf16[128,256]{1,0:T(8,128)(2,1)S(1)} %get-tuple-element.115), channel_id=1, source_target_pairs={{0,6},{1,7},{2,4},{3,5},{4,2},{5,3},{6,0},{7,1},{8,14},{9,15},{10,... | collective-permute-start | bytes 196616 | tf_op jit(solution)/shard_map/ppermute | solution.py:259
  49.7 7.1 %collective-permute-start.12 = (bf16[128,256]{1,0:T(8,128)(2,1)S(1)}, bf16[128,256]{1,0:T(8,128)(2,1)S(1)}, u32[]{:S(2)}, u32[]{:S(2)}) collective-permute-start(bf16[128,256]{1,0:T(8,128)(2,1)S(1)} %get-tuple-element.116), channel_id=1, source_target_pairs={{0,4},{1,5},{2,6},{3,7},{4,0},{5,1},{6,2},{7,3},{8,12},{9,13},{10,... | collective-permute-start | bytes 196616 | tf_op jit(solution)/shard_map/ppermute | solution.py:259
  49.7 7.4 %collective-permute-start.11 = (bf16[128,256]{1,0:T(8,128)(2,1)S(1)}, bf16[128,256]{1,0:T(8,128)(2,1)S(1)}, u32[]{:S(2)}, u32[]{:S(2)}) collective-permute-start(bf16[128,256]{1,0:T(8,128)(2,1)S(1)} %get-tuple-element.117), channel_id=1, source_target_pairs={{0,2},{1,3},{2,0},{3,1},{4,6},{5,7},{6,4},{7,5},{8,10},{9,11},{10,... | collective-permute-start | bytes 196616 | tf_op jit(solution)/shard_map/ppermute | solution.py:259
  52.4 7.1 %collective-permute-start.18 = (bf16[128,256]{1,0:T(8,128)(2,1)S(1)}, bf16[128,256]{1,0:T(8,128)(2,1)S(1)}, u32[]{:S(2)}, u32[]{:S(2)}) collective-permute-start(bf16[128,256]{1,0:T(8,128)(2,1)S(1)} %get-tuple-element.112), channel_id=1, source_target_pairs={{0,2},{1,3},{2,0},{3,1},{4,6},{5,7},{6,4},{7,5},{8,10},{9,11},{10,... | collective-permute-start | bytes 196616 | tf_op jit(solution)/shard_map/ppermute | solution.py:259
  52.5 9.3 %collective-permute-start.20 = (bf16[128,256]{1,0:T(8,128)(2,1)S(1)}, bf16[128,256]{1,0:T(8,128)(2,1)S(1)}, u32[]{:S(2)}, u32[]{:S(2)}) collective-permute-start(bf16[128,256]{1,0:T(8,128)(2,1)S(1)} %get-tuple-element.113), channel_id=1, source_target_pairs={{0,6},{1,7},{2,4},{3,5},{4,2},{5,3},{6,0},{7,1},{8,14},{9,15},{10,... | collective-permute-start | bytes 196616 | tf_op jit(solution)/shard_map/ppermute | solution.py:259
  54.8 11.1 %collective-permute-start.19 = (bf16[128,256]{1,0:T(8,128)(2,1)S(1)}, bf16[128,256]{1,0:T(8,128)(2,1)S(1)}, u32[]{:S(2)}, u32[]{:S(2)}) collective-permute-start(bf16[128,256]{1,0:T(8,128)(2,1)S(1)} %get-tuple-element.114), channel_id=1, source_target_pairs={{0,4},{1,5},{2,6},{3,7},{4,0},{5,1},{6,2},{7,3},{8,12},{9,13},{10,... | collective-permute-start | bytes 196616 | tf_op jit(solution)/shard_map/ppermute | solution.py:259
  57.3 10.5 %collective-permute-start.16 = (bf16[128,256]{1,0:T(8,128)(2,1)S(1)}, bf16[128,256]{1,0:T(8,128)(2,1)S(1)}, u32[]{:S(2)}, u32[]{:S(2)}) collective-permute-start(bf16[128,256]{1,0:T(8,128)(2,1)S(1)} %convolution_convert_fusion.1), channel_id=1, source_target_pairs={{0,6},{1,7},{2,4},{3,5},{4,2},{5,3},{6,0},{7,1},{8,14},{9,15},{10,... | collective-permute-start | bytes 196616 | tf_op jit(solution)/shard_map/ppermute | solution.py:259
  59.1 11.4 %collective-permute-start.15 = (bf16[128,256]{1,0:T(8,128)(2,1)S(1)}, bf16[128,256]{1,0:T(8,128)(2,1)S(1)}, u32[]{:S(2)}, u32[]{:S(2)}) collective-permute-start(bf16[128,256]{1,0:T(8,128)(2,1)S(1)} %convolution_convert_fusion.1), channel_id=1, source_target_pairs={{0,4},{1,5},{2,6},{3,7},{4,0},{5,1},{6,2},{7,3},{8,12},{9,13},{10,... | collective-permute-start | bytes 196616 | tf_op jit(solution)/shard_map/ppermute | solution.py:259
  59.5 11.1 %collective-permute-start.14 = (bf16[128,256]{1,0:T(8,128)(2,1)S(1)}, bf16[128,256]{1,0:T(8,128)(2,1)S(1)}, u32[]{:S(2)}, u32[]{:S(2)}) collective-permute-start(bf16[128,256]{1,0:T(8,128)(2,1)S(1)} %convolution_convert_fusion.1), channel_id=1, source_target_pairs={{0,2},{1,3},{2,0},{3,1},{4,6},{5,7},{6,4},{7,5},{8,10},{9,11},{10,... | collective-permute-start | bytes 196616 | tf_op jit(solution)/shard_map/ppermute | solution.py:259
  76.0 9.2 %collective-permute-start.26 = (bf16[512,256]{1,0:T(8,128)(2,1)S(1)}, bf16[512,256]{1,0:T(8,128)(2,1)S(1)}, u32[]{:S(2)}, u32[]{:S(2)}) collective-permute-start(bf16[512,256]{1,0:T(8,128)(2,1)S(1)} %get-tuple-element.107), channel_id=1, source_target_pairs={{0,16},{8,24},{16,0},{24,8},{1,17},{9,25},{17,1},{25,9},{2,18},{10... | collective-permute-start | bytes 786440 | tf_op jit(solution)/shard_map/ppermute | solution.py:259
  76.8 9.5 %collective-permute-start.29 = (bf16[512,256]{1,0:T(8,128)(2,1)S(1)}, bf16[512,256]{1,0:T(8,128)(2,1)S(1)}, u32[]{:S(2)}, u32[]{:S(2)}) collective-permute-start(bf16[512,256]{1,0:T(8,128)(2,1)S(1)} %get-tuple-element.110), channel_id=1, source_target_pairs={{0,1},{1,0},{2,3},{3,2},{4,5},{5,4},{6,7},{7,6},{8,9},{9,8},{10,11... | collective-permute-start | bytes 786440 | tf_op jit(solution)/shard_map/ppermute | solution.py:259
  80.8 10.0 %collective-permute-start.25 = (bf16[512,256]{1,0:T(8,128)(2,1)S(1)}, bf16[512,256]{1,0:T(8,128)(2,1)S(1)}, u32[]{:S(2)}, u32[]{:S(2)}) collective-permute-start(bf16[512,256]{1,0:T(8,128)(2,1)S(1)} %get-tuple-element.105), channel_id=1, source_target_pairs={{0,16},{8,24},{16,0},{24,8},{1,17},{9,25},{17,1},{25,9},{2,18},{10... | collective-permute-start | bytes 786440 | tf_op jit(solution)/shard_map/ppermute | solution.py:259
  81.5 10.0 %collective-permute-start.28 = (bf16[512,256]{1,0:T(8,128)(2,1)S(1)}, bf16[512,256]{1,0:T(8,128)(2,1)S(1)}, u32[]{:S(2)}, u32[]{:S(2)}) collective-permute-start(bf16[512,256]{1,0:T(8,128)(2,1)S(1)} %get-tuple-element.108), channel_id=1, source_target_pairs={{0,1},{1,0},{2,3},{3,2},{4,5},{5,4},{6,7},{7,6},{8,9},{9,8},{10,11... | collective-permute-start | bytes 786440 | tf_op jit(solution)/shard_map/ppermute | solution.py:259
  85.3 10.8 %collective-permute-start.27 = (bf16[512,256]{1,0:T(8,128)(2,1)S(1)}, bf16[512,256]{1,0:T(8,128)(2,1)S(1)}, u32[]{:S(2)}, u32[]{:S(2)}) collective-permute-start(bf16[512,256]{1,0:T(8,128)(2,1)S(1)} %add_convert_fusion.2), channel_id=1, source_target_pairs={{0,1},{1,0},{2,3},{3,2},{4,5},{5,4},{6,7},{7,6},{8,9},{9,8},{10,11... | collective-permute-start | bytes 786440 | tf_op jit(solution)/shard_map/ppermute | solution.py:259
  86.4 9.7 %collective-permute-start.30 = (bf16[512,256]{1,0:T(8,128)(2,1)S(1)}, bf16[512,256]{1,0:T(8,128)(2,1)S(1)}, u32[]{:S(2)}, u32[]{:S(2)}) collective-permute-start(bf16[512,256]{1,0:T(8,128)(2,1)S(1)} %add_convert_fusion.1), channel_id=1, source_target_pairs={{0,16},{8,24},{16,0},{24,8},{1,17},{9,25},{17,1},{25,9},{2,18},{10... | collective-permute-start | bytes 786440 | tf_op jit(solution)/shard_map/ppermute | solution.py:259
  (9 other events, 95.4 us)

commit v7 on v6

--- a/solution.py
+++ b/solution.py
@@ -13,7 +13,7 @@
 BOTH = ("grp", "dom")
 EPS = 1e-06
 VMEM_LIMIT = 24 * 2**20
-LAST_STEPS = 4
+LAST_STEPS = 2
 
 
 def dot(a, b, ca=1, cb=0):
@@ -198,10 +198,9 @@
 
 
 def last_body(
-    own,
-    xa,
+    begun_a,
+    begun_b,
     ya,
-    yb,
     xb,
     updated,
     w_out,
@@ -211,14 +210,14 @@
     term_ref,
     sent,
 ):
-    rows = own.shape[0]
+    rows = updated.shape[0]
     step = rows // LAST_STEPS
     copies = []
     for i in range(LAST_STEPS):
         at = slice(i * step, (i + 1) * step)
-        first, second = (xa, ya) if 2 * i < LAST_STEPS else (yb, xb)
+        begun, second = (begun_a, ya) if 2 * i < LAST_STEPS else (begun_b, xb)
         there = slice(i * step % (rows // 2), i * step % (rows // 2) + step)
-        smooth = own[at, :] + first[there, :].astype(F32) + second[there, :].astype(F32)
+        smooth = begun[there, :] + second[there, :].astype(F32)
         term = smooth * lax.rsqrt(jnp.mean(smooth * smooth, axis=1, keepdims=True) + EPS)
         term_ref[at, :] = term
         copies.append(pltpu.make_async_copy(term_ref.at[at], term_hbm.at[at], sent.at[2 * i]))
@@ -355,11 +354,13 @@
     second_b = over_x((pass_b + far_b.astype(F32)).astype(BF16))
     (own,) = smooth_down([(own_tiles, 0, F32)], both, rows, "down_own")
 
+    begun_a = own[:half] + first_a.astype(F32)
+    begun_b = own[half:] + first_b.astype(F32)
     return call_flat(
         last_body,
         "last",
         [pltpu.HBM((rows, c), BF16), pltpu.HBM((rows, c), F32)],
-        [own, first_a, second_a, first_b, second_b, updated, w_out],
+        [begun_a, begun_b, second_a, second_b, updated, w_out],
         out_specs=[HBM] * 2,
         scratch=[
             pltpu.VMEM((rows, c), BF16),

time: 97.9 us -> 97.8 us (level)
  no operation moved by 1% of the time
where the time goes in v7:
time: 97.8 us; the launch traced here: 97.7 us
  starting transfers between devices  36.6 us (37%)
  waiting for transfers between devices  29.8 us (30%)
  Pallas kernels  29.4 us (30%)
  between operations  1.08 us (1%)
    ppermute x30, starting transfers between devices, pair(): return lambda v: lax.ppermute(v, axis, [(i, i ^ flip) for i in range(size)])  33 us
    ppermute x30, waiting for transfers between devices, pair(): return lambda v: lax.ppermute(v, axis, [(i, i ^ flip) for i in range(size)])  29.8 us
    pallas_call x12, Pallas kernels, call_flat(): pl.pallas_call(body, in_specs=in_specs or [VMEM] * len(args), out_specs=o...  29.4 us
    ppermute x1, starting transfers between devices, shards(): lax.ppermute(to_rest, BOTH, [(p, (p + (1 if p % 2 else -1)) % parts) for...  3.62 us
  transfers between devices with their start and end apart: 31, of which 15 were waited for; matrix products, arithmetic and copies ran while one was open for 1% of the time, Pallas kernels for 20%

profile of v7, /device:TPU:0, one launch (start us, length us, event | category | flops | bytes accessed | tf_op | source)
XLA Modules:
  0.0 97.7 jit_solution(15977424356605340875)
XLA Ops:
  0.6 1.6 %send_rows.1 = (bf16[128,256]{1,0:T(8,128)(2,1)S(1)}, bf16[128,256]{1,0:T(8,128)(2,1)S(1)}, bf16[1024,256]{1,0:T(8,128)(2,1)S(1)}, bf16[256,256]{1,0:T(8,128)(2,...) custom-call(s32[1,256]{1,0:T(1,128)} %bitcast.35, ...), custom_call_target="tpu_custom_call" | custom-call | flops 1 | bytes 1 | tf_op jit(solution)/shard_map/send_rows/pallas_call | solution.py:28
  2.2 3.0 %collective-permute-start = (bf16[128,256]{1,0:T(8,128)(2,1)S(1)}, bf16[128,256]{1,0:T(8,128)(2,1)S(1)}, u32[]{:S(2)}, u32[]{:S(2)}) collective-permute-start(bf16[128,256]{1,0:T(8,128)(2,1)S(1)} %get-tuple-element.66), channel_id=1, source_target_pairs={{0,1},{1,0},{2,3},{3,2},{4,5},{5,4},{6,7},{7,6},{8,9},{9,8},{10,11... | collective-permute-start | bytes 196616 | tf_op jit(solution)/shard_map/ppermute | solution.py:258
  5.3 3.6 %collective-permute-start.1 = (bf16[128,256]{1,0:T(8,128)(2,1)S(1)}, bf16[128,256]{1,0:T(8,128)(2,1)S(1)}, u32[]{:S(2)}, u32[]{:S(2)}) collective-permute-start(bf16[128,256]{1,0:T(8,128)(2,1)S(1)} %get-tuple-element.67), channel_id=1, source_target_pairs={{0,31},{1,2},{2,1},{3,4},{4,3},{5,6},{6,5},{7,8},{8,7},{9,10},{10,... | collective-permute-start | bytes 196616 | tf_op jit(solution)/shard_map/ppermute | solution.py:289
  8.9 5.5 %own_edges.1.pre = f32[8,1024,256]{2,1,0:T(8,128)S(1)} custom-call(bf16[1024,256]{1,0:T(8,128)(2,1)S(1)} %get-tuple-element.57.nodes, bf16[256,256]{1,0:T(8,128)(2,1)S(1)} %get-tuple-element.58.w_src, s32[8,1024]{1,0:T(8,128)S(1)} %get-tuple-element.59.links, bf16[256,256]{1,0:T(8,128)(2,1)S(1)} %get-tuple-element.64.w_dst, f32[1,256]{1,0:T(1,128)S(1)} %get-tuple-element.65.bias), custom_call_target="tpu_custom_call" | custom-call | flops 1 | bytes 1 | tf_op jit(solution)/shard_map/own_edges/pallas_call | solution.py:28
  14.4 4.6 %edges.1 = (bf16[1024,256]{1,0:T(8,128)(2,1)S(1)}, bf16[1024,256]{1,0:T(8,128)(2,1)S(1)}, bf16[256,256]{1,0:T(8,128)(2,1)S(1)}) custom-call(bf16[1024,256]{1,0:T(8,128)(2,1)S(1)} %get-tuple-element.57.nodes, bf16[256,256]{1,0:T(8,128)(2,1)S(1)} %get-tuple-element.58.w_src, s32[8,1024]{1,0:T(8,128)S(1)} %get-tuple-element.59.links, ...), custom_call_target="tpu_custom_call" | custom-call | flops 1 | bytes 1 | tf_op jit(solution)/shard_map/edges/pallas_call | solution.py:28
  20.0 2.7 %collective-permute-start.4 = (bf16[256,256]{1,0:T(8,128)(2,1)S(1)}, bf16[256,256]{1,0:T(8,128)(2,1)S(1)}, u32[]{:S(2)}, u32[]{:S(2)}) collective-permute-start(bf16[256,256]{1,0:T(8,128)(2,1)S(1)} %get-tuple-element.72.refs_3_.refs_2_), channel_id=1, source_target_pairs={{0,6},{1,7},{2,4},{3,5},{4,2},{5,3},{6,0},{7,1},{8,14},{9,15},{10,... | collective-permute-start | bytes 393224 | tf_op jit(solution)/shard_map/ppermute | solution.py:258
  24.4 3.9 %collective-permute-done.4.refs_6_.refs_5_ = bf16[256,256]{1,0:T(8,128)(2,1)S(1)} collective-permute-done((bf16[256,256]{1,0:T(8,128)(2,1)S(1)}, bf16[256,256]{1,0:T(8,128)(2,1)S(1)}, u32[]{:S(2)}, u32[]{:S(2)}) %collective-permute-start.4) | collective-permute-done | bytes 131104 | tf_op jit(solution)/shard_map/ppermute | solution.py:258
  28.2 6.2 %collective-permute-done.3.refs_5_.refs_4_ = bf16[256,256]{1,0:T(8,128)(2,1)S(1)} collective-permute-done((bf16[256,256]{1,0:T(8,128)(2,1)S(1)}, bf16[256,256]{1,0:T(8,128)(2,1)S(1)}, u32[]{:S(2)}, u32[]{:S(2)}) %collective-permute-start.3) | collective-permute-done | bytes 131104 | tf_op jit(solution)/shard_map/ppermute | solution.py:258
  36.4 4.1 %up_near_side.1 = (bf16[1024,1024]{1,0:T(8,128)(2,1)S(1)}, bf16[1024,1024]{1,0:T(8,128)(2,1)S(1)}, bf16[1024,1024]{1,0:T(8,128)(2,1)S(1)}, bf16[1024,256]{1,0:T(8,128)(2,1)S(1)}) custom-call(bf16[1024,256]{1,0:T(8,128)(2,1)S(1)} %get-tuple-element.78.refs_0_, bf16[1024,256]{1,0:T(8,128)(2,1)S(1)} %collective-permute-done.5.refs_1_, ...), custom_call_target="tpu_custom_call" | custom-call | flops 805306368 | bytes 1 | tf_op jit(solution)/shard_map/up_near_side/pallas_call | solution.py:28
  40.5 3.9 %up_near_other.1 = (bf16[1024,1024]{1,0:T(8,128)(2,1)S(1)}, bf16[1024,1024]{1,0:T(8,128)(2,1)S(1)}, bf16[1024,1024]{1,0:T(8,128)(2,1)S(1)}, bf16[1024,256]{1,0:T(8,128)(2,1)S(1)}) custom-call(bf16[1024,256]{1,0:T(8,128)(2,1)S(1)} %get-tuple-element.78.refs_0_, bf16[1024,256]{1,0:T(8,128)(2,1)S(1)} %collective-permute-done.5.refs_1_, ...), custom_call_target="tpu_custom_call" | custom-call | flops 805306368 | bytes 1 | tf_op jit(solution)/shard_map/up_near_other/pallas_call | solution.py:28
  48.0 1.8 %collective-permute-start.13 = (bf16[128,256]{1,0:T(8,128)(2,1)S(1)}, bf16[128,256]{1,0:T(8,128)(2,1)S(1)}, u32[]{:S(2)}, u32[]{:S(2)}) collective-permute-start(bf16[128,256]{1,0:T(8,128)(2,1)S(1)} %get-tuple-element.117), channel_id=1, source_target_pairs={{0,6},{1,7},{2,4},{3,5},{4,2},{5,3},{6,0},{7,1},{8,14},{9,15},{10,... | collective-permute-start | bytes 196616 | tf_op jit(solution)/shard_map/ppermute | solution.py:258
  49.7 2.7 %collective-permute-start.11 = (bf16[128,256]{1,0:T(8,128)(2,1)S(1)}, bf16[128,256]{1,0:T(8,128)(2,1)S(1)}, u32[]{:S(2)}, u32[]{:S(2)}) collective-permute-start(bf16[128,256]{1,0:T(8,128)(2,1)S(1)} %get-tuple-element.119), channel_id=1, source_target_pairs={{0,2},{1,3},{2,0},{3,1},{4,6},{5,7},{6,4},{7,5},{8,10},{9,11},{10,... | collective-permute-start | bytes 196616 | tf_op jit(solution)/shard_map/ppermute | solution.py:258
  52.5 1.7 %collective-permute-start.20 = (bf16[128,256]{1,0:T(8,128)(2,1)S(1)}, bf16[128,256]{1,0:T(8,128)(2,1)S(1)}, u32[]{:S(2)}, u32[]{:S(2)}) collective-permute-start(bf16[128,256]{1,0:T(8,128)(2,1)S(1)} %get-tuple-element.115), channel_id=1, source_target_pairs={{0,6},{1,7},{2,4},{3,5},{4,2},{5,3},{6,0},{7,1},{8,14},{9,15},{10,... | collective-permute-start | bytes 196616 | tf_op jit(solution)/shard_map/ppermute | solution.py:258
  57.3 1.8 %collective-permute-start.16 = (bf16[128,256]{1,0:T(8,128)(2,1)S(1)}, bf16[128,256]{1,0:T(8,128)(2,1)S(1)}, u32[]{:S(2)}, u32[]{:S(2)}) collective-permute-start(bf16[128,256]{1,0:T(8,128)(2,1)S(1)} %convolution_convert_fusion.1), channel_id=1, source_target_pairs={{0,6},{1,7},{2,4},{3,5},{4,2},{5,3},{6,0},{7,1},{8,14},{9,15},{10,... | collective-permute-start | bytes 196616 | tf_op jit(solution)/shard_map/ppermute | solution.py:258
  59.5 2.3 %collective-permute-start.14 = (bf16[128,256]{1,0:T(8,128)(2,1)S(1)}, bf16[128,256]{1,0:T(8,128)(2,1)S(1)}, u32[]{:S(2)}, u32[]{:S(2)}) collective-permute-start(bf16[128,256]{1,0:T(8,128)(2,1)S(1)} %convolution_convert_fusion.1), channel_id=1, source_target_pairs={{0,2},{1,3},{2,0},{3,1},{4,6},{5,7},{6,4},{7,5},{8,10},{9,11},{10,... | collective-permute-start | bytes 196616 | tf_op jit(solution)/shard_map/ppermute | solution.py:258
  61.8 4.1 %collective-permute-done.19 = bf16[128,256]{1,0:T(8,128)(2,1)S(1)} collective-permute-done((bf16[128,256]{1,0:T(8,128)(2,1)S(1)}, bf16[128,256]{1,0:T(8,128)(2,1)S(1)}, u32[]{:S(2)}, u32[]{:S(2)}) %collective-permute-start.19) | collective-permute-done | bytes 65568 | tf_op jit(solution)/shard_map/ppermute | solution.py:258
  66.1 1.8 %collective-permute-start.23 = (bf16[128,256]{1,0:T(8,128)(2,1)S(1)}, bf16[128,256]{1,0:T(8,128)(2,1)S(1)}, u32[]{:S(2)}, u32[]{:S(2)}) collective-permute-start(bf16[128,256]{1,0:T(8,128)(2,1)S(1)} %convolution_convert_fusion), channel_id=1, source_target_pairs={{0,6},{1,7},{2,4},{3,5},{4,2},{5,3},{6,0},{7,1},{8,14},{9,15},{10,... | collective-permute-start | bytes 196616 | tf_op jit(solution)/shard_map/ppermute | solution.py:258
  67.9 2.7 %collective-permute-start.21 = (bf16[128,256]{1,0:T(8,128)(2,1)S(1)}, bf16[128,256]{1,0:T(8,128)(2,1)S(1)}, u32[]{:S(2)}, u32[]{:S(2)}) collective-permute-start(bf16[128,256]{1,0:T(8,128)(2,1)S(1)} %convolution_convert_fusion), channel_id=1, source_target_pairs={{0,2},{1,3},{2,0},{3,1},{4,6},{5,7},{6,4},{7,5},{8,10},{9,11},{10,... | collective-permute-start | bytes 196616 | tf_op jit(solution)/shard_map/ppermute | solution.py:258
  70.7 1.6 %collective-permute-done.23 = bf16[128,256]{1,0:T(8,128)(2,1)S(1)} collective-permute-done((bf16[128,256]{1,0:T(8,128)(2,1)S(1)}, bf16[128,256]{1,0:T(8,128)(2,1)S(1)}, u32[]{:S(2)}, u32[]{:S(2)}) %collective-permute-start.23) | collective-permute-done | bytes 65568 | tf_op jit(solution)/shard_map/ppermute | solution.py:258
  76.8 1.6 %collective-permute-start.29 = (bf16[512,256]{1,0:T(8,128)(2,1)S(1)}, bf16[512,256]{1,0:T(8,128)(2,1)S(1)}, u32[]{:S(2)}, u32[]{:S(2)}) collective-permute-start(bf16[512,256]{1,0:T(8,128)(2,1)S(1)} %get-tuple-element.110), channel_id=1, source_target_pairs={{0,1},{1,0},{2,3},{3,2},{4,5},{5,4},{6,7},{7,6},{8,9},{9,8},{10,11... | collective-permute-start | bytes 786440 | tf_op jit(solution)/shard_map/ppermute | solution.py:258
  78.4 2.4 %down_near.1 = (bf16[512,256]{1,0:T(8,128)(2,1)S(1)}, bf16[512,256]{1,0:T(8,128)(2,1)S(1)}, f32[512,256]{1,0:T(8,128)S(1)}, f32[512,256]{1,0:T(8,128)S(1)}) custom-call(bf16[4,256,1024]{2,1,0:T(8,128)(2,1)S(1)} %bitcast.16, bf16[4,256,1024]{2,1,0:T(8,128)(2,1)S(1)} %bitcast.20, bf16[4,256,1024]{2,1,0:T(8,128)(2,1)S(1)} %bitcast.18, ...), custom_call_target="tpu_custom_call" | custom-call | flops 1 | bytes 1 | tf_op jit(solution)/shard_map/down_near/pallas_call | solution.py:28
  87.8 3.0 %collective-permute-done.25 = bf16[512,256]{1,0:T(8,128)(2,1)S(1)} collective-permute-done((bf16[512,256]{1,0:T(8,128)(2,1)S(1)}, bf16[512,256]{1,0:T(8,128)(2,1)S(1)}, u32[]{:S(2)}, u32[]{:S(2)}) %collective-permute-start.25) | collective-permute-done | bytes 262176 | tf_op jit(solution)/shard_map/ppermute | solution.py:258
  91.7 4.4 %collective-permute-done.28.ya = bf16[512,256]{1,0:T(8,128)(2,1)S(1)} collective-permute-done((bf16[512,256]{1,0:T(8,128)(2,1)S(1)}, bf16[512,256]{1,0:T(8,128)(2,1)S(1)}, u32[]{:S(2)}, u32[]{:S(2)}) %collective-permute-start.28) | collective-permute-done | bytes 262176 | tf_op jit(solution)/shard_map/ppermute | solution.py:258
  96.1 1.4 %last.1 = (bf16[1024,256]{1,0:T(8,128)(2,1)}, f32[1024,256]{1,0:T(8,128)}) custom-call(f32[512,256]{1,0:T(8,128)S(1)} %get-tuple-element.113.begun_a, f32[512,256]{1,0:T(8,128)S(1)} %get-tuple-element.112.begun_b, bf16[512,256]{1,0:T(8,128)(2,1)S(1)} %collective-permute-done.28.ya, bf16[512,256]{1,0:T(8,128)(2,1)S(1)} %collective-permute-done.30.xb, ...), custom_call_target="tpu_custom_call" | custom-call | flops 1 | bytes 1 | tf_op jit(solution)/shard_map/last/pallas_call | solution.py:28
  (66 shorter events, 24.3 us)
Async XLA Ops:
  2.2 12.2 %collective-permute-start = (bf16[128,256]{1,0:T(8,128)(2,1)S(1)}, bf16[128,256]{1,0:T(8,128)(2,1)S(1)}, u32[]{:S(2)}, u32[]{:S(2)}) collective-permute-start(bf16[128,256]{1,0:T(8,128)(2,1)S(1)} %get-tuple-element.66), channel_id=1, source_target_pairs={{0,1},{1,0},{2,3},{3,2},{4,5},{5,4},{6,7},{7,6},{8,9},{9,8},{10,11... | collective-permute-start | bytes 196616 | tf_op jit(solution)/shard_map/ppermute | solution.py:258
  5.3 9.1 %collective-permute-start.1 = (bf16[128,256]{1,0:T(8,128)(2,1)S(1)}, bf16[128,256]{1,0:T(8,128)(2,1)S(1)}, u32[]{:S(2)}, u32[]{:S(2)}) collective-permute-start(bf16[128,256]{1,0:T(8,128)(2,1)S(1)} %get-tuple-element.67), channel_id=1, source_target_pairs={{0,31},{1,2},{2,1},{3,4},{4,3},{5,6},{6,5},{7,8},{8,7},{9,10},{10,... | collective-permute-start | bytes 196616 | tf_op jit(solution)/shard_map/ppermute | solution.py:289
  19.0 15.4 %collective-permute-start.6 = (bf16[1024,256]{1,0:T(8,128)(2,1)S(1)}, bf16[1024,256]{1,0:T(8,128)(2,1)S(1)}, u32[]{:S(2)}, u32[]{:S(2)}) collective-permute-start(bf16[1024,256]{1,0:T(8,128)(2,1)S(1)} %get-tuple-element.78.refs_0_), channel_id=1, source_target_pairs={{0,1},{1,0},{2,3},{3,2},{4,5},{5,4},{6,7},{7,6},{8,9},{9,8},{10,11... | collective-permute-start | bytes 1572872 | tf_op jit(solution)/shard_map/ppermute | solution.py:258
  19.1 15.3 %collective-permute-start.5 = (bf16[1024,256]{1,0:T(8,128)(2,1)S(1)}, bf16[1024,256]{1,0:T(8,128)(2,1)S(1)}, u32[]{:S(2)}, u32[]{:S(2)}) collective-permute-start(bf16[1024,256]{1,0:T(8,128)(2,1)S(1)} %get-tuple-element.78.refs_0_), channel_id=1, source_target_pairs={{0,16},{8,24},{16,0},{24,8},{1,17},{9,25},{17,1},{25,9},{2,18},{10... | collective-permute-start | bytes 1572872 | tf_op jit(solution)/shard_map/ppermute | solution.py:258
  20.0 8.2 %collective-permute-start.4 = (bf16[256,256]{1,0:T(8,128)(2,1)S(1)}, bf16[256,256]{1,0:T(8,128)(2,1)S(1)}, u32[]{:S(2)}, u32[]{:S(2)}) collective-permute-start(bf16[256,256]{1,0:T(8,128)(2,1)S(1)} %get-tuple-element.72.refs_3_.refs_2_), channel_id=1, source_target_pairs={{0,6},{1,7},{2,4},{3,5},{4,2},{5,3},{6,0},{7,1},{8,14},{9,15},{10,... | collective-permute-start | bytes 393224 | tf_op jit(solution)/shard_map/ppermute | solution.py:258
  22.7 11.8 %collective-permute-start.3 = (bf16[256,256]{1,0:T(8,128)(2,1)S(1)}, bf16[256,256]{1,0:T(8,128)(2,1)S(1)}, u32[]{:S(2)}, u32[]{:S(2)}) collective-permute-start(bf16[256,256]{1,0:T(8,128)(2,1)S(1)} %get-tuple-element.72.refs_3_.refs_2_), channel_id=1, source_target_pairs={{0,4},{1,5},{2,6},{3,7},{4,0},{5,1},{6,2},{7,3},{8,12},{9,13},{10,... | collective-permute-start | bytes 393224 | tf_op jit(solution)/shard_map/ppermute | solution.py:258
  23.0 11.4 %collective-permute-start.2 = (bf16[256,256]{1,0:T(8,128)(2,1)S(1)}, bf16[256,256]{1,0:T(8,128)(2,1)S(1)}, u32[]{:S(2)}, u32[]{:S(2)}) collective-permute-start(bf16[256,256]{1,0:T(8,128)(2,1)S(1)} %get-tuple-element.72.refs_3_.refs_2_), channel_id=1, source_target_pairs={{0,2},{1,3},{2,0},{3,1},{4,6},{5,7},{6,4},{7,5},{8,10},{9,11},{10,... | collective-permute-start | bytes 393224 | tf_op jit(solution)/shard_map/ppermute | solution.py:258
  34.6 9.8 %collective-permute-start.9 = (bf16[512,256]{1,0:T(8,128)(2,1)S(1)}, bf16[512,256]{1,0:T(8,128)(2,1)S(1)}, u32[]{:S(2)}, u32[]{:S(2)}) collective-permute-start(bf16[512,256]{1,0:T(8,128)(2,1)S(1)} %slice.37), channel_id=1, source_target_pairs={{0,16},{8,24},{16,0},{24,8},{1,17},{9,25},{17,1},{25,9},{2,18},{10... | collective-permute-start | bytes 786440 | tf_op jit(solution)/shard_map/ppermute | solution.py:258
  35.2 9.2 %collective-permute-start.8 = (bf16[512,256]{1,0:T(8,128)(2,1)S(1)}, bf16[512,256]{1,0:T(8,128)(2,1)S(1)}, u32[]{:S(2)}, u32[]{:S(2)}) collective-permute-start(bf16[512,256]{1,0:T(8,128)(2,1)S(1)} %slice.36), channel_id=1, source_target_pairs={{0,1},{1,0},{2,3},{3,2},{4,5},{5,4},{6,7},{7,6},{8,9},{9,8},{10,11... | collective-permute-start | bytes 786440 | tf_op jit(solution)/shard_map/ppermute | solution.py:258
  48.0 6.8 %collective-permute-start.13 = (bf16[128,256]{1,0:T(8,128)(2,1)S(1)}, bf16[128,256]{1,0:T(8,128)(2,1)S(1)}, u32[]{:S(2)}, u32[]{:S(2)}) collective-permute-start(bf16[128,256]{1,0:T(8,128)(2,1)S(1)} %get-tuple-element.117), channel_id=1, source_target_pairs={{0,6},{1,7},{2,4},{3,5},{4,2},{5,3},{6,0},{7,1},{8,14},{9,15},{10,... | collective-permute-start | bytes 196616 | tf_op jit(solution)/shard_map/ppermute | solution.py:258
  49.7 7.1 %collective-permute-start.12 = (bf16[128,256]{1,0:T(8,128)(2,1)S(1)}, bf16[128,256]{1,0:T(8,128)(2,1)S(1)}, u32[]{:S(2)}, u32[]{:S(2)}) collective-permute-start(bf16[128,256]{1,0:T(8,128)(2,1)S(1)} %get-tuple-element.118), channel_id=1, source_target_pairs={{0,4},{1,5},{2,6},{3,7},{4,0},{5,1},{6,2},{7,3},{8,12},{9,13},{10,... | collective-permute-start | bytes 196616 | tf_op jit(solution)/shard_map/ppermute | solution.py:258
  49.7 7.4 %collective-permute-start.11 = (bf16[128,256]{1,0:T(8,128)(2,1)S(1)}, bf16[128,256]{1,0:T(8,128)(2,1)S(1)}, u32[]{:S(2)}, u32[]{:S(2)}) collective-permute-start(bf16[128,256]{1,0:T(8,128)(2,1)S(1)} %get-tuple-element.119), channel_id=1, source_target_pairs={{0,2},{1,3},{2,0},{3,1},{4,6},{5,7},{6,4},{7,5},{8,10},{9,11},{10,... | collective-permute-start | bytes 196616 | tf_op jit(solution)/shard_map/ppermute | solution.py:258
  52.4 7.1 %collective-permute-start.18 = (bf16[128,256]{1,0:T(8,128)(2,1)S(1)}, bf16[128,256]{1,0:T(8,128)(2,1)S(1)}, u32[]{:S(2)}, u32[]{:S(2)}) collective-permute-start(bf16[128,256]{1,0:T(8,128)(2,1)S(1)} %get-tuple-element.114), channel_id=1, source_target_pairs={{0,2},{1,3},{2,0},{3,1},{4,6},{5,7},{6,4},{7,5},{8,10},{9,11},{10,... | collective-permute-start | bytes 196616 | tf_op jit(solution)/shard_map/ppermute | solution.py:258
  52.5 9.3 %collective-permute-start.20 = (bf16[128,256]{1,0:T(8,128)(2,1)S(1)}, bf16[128,256]{1,0:T(8,128)(2,1)S(1)}, u32[]{:S(2)}, u32[]{:S(2)}) collective-permute-start(bf16[128,256]{1,0:T(8,128)(2,1)S(1)} %get-tuple-element.115), channel_id=1, source_target_pairs={{0,6},{1,7},{2,4},{3,5},{4,2},{5,3},{6,0},{7,1},{8,14},{9,15},{10,... | collective-permute-start | bytes 196616 | tf_op jit(solution)/shard_map/ppermute | solution.py:258
  54.8 11.1 %collective-permute-start.19 = (bf16[128,256]{1,0:T(8,128)(2,1)S(1)}, bf16[128,256]{1,0:T(8,128)(2,1)S(1)}, u32[]{:S(2)}, u32[]{:S(2)}) collective-permute-start(bf16[128,256]{1,0:T(8,128)(2,1)S(1)} %get-tuple-element.116), channel_id=1, source_target_pairs={{0,4},{1,5},{2,6},{3,7},{4,0},{5,1},{6,2},{7,3},{8,12},{9,13},{10,... | collective-permute-start | bytes 196616 | tf_op jit(solution)/shard_map/ppermute | solution.py:258
  57.3 10.5 %collective-permute-start.16 = (bf16[128,256]{1,0:T(8,128)(2,1)S(1)}, bf16[128,256]{1,0:T(8,128)(2,1)S(1)}, u32[]{:S(2)}, u32[]{:S(2)}) collective-permute-start(bf16[128,256]{1,0:T(8,128)(2,1)S(1)} %convolution_convert_fusion.1), channel_id=1, source_target_pairs={{0,6},{1,7},{2,4},{3,5},{4,2},{5,3},{6,0},{7,1},{8,14},{9,15},{10,... | collective-permute-start | bytes 196616 | tf_op jit(solution)/shard_map/ppermute | solution.py:258
  59.1 11.4 %collective-permute-start.15 = (bf16[128,256]{1,0:T(8,128)(2,1)S(1)}, bf16[128,256]{1,0:T(8,128)(2,1)S(1)}, u32[]{:S(2)}, u32[]{:S(2)}) collective-permute-start(bf16[128,256]{1,0:T(8,128)(2,1)S(1)} %convolution_convert_fusion.1), channel_id=1, source_target_pairs={{0,4},{1,5},{2,6},{3,7},{4,0},{5,1},{6,2},{7,3},{8,12},{9,13},{10,... | collective-permute-start | bytes 196616 | tf_op jit(solution)/shard_map/ppermute | solution.py:258
  59.5 11.1 %collective-permute-start.14 = (bf16[128,256]{1,0:T(8,128)(2,1)S(1)}, bf16[128,256]{1,0:T(8,128)(2,1)S(1)}, u32[]{:S(2)}, u32[]{:S(2)}) collective-permute-start(bf16[128,256]{1,0:T(8,128)(2,1)S(1)} %convolution_convert_fusion.1), channel_id=1, source_target_pairs={{0,2},{1,3},{2,0},{3,1},{4,6},{5,7},{6,4},{7,5},{8,10},{9,11},{10,... | collective-permute-start | bytes 196616 | tf_op jit(solution)/shard_map/ppermute | solution.py:258
  76.0 9.2 %collective-permute-start.27 = (bf16[512,256]{1,0:T(8,128)(2,1)S(1)}, bf16[512,256]{1,0:T(8,128)(2,1)S(1)}, u32[]{:S(2)}, u32[]{:S(2)}) collective-permute-start(bf16[512,256]{1,0:T(8,128)(2,1)S(1)} %get-tuple-element.108), channel_id=1, source_target_pairs={{0,16},{8,24},{16,0},{24,8},{1,17},{9,25},{17,1},{25,9},{2,18},{10... | collective-permute-start | bytes 786440 | tf_op jit(solution)/shard_map/ppermute | solution.py:258
  76.8 9.6 %collective-permute-start.29 = (bf16[512,256]{1,0:T(8,128)(2,1)S(1)}, bf16[512,256]{1,0:T(8,128)(2,1)S(1)}, u32[]{:S(2)}, u32[]{:S(2)}) collective-permute-start(bf16[512,256]{1,0:T(8,128)(2,1)S(1)} %get-tuple-element.110), channel_id=1, source_target_pairs={{0,1},{1,0},{2,3},{3,2},{4,5},{5,4},{6,7},{7,6},{8,9},{9,8},{10,11... | collective-permute-start | bytes 786440 | tf_op jit(solution)/shard_map/ppermute | solution.py:258
  80.8 10.0 %collective-permute-start.25 = (bf16[512,256]{1,0:T(8,128)(2,1)S(1)}, bf16[512,256]{1,0:T(8,128)(2,1)S(1)}, u32[]{:S(2)}, u32[]{:S(2)}) collective-permute-start(bf16[512,256]{1,0:T(8,128)(2,1)S(1)} %get-tuple-element.105), channel_id=1, source_target_pairs={{0,16},{8,24},{16,0},{24,8},{1,17},{9,25},{17,1},{25,9},{2,18},{10... | collective-permute-start | bytes 786440 | tf_op jit(solution)/shard_map/ppermute | solution.py:258
  81.5 10.0 %collective-permute-start.26 = (bf16[512,256]{1,0:T(8,128)(2,1)S(1)}, bf16[512,256]{1,0:T(8,128)(2,1)S(1)}, u32[]{:S(2)}, u32[]{:S(2)}) collective-permute-start(bf16[512,256]{1,0:T(8,128)(2,1)S(1)} %get-tuple-element.106), channel_id=1, source_target_pairs={{0,1},{1,0},{2,3},{3,2},{4,5},{5,4},{6,7},{7,6},{8,9},{9,8},{10,11... | collective-permute-start | bytes 786440 | tf_op jit(solution)/shard_map/ppermute | solution.py:258
  85.3 10.8 %collective-permute-start.28 = (bf16[512,256]{1,0:T(8,128)(2,1)S(1)}, bf16[512,256]{1,0:T(8,128)(2,1)S(1)}, u32[]{:S(2)}, u32[]{:S(2)}) collective-permute-start(bf16[512,256]{1,0:T(8,128)(2,1)S(1)} %add_convert_fusion.2), channel_id=1, source_target_pairs={{0,1},{1,0},{2,3},{3,2},{4,5},{5,4},{6,7},{7,6},{8,9},{9,8},{10,11... | collective-permute-start | bytes 786440 | tf_op jit(solution)/shard_map/ppermute | solution.py:258
  86.4 9.7 %collective-permute-start.30 = (bf16[512,256]{1,0:T(8,128)(2,1)S(1)}, bf16[512,256]{1,0:T(8,128)(2,1)S(1)}, u32[]{:S(2)}, u32[]{:S(2)}) collective-permute-start(bf16[512,256]{1,0:T(8,128)(2,1)S(1)} %add_convert_fusion.1), channel_id=1, source_target_pairs={{0,16},{8,24},{16,0},{24,8},{1,17},{9,25},{17,1},{25,9},{2,18},{10... | collective-permute-start | bytes 786440 | tf_op jit(solution)/shard_map/ppermute | solution.py:258
  (9 other events, 97.9 us)
